TPU v7x, 32 devices: a whole 2x2x4 slice. The times are simulated.
32 devices in a mesh: rows: 16 (over z, y, x), grp: 2 (over core).
Axes of the slice: x: 2, y: 2, z: 4, core: 2. Of those that a mesh axis runs over, the one named last changes fastest.
Arguments:
- nodes_in: bfloat16 [131072, 384], P(('rows', 'grp')), may hold values from -6 to 6
- out_grad: bfloat16 [131072, 384], P(('rows', 'grp')), may hold values from -6 to 6
- neighbours: int32 [131072, 27], P(('rows', 'grp')), may hold values from -1 to 128, as said below
- node_mask: int32 [131072], P(('rows', 'grp')), may hold values from 0 to 1
- master: float32 [1785856], P(('rows', 'grp')), may hold values from -1.6 to 1.6
- first_moment: float32 [1785856], P(('rows', 'grp')), may hold values from -128 to 128
- second_moment: float32 [1785856], P(('rows', 'grp')), may hold values from 1703.936 to 6946.816
Outputs:
- output: bfloat16 [131072, 384], P(('rows', 'grp'))
- node_grad: float32 [131072, 384], P(('rows', 'grp'))
- new_master: float32 [1785856], P(('rows', 'grp'))
- new_first: float32 [1785856], P(('rows', 'grp'))
- new_second: float32 [1785856], P(('rows', 'grp'))
- new_low: bfloat16 [1785856], P(('rows', 'grp'))
- final_bias_grad: float32 [384], replicated
Inputs may be any that keep to these rules, and one draw needn't show every extreme that they name: `neighbours`: entry 13 of every row is 64. Every other entry is either -1 or 64 plus the signed distance in node order from the row's node to a node within 64 positions. Entries 0 and 26 are 0 and 128 wherever those nodes exist.
All inputs are finite; a program needn't handle non-finite values.
Results may differ from a plain program's by a relative error of at most 0.012.
Values may be sent and summed in bfloat16 or wider, within the bound.
A program may use at most 448 MiB of HBM per device.

v0:
```python
import math

import jax
import jax.numpy as jnp
from jax import lax
from jax.sharding import PartitionSpec as P

C = 384
HEADS = 12
HD = 32
F = 1536
WINDOW_NODES = 32
WINDOW_DILATION = 4
HALO = 64
STEP = 5


eps_norm = 1e-05
masked_score = -1000000000.0


def extended_2(block, sides, width):
    for axis, dim in sides:
        count = lax.axis_size(axis)
        forward = [(i, i + 1) for i in range(count - 1)]
        backward = [(target, source) for source, target in forward]
        low = lax.ppermute(
            lax.slice_in_dim(block, block.shape[dim] - width, None, axis=dim), axis, forward
        )
        high = lax.ppermute(lax.slice_in_dim(block, 0, width, axis=dim), axis, backward)
        block = jnp.concatenate([low, block, high], axis=dim)
    return block


def layout(channels, hidden_units):
    return [
        ("batch_gain", (channels,)),
        ("batch_shift", (channels,)),
        ("first_gain", (channels,)),
        ("first_shift", (channels,)),
        ("query_bias", (channels,)),
        ("value_bias", (channels,)),
        ("output_bias", (channels,)),
        ("second_gain", (channels,)),
        ("second_shift", (channels,)),
        ("hidden_bias", (hidden_units,)),
        ("final_bias", (channels,)),
        ("conv_weight", (27, channels)),
        ("joint_weight", (channels, 3 * channels)),
        ("output_weight", (channels, channels)),
        ("hidden_weight", (channels, hidden_units)),
        ("final_weight", (hidden_units, channels)),
    ]


def unpack(flat, channels, hidden_units):
    pieces = {}
    offset = 0
    for segment_name, segment_shape in layout(channels, hidden_units):
        entries = math.prod(segment_shape)
        pieces[segment_name] = flat[offset : offset + entries].reshape(segment_shape)
        offset += entries
    return pieces


def layer_norm(value_rows, norm_gain, norm_shift):
    center = value_rows - jnp.mean(value_rows, axis=-1, keepdims=True)
    spread = jnp.mean(center * center, axis=-1, keepdims=True)
    return center * lax.rsqrt(spread + eps_norm) * norm_gain + norm_shift


def contract_rows(left, right):
    return lax.dot_general(
        left, right, (((0,), (0,)), ((), ())), preferred_element_type=jnp.float32
    )


def contract_last(left, right):
    return lax.dot_general(
        left, right, (((1,), (1,)), ((), ())), preferred_element_type=jnp.float32
    )


def split_into_windows(value_rows):
    trailing_rows = value_rows.shape[1:]
    launch_grid = value_rows.reshape(
        (value_rows.shape[0] // (WINDOW_NODES * WINDOW_DILATION), WINDOW_NODES, WINDOW_DILATION)
        + trailing_rows
    )
    return jnp.swapaxes(launch_grid, 1, 2).reshape(value_rows.shape)


def out_of_windows(value_rows):
    trailing_rows = value_rows.shape[1:]
    launch_grid = value_rows.reshape(
        (value_rows.shape[0] // (WINDOW_NODES * WINDOW_DILATION), WINDOW_DILATION, WINDOW_NODES)
        + trailing_rows
    )
    return jnp.swapaxes(launch_grid, 1, 2).reshape(value_rows.shape)


def window_scores(queries, window_keys, key_live):
    scores = jnp.einsum(
        "wqhd,wkhd->whqk", queries, window_keys, preferred_element_type=jnp.float32
    ) * HD ** (-0.5)
    return jnp.where(key_live[:, None, None, :] > 0, scores, masked_score)


def shards(nodes_in, out_grad, neighbours, node_mask, master, first_moment, second_moment):
    node_count = nodes_in.shape[0]
    score_scale = HD ** (-0.5)
    weights_low = lax.all_gather(master.astype(jnp.bfloat16), ("rows", "grp"), axis=0, tiled=True)
    params = unpack(weights_low, C, F)
    vectors = {
        segment_name: params[segment_name].astype(jnp.float32)
        for segment_name, segment_shape in layout(C, F)[:11]
    }
    conv_weight = params["conv_weight"].astype(jnp.float32)
    extended = extended_2(nodes_in, ((("rows", "grp"), 0),), HALO)
    row_place = lax.broadcasted_iota(jnp.int32, (node_count, 27), 0)
    present = neighbours >= 0
    local_index = jnp.where(present, neighbours + row_place, 0)
    present_float = present.astype(jnp.float32)
    convolved = jnp.zeros((node_count, C), jnp.float32)
    for offset_index in range(27):
        picked = jnp.take(extended, local_index[:, offset_index], axis=0).astype(jnp.float32)
        convolved = (
            convolved
            + picked * present_float[:, offset_index : offset_index + 1] * conv_weight[offset_index]
        )
    live_rows = node_mask.astype(jnp.float32)[:, None]
    first_total, sum_two, live_total = lax.psum(
        (
            jnp.sum(live_rows * convolved, axis=0),
            jnp.sum(live_rows * convolved * convolved, axis=0),
            jnp.sum(live_rows),
        ),
        ("rows", "grp"),
    )
    average = first_total / live_total
    variance = sum_two / live_total - average * average
    inverse_scale = lax.rsqrt(variance + eps_norm)
    centered = (convolved - average) * inverse_scale
    batch_gain = vectors["batch_gain"]
    first_sum = nodes_in.astype(jnp.float32) + (centered * batch_gain + vectors["batch_shift"])
    normed_first, first_norm_back = jax.vjp(
        layer_norm, first_sum, vectors["first_gain"], vectors["first_shift"]
    )
    attend_input = normed_first.astype(jnp.bfloat16)
    joint_bias = jnp.concatenate(
        [vectors["query_bias"], jnp.zeros((C,), jnp.float32), vectors["value_bias"]]
    )
    projected = (
        jnp.dot(attend_input, params["joint_weight"], preferred_element_type=jnp.float32)
        + joint_bias
    )
    windowed = split_into_windows(projected.astype(jnp.bfloat16))
    block_shape = (node_count // WINDOW_NODES, WINDOW_NODES, HEADS, HD)
    queries = windowed[:, :C].reshape(block_shape)
    window_keys = windowed[:, C : 2 * C].reshape(block_shape)
    window_values = windowed[:, 2 * C :].reshape(block_shape)
    key_live = split_into_windows(node_mask).reshape(node_count // WINDOW_NODES, WINDOW_NODES)
    scores = window_scores(queries, window_keys, key_live)
    row_max = jnp.max(scores, axis=-1, keepdims=True)
    expo = jnp.exp(scores - row_max)
    row_total = jnp.sum(expo, axis=-1, keepdims=True)
    row_log = row_max + jnp.log(row_total)
    forward_weights = (expo / row_total).astype(jnp.bfloat16)
    attended = jnp.einsum(
        "whqk,wkhd->wqhd", forward_weights, window_values, preferred_element_type=jnp.float32
    ).astype(jnp.bfloat16)
    attended = out_of_windows(attended.reshape(node_count, C))
    branch = (
        jnp.dot(attended, params["output_weight"], preferred_element_type=jnp.float32)
        + vectors["output_bias"]
    )
    second_sum = first_sum + branch
    normed_second, second_norm_back = jax.vjp(
        layer_norm, second_sum, vectors["second_gain"], vectors["second_shift"]
    )
    hidden_input = normed_second.astype(jnp.bfloat16)
    hidden_pre = (
        jnp.dot(hidden_input, params["hidden_weight"], preferred_element_type=jnp.float32)
        + vectors["hidden_bias"]
    )
    activated_float, gelu_back = jax.vjp(jax.nn.gelu, hidden_pre)
    activated = activated_float.astype(jnp.bfloat16)
    result = (
        jnp.dot(activated, params["final_weight"], preferred_element_type=jnp.float32)
        + vectors["final_bias"]
    )
    output = (second_sum + result).astype(jnp.bfloat16)
    delta_out = out_grad.astype(jnp.float32)
    delta_final_weight = contract_rows(activated, out_grad)
    delta_final_bias = jnp.sum(delta_out, axis=0)
    delta_activated = contract_last(out_grad, params["final_weight"])
    delta_pre = gelu_back(delta_activated)[0].astype(jnp.bfloat16)
    delta_hidden_weight = contract_rows(hidden_input, delta_pre)
    delta_hidden_bias = jnp.sum(delta_pre.astype(jnp.float32), axis=0)
    delta_hidden_input = contract_last(delta_pre, params["hidden_weight"])
    delta_norm_two, delta_second_gain, delta_second_shift = second_norm_back(delta_hidden_input)
    delta_second = delta_out + delta_norm_two
    delta_branch = delta_second.astype(jnp.bfloat16)
    delta_output_weight = contract_rows(attended, delta_branch)
    delta_output_bias = jnp.sum(delta_branch.astype(jnp.float32), axis=0)
    delta_attended = contract_last(delta_branch, params["output_weight"]).astype(jnp.bfloat16)
    delta_window_rows = split_into_windows(delta_attended).reshape(block_shape)
    attention_weights = jnp.exp(window_scores(queries, window_keys, key_live) - row_log)
    delta_weights = jnp.einsum(
        "wqhd,wkhd->whqk", delta_window_rows, window_values, preferred_element_type=jnp.float32
    )
    delta_scores = attention_weights * (
        delta_weights - jnp.sum(attention_weights * delta_weights, axis=-1, keepdims=True)
    )
    delta_scores = delta_scores.astype(jnp.bfloat16)
    weights_rounded = attention_weights.astype(jnp.bfloat16)
    delta_query = (
        jnp.einsum("whqk,wkhd->wqhd", delta_scores, window_keys, preferred_element_type=jnp.float32)
        * score_scale
    )
    delta_key = (
        jnp.einsum("whqk,wqhd->wkhd", delta_scores, queries, preferred_element_type=jnp.float32)
        * score_scale
    )
    delta_value = jnp.einsum(
        "whqk,wqhd->wkhd", weights_rounded, delta_window_rows, preferred_element_type=jnp.float32
    )
    delta_joint = jnp.concatenate(
        [
            delta_query.reshape(node_count, C),
            delta_key.reshape(node_count, C),
            delta_value.reshape(node_count, C),
        ],
        axis=1,
    ).astype(jnp.bfloat16)
    delta_projected = out_of_windows(delta_joint)
    delta_joint_weight = contract_rows(attend_input, delta_projected)
    joint_sums = jnp.sum(delta_projected.astype(jnp.float32), axis=0)
    delta_attend_input = contract_last(delta_projected, params["joint_weight"])
    delta_norm_one, delta_first_gain, delta_first_shift = first_norm_back(delta_attend_input)
    delta_first = delta_second + delta_norm_one
    local_gain = jnp.sum(delta_first * centered, axis=0)
    local_shift = jnp.sum(delta_first, axis=0)
    gain_total, shift_total, bias_total = lax.psum(
        (local_gain, local_shift, delta_final_bias), ("rows", "grp")
    )
    sum_centered = batch_gain * shift_total
    sum_spread = batch_gain * gain_total / inverse_scale
    delta_variance = -0.5 * inverse_scale * inverse_scale * inverse_scale * sum_spread
    delta_average = -sum_centered * inverse_scale - 2.0 * average * delta_variance
    delta_conv = (
        delta_first * batch_gain * inverse_scale
        + live_rows * (delta_average + 2.0 * convolved * delta_variance) / live_total
    )
    delta_conv = delta_conv.astype(jnp.bfloat16).astype(jnp.float32)
    delta_extended = jnp.zeros((node_count + 2 * HALO, C), jnp.float32)
    conv_rows = []
    for offset_index in range(27):
        column_index = local_index[:, offset_index]
        present_column = present_float[:, offset_index : offset_index + 1]
        picked = jnp.take(extended, column_index, axis=0).astype(jnp.float32)
        conv_rows.append(jnp.sum(delta_conv * picked * present_column, axis=0))
        delta_extended = delta_extended.at[column_index].add(
            delta_conv * present_column * conv_weight[offset_index]
        )
    delta_conv_weight = jnp.stack(conv_rows)
    edge_rows = jnp.concatenate(
        [delta_extended[:HALO], delta_extended[node_count + HALO :]], axis=0
    )
    padded = extended_2(edge_rows.astype(jnp.bfloat16), ((("rows", "grp"), 0),), HALO).astype(
        edge_rows.dtype
    )
    delta_inner = delta_extended[HALO : node_count + HALO]
    delta_inner = delta_inner.at[:HALO].add(padded[:HALO])
    delta_inner = delta_inner.at[node_count - HALO :].add(padded[3 * HALO :])
    node_grad = delta_first + delta_inner
    gradients = {
        "batch_gain": local_gain,
        "batch_shift": local_shift,
        "first_gain": delta_first_gain,
        "first_shift": delta_first_shift,
        "query_bias": joint_sums[:C],
        "value_bias": joint_sums[2 * C :],
        "output_bias": delta_output_bias,
        "second_gain": delta_second_gain,
        "second_shift": delta_second_shift,
        "hidden_bias": delta_hidden_bias,
        "final_bias": delta_final_bias,
        "conv_weight": delta_conv_weight,
        "joint_weight": delta_joint_weight,
        "output_weight": delta_output_weight,
        "hidden_weight": delta_hidden_weight,
        "final_weight": delta_final_weight,
    }
    flat_grads = jnp.concatenate(
        [gradients[segment_name].reshape(-1) for segment_name, segment_shape in layout(C, F)]
    )
    shard_size = master.shape[0]
    total_params = shard_size * lax.axis_size(("rows", "grp"))
    flat_grads = jnp.pad(flat_grads, (0, total_params - flat_grads.shape[0]))
    shard_delta = lax.psum_scatter(flat_grads, ("rows", "grp"), scatter_dimension=0, tiled=True)
    position = lax.axis_index(("rows", "grp")) * shard_size + lax.iota(jnp.int32, shard_size)
    step_rate = jnp.where(position < 10 * C + F, 0.2, 0.03)
    new_first = 0.9 * first_moment + 0.1 * shard_delta
    new_second = 0.95 * second_moment + 0.05 * shard_delta * shard_delta
    first_hat = new_first / (1.0 - 0.9**STEP)
    second_hat = new_second / (1.0 - 0.95**STEP)
    new_master = master - step_rate * (first_hat / (jnp.sqrt(second_hat) + 1e-08) + 0.01 * master)
    return (
        output,
        node_grad,
        new_master,
        new_first,
        new_second,
        new_master.astype(jnp.bfloat16),
        bias_total,
    )


def solution(mesh):
    in_specs = (
        P(("rows", "grp"), None),
        P(("rows", "grp"), None),
        P(("rows", "grp"), None),
        P(("rows", "grp")),
        P(("rows", "grp")),
        P(("rows", "grp")),
        P(("rows", "grp")),
    )
    out_specs = (
        P(("rows", "grp"), None),
        P(("rows", "grp"), None),
        P(("rows", "grp")),
        P(("rows", "grp")),
        P(("rows", "grp")),
        P(("rows", "grp")),
        P(),
    )
    return jax.shard_map(shards, mesh=mesh, in_specs=in_specs, out_specs=out_specs, check_vma=False)
```

profile of v0, /device:TPU:0, one launch (start us, length us, event | category | flops | bytes accessed | tf_op | source)
XLA Modules:
  0.0 2575.4 jit_solution(18132532627541293031)
XLA Ops:
  41.0 17.3 gather_fusion.16
  58.3 17.1 gather_fusion.17
  92.6 17.2 gather_fusion.19
  109.7 17.1 gather_fusion.20
  126.9 17.1 gather_fusion.21
  144.0 17.2 gather_fusion.22
  178.3 17.2 gather_fusion.24
  195.4 17.2 gather_fusion.25
  229.7 17.1 gather_fusion
  264.0 17.1 gather_fusion.2
  400.9 17.2 gather_fusion.10
  486.5 17.1 gather_fusion.15
  503.7 57.2 %reduce.6 = bf16[32,55808]{1,0:T(8,128)(2,1)} reduce(bf16[32,1,55808]{2,1,0:T(2,128)(2,1)} %all-gather.3.cloned.1.call-done, bf16[]{:T(256)} %constant.156), dimensions={1}, to_apply=%all-gather.reduce_sub_computation | reduce | bytes 7143426 | tf_op jit(solution)/shard_map/all_gather | solution.py:112
  581.7 85.1 %fusion.68 = (f32[384]{0:T(512)}, f32[384]{0:T(512)}, f32[4096,384]{1,0:T(8,128)}) fusion(f32[4096]{0:T(1024)} %convert_element_type.257, f32[384]{0:T(512)} %get-tuple-element.200, f32[4096]{0:T(1024)S(1)} %bitcast.152, bf16[4096,384]{1,0:T(8,128)(2,1)S(1)} %copy-done.4, pred[4096]{0:T(1024)(128)(4,1)} %get-tuple-element.234, f32[384]{0:T(512)} %get-tuple-element.201, ...), kind=kLoop, calls=%fused_computation.215 | loop fusion | flops 217054464 | bytes 91840000 | tf_op jit(solution)/shard_map/reduce_sum | solution.py:135
  666.8 44.8 %all-reduce.3 = (f32[384]{0:T(512)S(1)}, f32[]{:T(128)}, f32[384]{0:T(512)S(1)}) all-reduce(f32[384]{0:T(512)} %get-tuple-element.37, f32[]{:T(128)} %convert_reduce_fusion.4, f32[384]{0:T(512)} %get-tuple-element.36), channel_id=1, replica_groups=mesh['rows'=16,'grp'=2] {'rows','grp'}, use_global_device_ids=true, to_apply=%region_1.3 | all-reduce | flops 769 | bytes 6152 | tf_op jit(solution)/shard_map/psum | solution.py:132
  764.9 19.1 reshape.821
  784.0 21.4 copy.113
  805.4 19.2 reshape.820
  824.6 21.5 copy.117
  846.0 19.4 fusion.329
  865.4 20.5 copy.104
  898.0 17.8 copy.106
  931.0 17.5 fusion.12
  978.4 20.8 multiply_convert_fusion
  999.2 26.5 %convert_reduce_fusion = (f32[1536]{0:T(1024)}, bf16[4096,1536]{1,0:T(8,128)(2,1)}) fusion(f32[4096,1536]{1,0:T(8,128)} %get-tuple-element.229, f32[1536]{0:T(1024)S(1)} %copy-done.173, bf16[4096,384]{1,0:T(8,128)(2,1)S(1)} %copy-done.31, bf16[1536,384]{1,0:T(8,128)(2,1)S(1)} %reshape.295), kind=kOutput, calls=%fused_computation.118 | convolution fusion | flops 4976540160 | bytes 42086400 | tf_op jit(solution)/shard_map/dot_general | solution.py:79
  1070.8 17.9 fusion.10
  1088.7 20.5 copy.112
  1138.0 20.6 fusion.330
  1175.4 19.6 copy.115
  1198.6 26.9 %copy.116 = bf16[128,32,12,32]{3,2,1,0:T(8,128)(2,1)} copy(bf16[128,32,12,32]{0,1,3,2:T(8,128)(2,1)S(1)} %fusion.212) | data formatting | bytes 6291456 | tf_op jit(solution)/shard_map/mul | solution.py:218
  1225.5 19.5 concatenate.32
  1245.1 19.6 copy.119
  1268.3 26.9 %copy.120 = bf16[128,32,12,32]{3,2,1,0:T(8,128)(2,1)} copy(bf16[128,32,12,32]{0,1,3,2:T(8,128)(2,1)S(1)} %fusion.213) | data formatting | bytes 6291456 | tf_op jit(solution)/shard_map/mul | solution.py:222
  1295.2 19.7 concatenate.33
  1417.3 41.0 %all-reduce.2 = (f32[384]{0:T(512)S(1)}, f32[384]{0:T(512)S(1)}, f32[384]{0:T(512)}) all-reduce(f32[384]{0:T(512)S(1)} %get-tuple-element.41, f32[384]{0:T(512)S(1)} %get-tuple-element.40, f32[384]{0:T(512)S(1)} %get-tuple-element.115), channel_id=1, replica_groups=mesh['rows'=16,'grp'=2] {'rows','grp'}, use_global_device_ids=true, to_apply=%region_20.22 | all-reduce | flops 1152 | bytes 9216 | tf_op jit(solution)/shard_map/psum | solution.py:244
  1620.5 21.3 dynamic-update-slice.20
  1641.8 21.1 dynamic-update-slice.21
  1671.3 29.9 %scatter_custom_fusion = f32[4224,384]{1,0:T(8,128)} fusion(s32[4096]{0:T(1024)} %bitcast.314, bf16[4096,384]{1,0:T(8,128)(2,1)S(1)} %get-tuple-element.79, f32[]{:T(128)} %constant.120.clone.1, f32[384]{0:T(512)} %get-tuple-element.199, f32[4096]{0:T(1024)} %bitcast.231), kind=kCustom, calls=%fused_computation.217 | custom fusion | flops 6291456 | bytes 9652736 | tf_op jit(solution)/shard_map/scatter-add | solution.py:263
  1701.2 32.2 %scatter_custom_fusion.1 = f32[4224,384]{1,0:T(8,128)} fusion(f32[4224,384]{1,0:T(8,128)} %scatter_custom_fusion, s32[4096]{0:T(1024)} %bitcast.313, bf16[4096,384]{1,0:T(8,128)(2,1)S(1)} %get-tuple-element.79, f32[384]{0:T(512)} %get-tuple-element.218, f32[4096]{0:T(1024)} %bitcast.228), kind=kCustom, calls=%fused_computation.219 | custom fusion | flops 6291456 | bytes 9652224 | tf_op jit(solution)/shard_map/scatter-add | solution.py:263
  1733.4 32.3 %scatter_custom_fusion.2 = f32[4224,384]{1,0:T(8,128)} fusion(f32[4224,384]{1,0:T(8,128)} %scatter_custom_fusion.1, s32[4096]{0:T(1024)} %bitcast.312, bf16[4096,384]{1,0:T(8,128)(2,1)S(1)} %get-tuple-element.79, f32[384]{0:T(512)} %get-tuple-element.225, f32[4096]{0:T(1024)S(1)} %bitcast.226), kind=kCustom, calls=%fused_computation.221 | custom fusion | flops 6291456 | bytes 9652224 | tf_op jit(solution)/shard_map/scatter-add | solution.py:263
  1765.7 33.0 %scatter_custom_fusion.3 = f32[4224,384]{1,0:T(8,128)} fusion(f32[4224,384]{1,0:T(8,128)} %scatter_custom_fusion.2, s32[4096]{0:T(1024)} %bitcast.311, bf16[4096,384]{1,0:T(8,128)(2,1)S(1)} %get-tuple-element.79, f32[384]{0:T(512)} %get-tuple-element.224, f32[4096]{0:T(1024)S(1)} %bitcast.223), kind=kCustom, calls=%fused_computation.223 | custom fusion | flops 6291456 | bytes 9652224 | tf_op jit(solution)/shard_map/scatter-add | solution.py:263
  1798.7 32.7 %scatter_custom_fusion.4 = f32[4224,384]{1,0:T(8,128)} fusion(f32[4224,384]{1,0:T(8,128)} %scatter_custom_fusion.3, s32[4096]{0:T(1024)} %bitcast.310, bf16[4096,384]{1,0:T(8,128)(2,1)S(1)} %get-tuple-element.79, f32[384]{0:T(512)S(1)} %copy-done.169, f32[4096]{0:T(1024)S(1)} %bitcast.220), kind=kCustom, calls=%fused_computation.225 | custom fusion | flops 6291456 | bytes 9651712 | tf_op jit(solution)/shard_map/scatter-add | solution.py:263
  1831.4 32.3 %scatter_custom_fusion.5 = f32[4224,384]{1,0:T(8,128)} fusion(f32[4224,384]{1,0:T(8,128)} %scatter_custom_fusion.4, s32[4096]{0:T(1024)} %bitcast.309, bf16[4096,384]{1,0:T(8,128)(2,1)S(1)} %get-tuple-element.79, f32[384]{0:T(512)S(1)} %copy-done.168, f32[4096]{0:T(1024)S(1)} %bitcast.217), kind=kCustom, calls=%fused_computation.227 | custom fusion | flops 6291456 | bytes 9651712 | tf_op jit(solution)/shard_map/scatter-add | solution.py:263
  1863.7 32.7 %scatter_custom_fusion.6 = f32[4224,384]{1,0:T(8,128)} fusion(f32[4224,384]{1,0:T(8,128)} %scatter_custom_fusion.5, s32[4096]{0:T(1024)} %bitcast.308, bf16[4096,384]{1,0:T(8,128)(2,1)S(1)} %get-tuple-element.79, f32[384]{0:T(512)S(1)} %copy-done.167, f32[4096]{0:T(1024)S(1)} %bitcast.214), kind=kCustom, calls=%fused_computation.229 | custom fusion | flops 6291456 | bytes 9651712 | tf_op jit(solution)/shard_map/scatter-add | solution.py:263
  1896.4 32.3 %scatter_custom_fusion.7 = f32[4224,384]{1,0:T(8,128)} fusion(f32[4224,384]{1,0:T(8,128)} %scatter_custom_fusion.6, s32[4096]{0:T(1024)} %bitcast.307, bf16[4096,384]{1,0:T(8,128)(2,1)S(1)} %get-tuple-element.79, f32[384]{0:T(512)S(1)} %copy-done.166, f32[4096]{0:T(1024)S(1)} %bitcast.211), kind=kCustom, calls=%fused_computation.231 | custom fusion | flops 6291456 | bytes 9651712 | tf_op jit(solution)/shard_map/scatter-add | solution.py:263
  1928.7 32.3 %scatter_custom_fusion.8 = f32[4224,384]{1,0:T(8,128)} fusion(f32[4224,384]{1,0:T(8,128)} %scatter_custom_fusion.7, s32[4096]{0:T(1024)} %bitcast.306, bf16[4096,384]{1,0:T(8,128)(2,1)S(1)} %get-tuple-element.79, f32[384]{0:T(512)S(1)} %copy-done.165, f32[4096]{0:T(1024)S(1)} %bitcast.208), kind=kCustom, calls=%fused_computation.233 | custom fusion | flops 6291456 | bytes 9651712 | tf_op jit(solution)/shard_map/scatter-add | solution.py:263
  1961.0 32.5 %scatter_custom_fusion.9 = f32[4224,384]{1,0:T(8,128)} fusion(f32[4224,384]{1,0:T(8,128)} %scatter_custom_fusion.8, s32[4096]{0:T(1024)} %bitcast.305, bf16[4096,384]{1,0:T(8,128)(2,1)S(1)} %get-tuple-element.79, f32[384]{0:T(512)S(1)} %copy-done.164, f32[4096]{0:T(1024)S(1)} %bitcast.205), kind=kCustom, calls=%fused_computation.235 | custom fusion | flops 6291456 | bytes 9651712 | tf_op jit(solution)/shard_map/scatter-add | solution.py:263
  1993.5 32.3 %scatter_custom_fusion.10 = f32[4224,384]{1,0:T(8,128)} fusion(f32[4224,384]{1,0:T(8,128)} %scatter_custom_fusion.9, s32[4096]{0:T(1024)} %bitcast.304, bf16[4096,384]{1,0:T(8,128)(2,1)S(1)} %get-tuple-element.79, f32[384]{0:T(512)S(1)} %copy-done.163, f32[4096]{0:T(1024)S(1)} %bitcast.202), kind=kCustom, calls=%fused_computation.237 | custom fusion | flops 6291456 | bytes 9651712 | tf_op jit(solution)/shard_map/scatter-add | solution.py:263
  2025.8 32.3 %scatter_custom_fusion.11 = f32[4224,384]{1,0:T(8,128)} fusion(f32[4224,384]{1,0:T(8,128)} %scatter_custom_fusion.10, s32[4096]{0:T(1024)} %bitcast.303, bf16[4096,384]{1,0:T(8,128)(2,1)S(1)} %get-tuple-element.79, f32[384]{0:T(512)S(1)} %copy-done.162, f32[4096]{0:T(1024)S(1)} %bitcast.199), kind=kCustom, calls=%fused_computation.239 | custom fusion | flops 6291456 | bytes 9651712 | tf_op jit(solution)/shard_map/scatter-add | solution.py:263
  2058.1 32.5 %scatter_custom_fusion.12 = f32[4224,384]{1,0:T(8,128)} fusion(f32[4224,384]{1,0:T(8,128)} %scatter_custom_fusion.11, s32[4096]{0:T(1024)} %bitcast.302, bf16[4096,384]{1,0:T(8,128)(2,1)S(1)} %get-tuple-element.79, f32[384]{0:T(512)S(1)} %copy-done.161, f32[4096]{0:T(1024)S(1)} %bitcast.196), kind=kCustom, calls=%fused_computation.241 | custom fusion | flops 6291456 | bytes 9651712 | tf_op jit(solution)/shard_map/scatter-add | solution.py:263
  2090.6 32.3 %scatter_custom_fusion.13 = f32[4224,384]{1,0:T(8,128)} fusion(f32[4224,384]{1,0:T(8,128)} %scatter_custom_fusion.12, s32[4096]{0:T(1024)} %bitcast.301, bf16[4096,384]{1,0:T(8,128)(2,1)S(1)} %get-tuple-element.79, f32[384]{0:T(512)S(1)} %copy-done.160, f32[4096]{0:T(1024)S(1)} %bitcast.193), kind=kCustom, calls=%fused_computation.243 | custom fusion | flops 6291456 | bytes 9651712 | tf_op jit(solution)/shard_map/scatter-add | solution.py:263
  2122.9 32.3 %scatter_custom_fusion.14 = f32[4224,384]{1,0:T(8,128)} fusion(f32[4224,384]{1,0:T(8,128)} %scatter_custom_fusion.13, s32[4096]{0:T(1024)} %bitcast.300, bf16[4096,384]{1,0:T(8,128)(2,1)S(1)} %get-tuple-element.79, f32[384]{0:T(512)S(1)} %copy-done.159, f32[4096]{0:T(1024)S(1)} %bitcast.190), kind=kCustom, calls=%fused_computation.245 | custom fusion | flops 6291456 | bytes 9651712 | tf_op jit(solution)/shard_map/scatter-add | solution.py:263
  2155.2 32.7 %scatter_custom_fusion.15 = f32[4224,384]{1,0:T(8,128)} fusion(f32[4224,384]{1,0:T(8,128)} %scatter_custom_fusion.14, s32[4096]{0:T(1024)} %bitcast.299, bf16[4096,384]{1,0:T(8,128)(2,1)S(1)} %get-tuple-element.79, f32[384]{0:T(512)S(1)} %copy-done.158, f32[4096]{0:T(1024)S(1)} %bitcast.187), kind=kCustom, calls=%fused_computation.247 | custom fusion | flops 6291456 | bytes 9651712 | tf_op jit(solution)/shard_map/scatter-add | solution.py:263
  2187.9 32.3 %scatter_custom_fusion.16 = f32[4224,384]{1,0:T(8,128)} fusion(f32[4224,384]{1,0:T(8,128)} %scatter_custom_fusion.15, s32[4096]{0:T(1024)} %bitcast.298, bf16[4096,384]{1,0:T(8,128)(2,1)S(1)} %get-tuple-element.79, f32[384]{0:T(512)S(1)} %copy-done.157, f32[4096]{0:T(1024)S(1)} %bitcast.184), kind=kCustom, calls=%fused_computation.249 | custom fusion | flops 6291456 | bytes 9651712 | tf_op jit(solution)/shard_map/scatter-add | solution.py:263
  2220.2 32.3 %scatter_custom_fusion.17 = f32[4224,384]{1,0:T(8,128)} fusion(f32[4224,384]{1,0:T(8,128)} %scatter_custom_fusion.16, s32[4096]{0:T(1024)} %bitcast.297, bf16[4096,384]{1,0:T(8,128)(2,1)S(1)} %get-tuple-element.79, f32[384]{0:T(512)S(1)} %copy-done.156, f32[4096]{0:T(1024)S(1)} %bitcast.181), kind=kCustom, calls=%fused_computation.251 | custom fusion | flops 6291456 | bytes 9651712 | tf_op jit(solution)/shard_map/scatter-add | solution.py:263
  2252.5 32.5 %scatter_custom_fusion.18 = f32[4224,384]{1,0:T(8,128)} fusion(f32[4224,384]{1,0:T(8,128)} %scatter_custom_fusion.17, s32[4096]{0:T(1024)} %bitcast.295, bf16[4096,384]{1,0:T(8,128)(2,1)S(1)} %get-tuple-element.79, f32[384]{0:T(512)S(1)} %copy-done.155, f32[4096]{0:T(1024)S(1)} %bitcast.178), kind=kCustom, calls=%fused_computation.253 | custom fusion | flops 6291456 | bytes 9651712 | tf_op jit(solution)/shard_map/scatter-add | solution.py:263
  2285.0 32.3 %scatter_custom_fusion.19 = f32[4224,384]{1,0:T(8,128)} fusion(f32[4224,384]{1,0:T(8,128)} %scatter_custom_fusion.18, s32[4096]{0:T(1024)} %bitcast.294, bf16[4096,384]{1,0:T(8,128)(2,1)S(1)} %get-tuple-element.79, f32[384]{0:T(512)S(1)} %copy-done.154, f32[4096]{0:T(1024)S(1)} %bitcast.175), kind=kCustom, calls=%fused_computation.255 | custom fusion | flops 6291456 | bytes 9651712 | tf_op jit(solution)/shard_map/scatter-add | solution.py:263
  2317.3 32.3 %scatter_custom_fusion.20 = f32[4224,384]{1,0:T(8,128)} fusion(f32[4224,384]{1,0:T(8,128)} %scatter_custom_fusion.19, s32[4096]{0:T(1024)} %bitcast.293, bf16[4096,384]{1,0:T(8,128)(2,1)S(1)} %get-tuple-element.79, f32[384]{0:T(512)S(1)} %copy-done.153, f32[4096]{0:T(1024)S(1)} %bitcast.172), kind=kCustom, calls=%fused_computation.257 | custom fusion | flops 6291456 | bytes 9651712 | tf_op jit(solution)/shard_map/scatter-add | solution.py:263
  2349.6 32.5 %scatter_custom_fusion.21 = f32[4224,384]{1,0:T(8,128)} fusion(f32[4224,384]{1,0:T(8,128)} %scatter_custom_fusion.20, s32[4096]{0:T(1024)} %bitcast.292, bf16[4096,384]{1,0:T(8,128)(2,1)S(1)} %get-tuple-element.79, f32[384]{0:T(512)S(1)} %copy-done.152, f32[4096]{0:T(1024)S(1)} %bitcast.169), kind=kCustom, calls=%fused_computation.259 | custom fusion | flops 6291456 | bytes 9651712 | tf_op jit(solution)/shard_map/scatter-add | solution.py:263
  2382.1 32.3 %scatter_custom_fusion.22 = f32[4224,384]{1,0:T(8,128)} fusion(f32[4224,384]{1,0:T(8,128)} %scatter_custom_fusion.21, s32[4096]{0:T(1024)} %bitcast.291, bf16[4096,384]{1,0:T(8,128)(2,1)S(1)} %get-tuple-element.79, f32[384]{0:T(512)S(1)} %copy-done.151, f32[4096]{0:T(1024)S(1)} %bitcast.166), kind=kCustom, calls=%fused_computation.261 | custom fusion | flops 6291456 | bytes 9651712 | tf_op jit(solution)/shard_map/scatter-add | solution.py:263
  2414.4 32.3 %scatter_custom_fusion.23 = f32[4224,384]{1,0:T(8,128)} fusion(f32[4224,384]{1,0:T(8,128)} %scatter_custom_fusion.22, s32[4096]{0:T(1024)} %bitcast.290, bf16[4096,384]{1,0:T(8,128)(2,1)S(1)} %get-tuple-element.79, f32[384]{0:T(512)S(1)} %copy-done.150, f32[4096]{0:T(1024)S(1)} %bitcast.163), kind=kCustom, calls=%fused_computation.263 | custom fusion | flops 6291456 | bytes 9651712 | tf_op jit(solution)/shard_map/scatter-add | solution.py:263
  2446.7 32.7 %scatter_custom_fusion.24 = f32[4224,384]{1,0:T(8,128)} fusion(f32[4224,384]{1,0:T(8,128)} %scatter_custom_fusion.23, s32[4096]{0:T(1024)} %bitcast.289, bf16[4096,384]{1,0:T(8,128)(2,1)S(1)} %get-tuple-element.79, f32[384]{0:T(512)S(1)} %copy-done.149, f32[4096]{0:T(1024)S(1)} %bitcast.160), kind=kCustom, calls=%fused_computation.265 | custom fusion | flops 6291456 | bytes 9651712 | tf_op jit(solution)/shard_map/scatter-add | solution.py:263
  2479.4 32.3 %scatter_custom_fusion.25 = f32[4224,384]{1,0:T(8,128)} fusion(f32[4224,384]{1,0:T(8,128)} %scatter_custom_fusion.24, s32[4096]{0:T(1024)} %bitcast.288, bf16[4096,384]{1,0:T(8,128)(2,1)S(1)} %get-tuple-element.79, f32[384]{0:T(512)S(1)} %copy-done.148, f32[4096]{0:T(1024)S(1)} %bitcast.157), kind=kCustom, calls=%fused_computation.267 | custom fusion | flops 6291456 | bytes 9651712 | tf_op jit(solution)/shard_map/scatter-add | solution.py:263
  2511.7 32.3 %scatter_custom_fusion.26 = f32[4224,384]{1,0:T(8,128)} fusion(f32[4224,384]{1,0:T(8,128)} %scatter_custom_fusion.25, s32[4096]{0:T(1024)} %bitcast.296, bf16[4096,384]{1,0:T(8,128)(2,1)S(1)} %get-tuple-element.79, f32[384]{0:T(512)S(1)} %copy-done.147, f32[4096]{0:T(1024)S(1)} %bitcast.154), kind=kCustom, calls=%fused_computation.269 | custom fusion | flops 6291456 | bytes 9651712 | tf_op jit(solution)/shard_map/scatter-add | solution.py:263
  (605 shorter events, 814.9 us)
Async XLA Ops:
  7.2 26.9 %copy-start.106 = (s32[4096]{0:T(1024)S(1)}, s32[4096]{0:T(1024)}, u32[]{:S(2)}) copy-start(s32[4096]{0:T(1024)} %param.16) | copy-start | bytes 49156
  7.2 496.5 %all-gather.3.cloned.1.call-start = ((), (), s32[]{:S(2)}) async-start(), calls=%async_computation | async-start | bytes 7366656 | tf_op jit(solution)/shard_map/all_gather | solution.py:112
  8.7 28.1 %collective-permute-start = (bf16[64,384]{1,0:T(8,128)(2,1)S(1)}, bf16[64,384]{1,0:T(8,128)(2,1)}, u32[]{:S(2)}, u32[]{:S(2)}) collective-permute-start(bf16[64,384]{1,0:T(8,128)(2,1)S(1)} %get-tuple-element.117), channel_id=1, source_target_pairs={{0,1},{1,2},{2,3},{3,4},{4,5},{5,6},{6,7},{7,8},{8,9},{9,10},{10,1... | collective-permute-start | bytes 147464 | tf_op jit(solution)/shard_map/ppermute | solution.py:27
  11.6 28.5 %collective-permute-start.1 = (bf16[64,384]{1,0:T(8,128)(2,1)}, bf16[64,384]{1,0:T(8,128)(2,1)}, u32[]{:S(2)}, u32[]{:S(2)}) collective-permute-start(bf16[64,384]{1,0:T(8,128)(2,1)} %get-tuple-element.116), channel_id=1, source_target_pairs={{1,0},{2,1},{3,2},{4,3},{5,4},{6,5},{7,6},{8,7},{9,8},{10,9},{11,1... | collective-permute-start | bytes 147464 | tf_op jit(solution)/shard_map/ppermute | solution.py:30
  14.7 2551.6 %all-reduce.6.cloned.1.call-start = ((), (), s32[]{:S(2)}) async-start(), calls=%async_computation.1 | async-start | bytes 14286848
  560.9 20.6 copy-start.55
  560.9 20.6 copy-start.57
  560.9 20.6 copy-start.59
  560.9 20.6 copy-start.61
  561.0 20.6 copy-start.63
  561.0 20.6 copy-start.65
  561.0 20.6 copy-start.67
  561.0 20.6 copy-start.69
  561.0 20.6 copy-start.71
  561.0 20.6 copy-start.73
  561.0 20.6 copy-start.75
  561.0 20.6 copy-start.77
  561.0 20.6 copy-start.79
  561.0 20.6 copy-start.81
  561.1 20.6 copy-start.83
  561.1 20.6 copy-start.85
  978.4 20.9 copy-start.39
  978.4 20.8 copy-start.31
  978.4 47.3 %slice-start.4 = ((s8[6291456]{0:T(1024)(128)(4,1)}), s8[4194304]{0:T(1024)(128)(4,1)S(1)}, s32[]{:S(2)}) async-start(s8[6291456]{0:T(1024)(128)(4,1)} %bitcast.138), calls=%async_computation.6 | async-start | bytes 8388608
  999.2 26.5 %slice-start.5 = ((s8[6291456]{0:T(1024)(128)(4,1)}), s8[2097152]{0:T(1024)(128)(4,1)S(1)}, s32[]{:S(2)}) async-start(s8[6291456]{0:T(1024)(128)(4,1)} %bitcast.138), calls=%async_computation.7 | async-start | bytes 4194304
  1368.6 27.4 %slice-start = ((s8[6291456]{0:T(1024)(128)(4,1)}), s8[2097152]{0:T(1024)(128)(4,1)S(1)}, s32[]{:S(2)}) async-start(s8[6291456]{0:T(1024)(128)(4,1)} %bitcast.134), calls=%async_computation.2 | async-start | bytes 4194304
  1384.5 28.3 %slice-start.2 = ((s8[6291456]{0:T(1024)(128)(4,1)}), s8[4194304]{0:T(1024)(128)(4,1)S(1)}, s32[]{:S(2)}) async-start(s8[6291456]{0:T(1024)(128)(4,1)} %bitcast.136), calls=%async_computation.4 | async-start | bytes 8388608
  1384.5 28.3 %slice-start.8 = ((s8[6291456]{0:T(1024)(128)(4,1)}), s8[4194304]{0:T(1024)(128)(4,1)S(1)}, s32[]{:S(2)}) async-start(s8[6291456]{0:T(1024)(128)(4,1)} %bitcast.144), calls=%async_computation.10 | async-start | bytes 8388608
  1412.9 46.0 %copy-start.56 = (f32[4096,1]{0,1:T(1,128)S(1)}, f32[4096,1]{0,1:T(1,128)}, u32[]{:S(2)}) copy-start(f32[4096,1]{0,1:T(1,128)} %get-tuple-element.177) | copy-start | bytes 49156
  1412.9 46.0 %copy-start.58 = (f32[4096,1]{0,1:T(1,128)S(1)}, f32[4096,1]{0,1:T(1,128)}, u32[]{:S(2)}) copy-start(f32[4096,1]{0,1:T(1,128)} %get-tuple-element.178) | copy-start | bytes 49156
  1412.9 46.0 %copy-start.60 = (f32[4096,1]{0,1:T(1,128)S(1)}, f32[4096,1]{0,1:T(1,128)}, u32[]{:S(2)}) copy-start(f32[4096,1]{0,1:T(1,128)} %get-tuple-element.179) | copy-start | bytes 49156
  1412.9 46.0 %copy-start.107 = (f32[4096]{0:T(1024)S(1)}, f32[4096]{0:T(1024)}, u32[]{:S(2)}) copy-start(f32[4096]{0:T(1024)} %convert_element_type.257) | copy-start | bytes 49156
  1413.0 46.0 %copy-start.137 = (pred[4096]{0:T(1024)(128)(4,1)S(1)}, pred[4096]{0:T(1024)(128)(4,1)}, u32[]{:S(2)}) copy-start(pred[4096]{0:T(1024)(128)(4,1)} %get-tuple-element.238) | copy-start | bytes 12292
  1413.0 46.0 %copy-start.138 = (pred[4096]{0:T(1024)(128)(4,1)S(1)}, pred[4096]{0:T(1024)(128)(4,1)}, u32[]{:S(2)}) copy-start(pred[4096]{0:T(1024)(128)(4,1)} %get-tuple-element.239) | copy-start | bytes 12292
  1413.0 46.0 %copy-start.139 = (pred[4096]{0:T(1024)(128)(4,1)S(1)}, pred[4096]{0:T(1024)(128)(4,1)}, u32[]{:S(2)}) copy-start(pred[4096]{0:T(1024)(128)(4,1)} %get-tuple-element.240) | copy-start | bytes 12292
  1413.0 46.0 %copy-start.142 = (f32[384]{0:T(512)S(1)}, f32[384]{0:T(512)}, u32[]{:S(2)}) copy-start(f32[384]{0:T(512)} %get-tuple-element.110) | copy-start | bytes 4612
  1417.3 41.6 %copy-start.144 = (f32[384]{0:T(512)}, f32[384]{0:T(512)S(1)}, u32[]{:S(2)}) copy-start(f32[384]{0:T(512)S(1)} %get-tuple-element.115) | copy-start | bytes 4612
  1417.3 41.6 %copy-start.145 = (f32[384]{0:T(512)}, f32[384]{0:T(512)S(1)}, u32[]{:S(2)}) copy-start(f32[384]{0:T(512)S(1)} %get-tuple-element.40) | copy-start | bytes 4612
  1417.3 41.7 %copy-start.146 = (f32[384]{0:T(512)}, f32[384]{0:T(512)S(1)}, u32[]{:S(2)}) copy-start(f32[384]{0:T(512)S(1)} %get-tuple-element.41) | copy-start | bytes 4612
  1765.7 33.0 %copy-start.169 = (f32[384]{0:T(512)S(1)}, f32[384]{0:T(512)}, u32[]{:S(2)}) copy-start(f32[384]{0:T(512)} %get-tuple-element.223) | copy-start | bytes 4612
  1798.7 32.7 %copy-start.168 = (f32[384]{0:T(512)S(1)}, f32[384]{0:T(512)}, u32[]{:S(2)}) copy-start(f32[384]{0:T(512)} %get-tuple-element.222) | copy-start | bytes 4612
  1831.4 32.3 %copy-start.167 = (f32[384]{0:T(512)S(1)}, f32[384]{0:T(512)}, u32[]{:S(2)}) copy-start(f32[384]{0:T(512)} %get-tuple-element.221) | copy-start | bytes 4612
  1863.7 32.7 %copy-start.166 = (f32[384]{0:T(512)S(1)}, f32[384]{0:T(512)}, u32[]{:S(2)}) copy-start(f32[384]{0:T(512)} %get-tuple-element.220) | copy-start | bytes 4612
  1896.4 32.3 %copy-start.165 = (f32[384]{0:T(512)S(1)}, f32[384]{0:T(512)}, u32[]{:S(2)}) copy-start(f32[384]{0:T(512)} %get-tuple-element.219) | copy-start | bytes 4612
  1928.7 32.3 %copy-start.164 = (f32[384]{0:T(512)S(1)}, f32[384]{0:T(512)}, u32[]{:S(2)}) copy-start(f32[384]{0:T(512)} %get-tuple-element.217) | copy-start | bytes 4612
  1961.0 32.5 %copy-start.163 = (f32[384]{0:T(512)S(1)}, f32[384]{0:T(512)}, u32[]{:S(2)}) copy-start(f32[384]{0:T(512)} %get-tuple-element.216) | copy-start | bytes 4612
  1993.5 32.3 %copy-start.162 = (f32[384]{0:T(512)S(1)}, f32[384]{0:T(512)}, u32[]{:S(2)}) copy-start(f32[384]{0:T(512)} %get-tuple-element.215) | copy-start | bytes 4612
  2025.8 32.3 %copy-start.161 = (f32[384]{0:T(512)S(1)}, f32[384]{0:T(512)}, u32[]{:S(2)}) copy-start(f32[384]{0:T(512)} %get-tuple-element.214) | copy-start | bytes 4612
  2058.1 32.5 %copy-start.160 = (f32[384]{0:T(512)S(1)}, f32[384]{0:T(512)}, u32[]{:S(2)}) copy-start(f32[384]{0:T(512)} %get-tuple-element.213) | copy-start | bytes 4612
  2090.6 32.3 %copy-start.159 = (f32[384]{0:T(512)S(1)}, f32[384]{0:T(512)}, u32[]{:S(2)}) copy-start(f32[384]{0:T(512)} %get-tuple-element.212) | copy-start | bytes 4612
  2122.9 32.3 %copy-start.158 = (f32[384]{0:T(512)S(1)}, f32[384]{0:T(512)}, u32[]{:S(2)}) copy-start(f32[384]{0:T(512)} %get-tuple-element.211) | copy-start | bytes 4612
  2155.2 32.7 %copy-start.157 = (f32[384]{0:T(512)S(1)}, f32[384]{0:T(512)}, u32[]{:S(2)}) copy-start(f32[384]{0:T(512)} %get-tuple-element.210) | copy-start | bytes 4612
  2187.9 32.3 %copy-start.156 = (f32[384]{0:T(512)S(1)}, f32[384]{0:T(512)}, u32[]{:S(2)}) copy-start(f32[384]{0:T(512)} %get-tuple-element.209) | copy-start | bytes 4612
  2220.2 32.3 %copy-start.155 = (f32[384]{0:T(512)S(1)}, f32[384]{0:T(512)}, u32[]{:S(2)}) copy-start(f32[384]{0:T(512)} %get-tuple-element.208) | copy-start | bytes 4612
  2252.5 32.5 %copy-start.154 = (f32[384]{0:T(512)S(1)}, f32[384]{0:T(512)}, u32[]{:S(2)}) copy-start(f32[384]{0:T(512)} %get-tuple-element.207) | copy-start | bytes 4612
  2285.0 32.3 %copy-start.153 = (f32[384]{0:T(512)S(1)}, f32[384]{0:T(512)}, u32[]{:S(2)}) copy-start(f32[384]{0:T(512)} %get-tuple-element.206) | copy-start | bytes 4612
  2317.3 32.3 %copy-start.152 = (f32[384]{0:T(512)S(1)}, f32[384]{0:T(512)}, u32[]{:S(2)}) copy-start(f32[384]{0:T(512)} %get-tuple-element.205) | copy-start | bytes 4612
  2349.6 32.5 %copy-start.151 = (f32[384]{0:T(512)S(1)}, f32[384]{0:T(512)}, u32[]{:S(2)}) copy-start(f32[384]{0:T(512)} %get-tuple-element.204) | copy-start | bytes 4612
  2382.1 32.3 %copy-start.150 = (f32[384]{0:T(512)S(1)}, f32[384]{0:T(512)}, u32[]{:S(2)}) copy-start(f32[384]{0:T(512)} %get-tuple-element.203) | copy-start | bytes 4612
  2414.4 32.3 %copy-start.149 = (f32[384]{0:T(512)S(1)}, f32[384]{0:T(512)}, u32[]{:S(2)}) copy-start(f32[384]{0:T(512)} %get-tuple-element.202) | copy-start | bytes 4612
  2446.7 32.7 %copy-start.148 = (f32[384]{0:T(512)S(1)}, f32[384]{0:T(512)}, u32[]{:S(2)}) copy-start(f32[384]{0:T(512)} %get-tuple-element.201) | copy-start | bytes 4612
  2479.4 32.3 %copy-start.147 = (f32[384]{0:T(512)S(1)}, f32[384]{0:T(512)}, u32[]{:S(2)}) copy-start(f32[384]{0:T(512)} %get-tuple-element.200) | copy-start | bytes 4612
  2547.4 15.4 collective-permute-start.2
  2548.9 13.9 collective-permute-start.3
  (134 other events, 1581.5 us)
Sparse Core Ops, SparseCore 0:
  14.8 76.6 all-gather.2
  1668.4 166.1 all-reduce.5
where the time goes:
time: 2600 us; the launch traced here: 2580 us
  other arithmetic  1170 us (45%)
  local copies, waits for them, and re-layouts  1050 us (40%)
  matrix products  243 us (9%)
  blocking collectives  85.8 us (3%)
    scatter-add x27, other arithmetic, shards(): delta_extended.at[column_index]  873 us
    gather x27, local copies, waits for them, and re-layouts, shards(): jnp.take(extended, local_index[:, offset_index], axis=0).astype(jnp.float32)  463 us
    reduce_sum x1, other arithmetic, shards(): jnp.sum(live_rows * convolved * convolved, axis=0)  85.1 us
    unnamed x403, local copies, waits for them, and re-layouts  78.6 us
    reduce_sum x5, other arithmetic, shards(): conv_rows.append(jnp.sum(delta_conv * picked * present_column, axis=0))  59.2 us
    all_gather x1, other arithmetic, shards(): lax.all_gather(master.astype(jnp.bfloat16), ('rows', 'grp'), axis=0, tile...  57.2 us
  transfers between devices with their start and end apart: 6, of which 0 were waited for; matrix products, arithmetic and copies ran while one was open for 54% of the time, Pallas kernels for 0%

commit v1 on v0

v1 whole, which is shorter than its diff:
```python
import functools

import jax
import jax.numpy as jnp
from jax import lax
from jax.experimental import pallas as pl
from jax.experimental.pallas import tpu as pltpu
from jax.sharding import PartitionSpec as P

C = 384
HEADS = 12
HD = 32
F = 1536
HALO = 64
STEP = 5
EPS = 1e-5
AXES = ("rows", "grp")
F32 = jnp.float32
BF = jnp.bfloat16

BLK = 128
T = 256
ROW_CONV = (10 * C + F) // 128
ROW_JOINT = ROW_CONV + 27 * C // 128
ROW_OUT = ROW_JOINT + C * 3 * C // 128
ROW_HIDDEN = ROW_OUT + C * C // 128
ROW_FINAL = ROW_HIDDEN + C * F // 128
ROW_END = ROW_FINAL + C * F // 128
VMEM = pltpu.CompilerParams(vmem_limit_bytes=60 * 1024 * 1024)


def nn(a, b):
    return jnp.dot(a, b, preferred_element_type=F32)


def nt(a, b):
    return lax.dot_general(a, b, (((1,), (1,)), ((), ())), preferred_element_type=F32)


def whole(*shape):
    return pl.BlockSpec(shape, lambda i: (0,) * len(shape), pipeline_mode=pl.Buffered(1))


def rows_of(width, size):
    return pl.BlockSpec((size, width), lambda i: (i, 0))


def unpack_kernel(flat_ref, wj, wjt, wo, wot, wh, wht, wf, wft, wide):
    wide[...] = flat_ref[...].astype(F32)
    for first, out, out_t in (
        (ROW_JOINT, wj, wjt),
        (ROW_OUT, wo, wot),
        (ROW_HIDDEN, wh, wht),
        (ROW_FINAL, wf, wft),
    ):
        rows, cols = out.shape
        per = cols // 128
        for k in range(per):
            for r in range(0, rows, C):
                piece = wide[pl.ds(first + r * per + k, C, stride=per), :]
                out[r : r + C, k * 128 : (k + 1) * 128] = piece.astype(BF)
                out_t[k * 128 : (k + 1) * 128, r : r + C] = piece.T.astype(BF)


def unpack(flat):
    shapes = []
    for shape in ((C, 3 * C), (C, C), (C, F), (F, C)):
        shapes += [shape, shape[::-1]]
    return pl.pallas_call(
        unpack_kernel,
        out_shape=[jax.ShapeDtypeStruct(s, BF) for s in shapes],
        scratch_shapes=[pltpu.VMEM(flat.shape, F32)],
        compiler_params=VMEM,
    )(flat)


def conv_kernel(near_ref, x_ref, w_ref, mask_ref, conv_ref, sums_ref):
    b = pl.program_id(0)

    @pl.when(b == 0)
    def _():
        sums_ref[...] = jnp.zeros_like(sums_ref)

    window = x_ref[pl.ds(pl.multiple_of(b * BLK, BLK), 2 * BLK), :]
    near = near_ref[...]
    place = near + lax.broadcasted_iota(jnp.int32, near.shape, 0)
    place = jnp.where(near < 0, -1, place).astype(F32).astype(BF)
    lane = lax.broadcasted_iota(jnp.int32, (BLK, 2 * BLK), 1).astype(F32).astype(BF)
    one, zero = jnp.ones((), BF), jnp.zeros((), BF)
    total = jnp.zeros((BLK, C), F32)
    for j in range(27):
        pick = jnp.where(place[:, j : j + 1] == lane, one, zero)
        total += nn(pick, window) * w_ref[j : j + 1, :]
    conv_ref[...] = total
    live = jnp.broadcast_to(mask_ref[0].astype(F32), (BLK, BLK)).T
    live = jnp.concatenate([live] * 3, axis=1)
    kept = total * live
    sums_ref[0] += jnp.sum(kept.reshape(BLK // 8, 8, C), axis=0)
    sums_ref[1] += jnp.sum((kept * total).reshape(BLK // 8, 8, C), axis=0)
    sums_ref[2] += jnp.sum(live.reshape(BLK // 8, 8, C), axis=0)


def convolve(near, extended, weight, mask3):
    n = near.shape[0]
    return pl.pallas_call(
        conv_kernel,
        grid=(n // BLK,),
        in_specs=[
            rows_of(27, BLK),
            whole(*extended.shape),
            whole(27, C),
            pl.BlockSpec((1, 1, 128), lambda i: (i, 0, 0)),
        ],
        out_specs=[rows_of(C, BLK), whole(3, 8, C)],
        out_shape=[jax.ShapeDtypeStruct((n, C), F32), jax.ShapeDtypeStruct((3, 8, C), F32)],
        compiler_params=VMEM,
    )(near, extended, weight, mask3)


def conv_back_kernel(near_ref, delta_ref, x_ref, w_ref, first_ref, grad_ref, dw_ref):
    b = pl.program_id(0)

    @pl.when(b == 0)
    def _():
        dw_ref[...] = jnp.zeros_like(dw_ref)

    start = pl.multiple_of(b * BLK, BLK)
    window = delta_ref[pl.ds(start, 2 * BLK), :]
    near = near_ref[pl.ds(start, 2 * BLK), :]
    place = near + lax.broadcasted_iota(jnp.int32, near.shape, 0) - BLK
    place = jnp.where(near < 0, -1, place).astype(F32)
    place = jnp.concatenate([place, jnp.zeros((2 * BLK, 128 - 27), F32)], axis=1).T.astype(BF)
    target = lax.broadcasted_iota(jnp.int32, (BLK, 2 * BLK), 0).astype(F32).astype(BF)
    one, zero = jnp.ones((), BF), jnp.zeros((), BF)
    x = x_ref[...].astype(F32)
    total = first_ref[...]
    for j in range(27):
        pick = jnp.where(place[j : j + 1, :] == target, one, zero)
        come = nn(pick, window)
        total += come * w_ref[j : j + 1, :]
        dw_ref[j] += jnp.sum((come * x).reshape(BLK // 8, 8, C), axis=0)
    grad_ref[...] = total


def convolve_back(near_ext, delta_ext, nodes, weight, delta_first):
    n = nodes.shape[0]
    return pl.pallas_call(
        conv_back_kernel,
        grid=(n // BLK,),
        in_specs=[
            whole(*near_ext.shape),
            whole(*delta_ext.shape),
            rows_of(C, BLK),
            whole(27, C),
            rows_of(C, BLK),
        ],
        out_specs=[rows_of(C, BLK), whole(27, 8, C)],
        out_shape=[jax.ShapeDtypeStruct((n, C), F32), jax.ShapeDtypeStruct((27, 8, C), F32)],
        compiler_params=VMEM,
    )(near_ext, delta_ext, nodes, weight, delta_first)


def mid_kernel(conv_ref,nodes_ref,dy_ref,mask_ref,bn_ref,vb_ref,wj_ref,wjt_ref,wo_ref,wot_ref,wh_ref,wht_ref,wf_ref,wft_ref,
    out_ref,dfirst_ref,flat_ref,bns_ref,
    gj_ref,go_ref,gh_ref,gf_ref,vs_ref,hb_ref,first_s,second_s,qkv_s,kn_s,vn_s,a_s,o_s,ob_s,do_s,dqkv_s,x_s,acc_s,dx_s):
    step=pl.program_id(0)
    rep=T//128
    @pl.when(step==0)
    def _():
        for r in (gj_ref,go_ref,gh_ref,gf_ref,vs_ref,hb_ref,bns_ref): r[...]=jnp.zeros_like(r)
    def col(i,n=C):
        v=vb_ref[pl.ds(i*C,n),:]
        return jnp.concatenate([v]*rep,axis=1) if rep>1 else v
    def fold(x):
        r=x[:,:128]
        for k in range(1,rep): r=r+x[:,128*k:128*(k+1)]
        return r
    scale_a=bn_ref[0:1,:]; shift_b=bn_ref[1:2,:]; r_row=bn_ref[2:3,:]; ar_row=bn_ref[3:4,:]
    first=nodes_ref[...].astype(F32)+(conv_ref[...]*scale_a+shift_b)
    firstT=first.T
    first_s[...]=firstT
    dy=dy_ref[...]
    dyT32=dy.astype(F32).T
    do_s[...]=dyT32
    def ln(x):
        m=jnp.mean(x,axis=0,keepdims=True); c=x-m
        rs=lax.rsqrt(jnp.mean(c*c,axis=0,keepdims=True)+EPS)
        return c*rs, rs
    xh1,rs1=ln(firstT)
    x1=(xh1*col(2)+col(3)).astype(BF)
    x_s[0]=x1
    q=nn(wjt_ref[0:C,:],x1)+col(4)
    qkv_s[0:C,:]=q.astype(BF)
    k=nn(wjt_ref[C:2*C,:],x1)
    qkv_s[C:2*C,:]=k.astype(BF)
    kn_s[...]=k.T.astype(BF)
    v=nn(wjt_ref[2*C:,:],x1)+col(5)
    qkv_s[2*C:,:]=v.astype(BF)
    vn_s[...]=v.T.astype(BF)
    scale=HD**-0.5
    c2=scale*1.4426950408889634
    pi=lax.broadcasted_iota(jnp.int32,(BLK,BLK),0); qi=lax.broadcasted_iota(jnp.int32,(BLK,BLK),1)
    same=(pi&3)==(qi&3)
    for b in range(rep):
        lv=jnp.broadcast_to(mask_ref[b].astype(F32),(BLK,BLK)).T
        live=(lv>0.5)&same
        bias=jnp.where(same,-1e9/scale,-1e30)
        live2=jnp.concatenate([live,live],axis=1); bias2=jnp.concatenate([bias,bias],axis=1)
        cs=slice(b*BLK,(b+1)*BLK)
        z=jnp.zeros((HD,BLK),BF)
        for g in range(3):
            kg=kn_s[cs,g*128:(g+1)*128]
            for hp in range(2):
                h0=hp*2
                def ex(i):
                    qh=qkv_s[g*128+i*32:g*128+(i+1)*32,cs]
                    return jnp.concatenate([qh if t==i else z for t in range(4)],axis=0)
                s=nn(kg,jnp.concatenate([ex(h0),ex(h0+1)],axis=1))
                s=jnp.where(live2,s,bias2)
                m=jnp.max(s,axis=0,keepdims=True)
                e=jnp.exp2((s-m)*c2)
                l=jnp.sum(e,axis=0,keepdims=True)
                a=(e*(1.0/l)).astype(BF)
                for i in range(2):
                    h=g*4+h0+i
                    ah=a[:,i*128:(i+1)*128]
                    a_s[h,:,cs]=ah
                    o_s[h*32:(h+1)*32,cs]=nn(qkv_s[2*C+h*32:2*C+(h+1)*32,cs],ah)
    ob=o_s[...].astype(BF)
    ob_s[...]=ob
    secondT=first_s[...]+(nn(wot_ref[...],ob)+col(6))
    second_s[...]=secondT
    xh2,rs2=ln(secondT)
    x2=(xh2*col(7)+col(8)).astype(BF)
    x_s[1]=x2
    dyTb=do_s[...].astype(BF)
    FC=384
    c0=0.7978845608028654; c1=0.044715
    for f in range(F//FC):
        fs=slice(f*FC,(f+1)*FC)
        hb=vb_ref[9*C+f*FC:9*C+(f+1)*FC,:]
        hb=jnp.concatenate([hb]*rep,axis=1)
        h=nn(wht_ref[fs,:],x2)+hb
        h2=h*h
        t=jnp.tanh(h*(c0+(c0*c1)*h2))
        p=0.5+0.5*t
        act=(h*p).astype(BF)
        dg=p*(1.0+h*(1.0-p)*(2*c0+(6*c0*c1)*h2))
        da=nn(wf_ref[fs,:],dyTb)
        dp32=da*dg
        dpb=dp32.astype(BF)
        hb_ref[fs,:]+=fold(dpb.astype(F32))
        o=nn(wft_ref[:,fs],act)
        d=nn(wh_ref[:,fs],dpb)
        if f==0:
            acc_s[...]=o; dx_s[...]=d
        else:
            acc_s[...]+=o; dx_s[...]+=d
        gf_ref[fs,:]+=nn(act,dy)
        gh_ref[:,fs]+=nt(x2,dpb)
    outT=second_s[...]+(acc_s[...]+col(15-2))
    out_ref[...]=outT.T.astype(BF)
    def ln_back(x,dx,gain,vi):
        xh,rs=ln(x)
        vs_ref[vi]+=fold(dx*xh)
        vs_ref[vi+1]+=fold(dx)
        dh=dx*gain
        m1=jnp.mean(dh,axis=0,keepdims=True)
        m2=jnp.mean(dh*xh,axis=0,keepdims=True)
        return rs*(dh-m1-xh*m2)
    dsec=do_s[...]+ln_back(second_s[...],dx_s[...],col(7),0)
    second_s[...]=dsec
    dbr=dsec.astype(BF)
    vs_ref[2]+=fold(dbr.astype(F32))
    go_ref[...]+=nt(ob_s[...],dbr)
    dat=nn(wo_ref[...],dbr)
    do_s[...]=dat
    dob=dat.astype(BF)
    for b in range(rep):
        cs=slice(b*BLK,(b+1)*BLK)
        z=jnp.zeros((HD,BLK),BF)
        lrow=mask_ref[b].astype(F32)
        for g in range(3):
            vg=vn_s[cs,g*128:(g+1)*128]
            for hp in range(2):
                h0=hp*2
                def ex(i):
                    qh=dob[g*128+i*32:g*128+(i+1)*32,cs]
                    return jnp.concatenate([qh if t==i else z for t in range(4)],axis=0)
                dA=nn(vg,jnp.concatenate([ex(h0),ex(h0+1)],axis=1))
                for i in range(2):
                    h=g*4+h0+i
                    hs=slice(h*32,(h+1)*32)
                    doh=dob[hs,cs]
                    delta=jnp.sum(doh.astype(F32)*o_s[hs,cs],axis=0,keepdims=True)
                    ah=a_s[h,:,cs]
                    ds=(ah.astype(F32)*(dA[:,i*128:(i+1)*128]-delta)).astype(BF)
                    kh=(qkv_s[C+h*32:C+(h+1)*32,cs].astype(F32)*lrow).astype(BF)
                    dqkv_s[h*32:(h+1)*32,cs]=(nn(kh,ds)*scale).astype(BF)
                    dqkv_s[C+h*32:C+(h+1)*32,cs]=(nt(qkv_s[hs,cs],ds)*(lrow*scale)).astype(BF)
                    dqkv_s[2*C+h*32:2*C+(h+1)*32,cs]=nt(doh,ah).astype(BF)
    vs_ref[3]+=fold(dqkv_s[0:C,:].astype(F32))
    vs_ref[4]+=fold(dqkv_s[2*C:,:].astype(F32))
    gj_ref[...]+=nt(x_s[0],dqkv_s[...])
    dx1=nn(wj_ref[...],dqkv_s[...])
    dfT=second_s[...]+ln_back(first_s[...],dx1,col(2),5)
    df=dfT.T
    dfirst_ref[...]=df
    cen=conv_ref[...]*r_row-ar_row
    bns_ref[0]+=jnp.sum((df*cen).reshape(T//8,8,C),axis=0)
    bns_ref[1]+=jnp.sum(df.reshape(T//8,8,C),axis=0)
    bns_ref[2]+=jnp.sum(dy.astype(F32).reshape(T//8,8,C),axis=0)
    @pl.when(step==pl.num_programs(0)-1)
    def _():
        flat_ref[...]=jnp.zeros_like(flat_ref)
        for vi,row in ((0,21),(1,24),(2,18),(3,12),(4,15),(5,6),(6,9)):
            for i in range(3):
                flat_ref[pl.ds(row+i,1),:]=jnp.sum(vs_ref[vi,i*128:(i+1)*128,:].T,axis=0,keepdims=True)
        for i in range(12):
            flat_ref[pl.ds(27+i,1),:]=jnp.sum(hb_ref[i*128:(i+1)*128,:].T,axis=0,keepdims=True)
        for first,mat in ((ROW_JOINT,gj_ref),(ROW_OUT,go_ref),(ROW_HIDDEN,gh_ref),(ROW_FINAL,gf_ref)):
            rows,cols=mat.shape
            per=cols//128
            for k in range(per):
                for r in range(0,rows,C):
                    flat_ref[pl.ds(first+r*per+k,C,stride=per),:]=mat[r:r+C,k*128:(k+1)*128]


def middle(conv,nodes,dy,mask3,bn,vb,ws,flat_rows):
    n=conv.shape[0]
    row=rows_of(C,T)
    in_specs=[row,row,row,pl.BlockSpec((T//128,1,128),lambda i:(i,0,0)),whole(8,C),whole(*vb.shape)]+[whole(*w.shape) for w in ws]
    outs=[((n,C),BF,row),((n,C),F32,row),((flat_rows,128),F32,whole(flat_rows,128)),((3,8,C),F32,whole(3,8,C))]
    scr=[pltpu.VMEM(s,d) for s,d in (((C,3*C),F32),((C,C),F32),((C,F),F32),((F,C),F32),((7,C,128),F32),((F,128),F32),((C,T),F32),((C,T),F32),((3*C,T),BF),((T,C),BF),((T,C),BF),((HEADS,BLK,T),BF),((C,T),F32),((C,T),BF),((C,T),F32),((3*C,T),BF),((2,C,T),BF),((C,T),F32),((C,T),F32))]
    return pl.pallas_call(mid_kernel,grid=(n//T,),in_specs=in_specs,out_specs=[o[2] for o in outs],
      out_shape=[jax.ShapeDtypeStruct(o[0],o[1]) for o in outs],scratch_shapes=scr,
      compiler_params=VMEM)(conv,nodes,dy,mask3,bn,vb,*ws)


def extended_2(block, width):
    count = lax.axis_size(AXES)
    forward = [(i, i + 1) for i in range(count - 1)]
    backward = [(target, source) for source, target in forward]
    low = lax.ppermute(block[block.shape[0] - width :], AXES, forward)
    high = lax.ppermute(block[:width], AXES, backward)
    return jnp.concatenate([low, block, high], axis=0)


def shards(nodes_in, out_grad, neighbours, node_mask, master, first_moment, second_moment):
    n = nodes_in.shape[0]
    shard = master.shape[0] // 128
    flat = lax.all_gather(
        master.reshape(shard, 128).astype(BF), AXES, axis=0, tiled=True
    )
    weights = unpack(flat)
    vectors = flat[:ROW_CONV].astype(F32).reshape(-1)
    spread = jnp.broadcast_to(vectors[:, None], (vectors.shape[0], 128))
    batch_gain, batch_shift = vectors[:C], vectors[C : 2 * C]
    conv_weight = flat[ROW_CONV:ROW_JOINT].astype(F32).reshape(27, C)
    extended = extended_2(nodes_in, HALO)
    near_ext = extended_2(neighbours, HALO)
    mask3 = node_mask.reshape(n // 128, 1, 128)
    convolved, sums = convolve(neighbours, extended, conv_weight, mask3)
    sums = lax.psum(jnp.sum(sums, axis=1), AXES)
    live_total = sums[2]
    average = sums[0] / live_total
    variance = sums[1] / live_total - average * average
    inverse = lax.rsqrt(variance + EPS)
    norm_rows = jnp.stack(
        [inverse * batch_gain, batch_shift - average * inverse * batch_gain, inverse, average * inverse]
        + [jnp.zeros((C,), F32)] * 4
    )
    output, delta_first, flat_grads, norm_sums = middle(
        convolved, nodes_in, out_grad, mask3, norm_rows, spread, weights, shard * lax.axis_size(AXES)
    )
    norm_sums = lax.psum(jnp.sum(norm_sums, axis=1), AXES)
    gain_total, shift_total, bias_total = norm_sums[0], norm_sums[1], norm_sums[2]
    shard_delta = lax.psum_scatter(flat_grads, AXES, scatter_dimension=0, tiled=True)
    sum_spread = batch_gain * gain_total / inverse
    delta_variance = -0.5 * inverse * inverse * inverse * sum_spread
    delta_average = -batch_gain * shift_total * inverse - 2.0 * average * delta_variance
    live_rows = node_mask.astype(F32)[:, None]
    delta_conv = (
        delta_first * (batch_gain * inverse)
        + live_rows * (delta_average + 2.0 * convolved * delta_variance) / live_total
    ).astype(BF)
    node_grad, conv_grad = convolve_back(
        near_ext, extended_2(delta_conv, HALO), nodes_in, conv_weight, delta_first
    )
    conv_grad = lax.psum(jnp.sum(conv_grad, axis=1), AXES)
    early = jnp.concatenate(
        [
            jnp.concatenate([gain_total, shift_total]).reshape(-1, 128),
            jnp.zeros((ROW_CONV - 2 * C // 128 - C // 128, 128), F32),
            bias_total.reshape(-1, 128),
            conv_grad.reshape(-1, 128),
        ]
    )
    me = lax.axis_index(AXES)
    early = jnp.pad(early, ((0, -early.shape[0] % shard + shard), (0, 0)))
    begin = jnp.minimum(me * shard, early.shape[0] - shard)
    shard_delta = shard_delta + lax.dynamic_slice(early, (begin, 0), (shard, 128))
    shard_delta = shard_delta.reshape(-1)
    position = me * master.shape[0] + lax.iota(jnp.int32, master.shape[0])
    step_rate = jnp.where(position < 10 * C + F, 0.2, 0.03)
    new_first = 0.9 * first_moment + 0.1 * shard_delta
    new_second = 0.95 * second_moment + 0.05 * shard_delta * shard_delta
    first_hat = new_first / (1.0 - 0.9**STEP)
    second_hat = new_second / (1.0 - 0.95**STEP)
    new_master = master - step_rate * (first_hat / (jnp.sqrt(second_hat) + 1e-08) + 0.01 * master)
    return (
        output,
        node_grad,
        new_master,
        new_first,
        new_second,
        new_master.astype(BF),
        bias_total,
    )


def solution(mesh):
    rows, flat = P(AXES, None), P(AXES)
    return jax.shard_map(
        shards,
        mesh=mesh,
        in_specs=(rows, rows, rows, flat, flat, flat, flat),
        out_specs=(rows, rows, flat, flat, flat, flat, P()),
        check_vma=False,
    )
```

time: 2600 us -> 603 us (0.23)
  other arithmetic: 1170 us -> 23.1 us
  local copies, waits for them, and re-layouts: 1050 us -> 23.3 us
  Pallas kernels: 0 us -> 278 us
  matrix products: 243 us -> 0 us
  blocking collectives: 85.8 us -> 208 us
  waiting for transfers between devices: 0.05 us -> 39.8 us
    scatter-add x29 -> x0, other arithmetic: 873 us -> none  [the longest x27 873 us: shards(): delta_extended.at[column_index]]
    gather x27 -> x0, local copies, waits for them, and re-layouts: 463 us -> none  [shards(): jnp.take(extended, local_index[:, offset_index], axis=0).astype(jnp.float32)]
    pallas_call x0 -> x4, Pallas kernels: none -> 278 us  [the longest x1 188 us: middle(): pl.pallas_call(mid_kernel, grid=(n // T,), in_specs=in_specs, out_specs=[...]
    dot_general x18 -> x0, matrix products: 243 us -> none  [the longest x4 51.1 us: contract_last(): lax.dot_general(left, right, (((1,), (1,)), ((), ())), preferred_element_...]
    reduce_sum x16 -> x3, other arithmetic: 175 us -> 2.65 us  [the longest x1 1.06 us: shards(): conv_grad = lax.psum(jnp.sum(conv_grad, axis=1), AXES)]
    reshape x19 -> x2, local copies, waits for them, and re-layouts: 162 us -> 0.64 us  [the longest x1 0.63 us: shards(): conv_weight = flat[ROW_CONV:ROW_JOINT].astype(F32).reshape(27, C)]
    unnamed x0 -> x1, blocking collectives: none -> 88.2 us
    dot_general x4 -> x0, local copies, waits for them, and re-layouts: 80.2 us -> none  [the longest x1 20.5 us: shards(): jnp.einsum('wqhd,wkhd->whqk', delta_window_rows, window_values, preferred...]
  transfers between devices with their start and end apart: 6 -> 8, of which waited for: 0 -> 1; matrix products, arithmetic and copies ran while one was open for 54% -> 18% of each run, Pallas kernels for 0% -> 7%
where the time goes in v1:
time: 603 us; the launch traced here: 602 us
  Pallas kernels  278 us (46%)
  blocking collectives  208 us (34%)
  waiting for transfers between devices  39.8 us (7%)
  local copies, waits for them, and re-layouts  23.3 us (4%)
  other arithmetic  23.1 us (4%)
  starting transfers between devices  14.6 us (2%)
  between operations  14.2 us (2%)
    pallas_call x1, Pallas kernels, middle(): pl.pallas_call(mid_kernel, grid=(n // T,), in_specs=in_specs, out_specs=[...  188 us
    unnamed x1, blocking collectives  88.2 us
    pallas_call x1, Pallas kernels, convolve_back(): pl.pallas_call(conv_back_kernel, grid=(n // BLK,), in_specs=[whole(*near_...  44 us
    pallas_call x1, Pallas kernels, convolve(): pl.pallas_call(conv_kernel, grid=(n // BLK,), in_specs=[rows_of(27, BLK),...  40.9 us
    psum x1, blocking collectives, shards(): conv_grad = lax.psum(jnp.sum(conv_grad, axis=1), AXES)  40.5 us
    psum x1, blocking collectives, shards(): norm_sums = lax.psum(jnp.sum(norm_sums, axis=1), AXES)  40.5 us
    all_gather x1, waiting for transfers between devices, shards(): lax.all_gather(master.reshape(shard, 128).astype(BF), AXES, axis=0, tiled...  39.8 us
    psum x1, blocking collectives, shards(): sums = lax.psum(jnp.sum(sums, axis=1), AXES)  39.1 us
  transfers between devices with their start and end apart: 8, of which 1 were waited for; matrix products, arithmetic and copies ran while one was open for 18% of the time, Pallas kernels for 7%

profile of v1, /device:TPU:0, one launch (start us, length us, event | category | flops | bytes accessed | tf_op | source)
XLA Modules:
  0.0 601.5 jit_solution(6741223681105639648)
XLA Ops:
  7.2 0.0 copy-start
  7.2 0.0 all-gather.3.cloned.1.call-start
  7.2 1.7 convert_bitcast_fusion
  9.0 0.0 all-gather.3.cloned.1.call-update
  9.0 0.8 fusion.16
  9.8 2.4 collective-permute-start
  12.2 1.3 collective-permute-start.1
  13.5 0.8 fusion.17
  14.3 5.1 collective-permute-start.2
  19.4 1.3 collective-permute-start.3
  20.7 3.0 copy.22.near_ref
  23.7 0.7 convert_element_type.24
  24.5 0.0 collective-permute-done.2
  24.5 0.0 collective-permute-done.3
  24.5 2.1 concatenate.20
  26.5 3.0 copy.23.near_ref
  29.6 0.0 collective-permute-done
  29.6 0.0 collective-permute-done.1
  29.6 0.0 copy-done
  29.6 5.0 pad_maximum_fusion.x_ref
  34.6 39.8 %all-gather.3.cloned.1.call-done = bf16[32,436,128]{2,1,0:T(8,128)(2,1)} async-done(((bf16[1,436,128]{2,1,0:T(8,128)(2,1)}), bf16[32,436,128]{2,1,0:T(8,128)(2,1)}) %all-gather.3.cloned.1.call-update) | async-done | bytes 3571728 | tf_op jit(solution)/shard_map/all_gather | solution.py:352
  74.4 5.6 reshape.64.flat_ref
  80.0 0.7 slice_convert_fusion
  80.7 0.7 fusion.4
  81.4 5.3 shard_map.127
  86.7 0.6 reshape.62.w_ref
  87.4 40.9 %shard_map.126 = (f32[4096,384]{1,0:T(8,128)}, f32[3,8,384]{2,1,0:T(8,128)}) custom-call(s32[4096,27]{1,0:T(8,128)} %copy.22.near_ref, bf16[4224,384]{1,0:T(8,128)(2,1)} %pad_maximum_fusion.x_ref, f32[27,384]{1,0:T(8,128)} %reshape.62.w_ref, s32[32,1,128]{2,1,0:T(1,128)} %bitcast.44), custom_call_target="tpu_custom_call" | custom-call | tf_op jit(solution)/shard_map/pallas_call | solution.py:105
  128.3 0.8 reduce_sum.27
  129.1 39.1 %psum.21 = f32[3,384]{1,0:T(4,128)S(1)} all-reduce(f32[3,384]{1,0:T(4,128)S(1)} %reduce_sum.27), channel_id=1, replica_groups=mesh['rows'=16,'grp'=2] {'rows','grp'}, use_global_device_ids=true, to_apply=%region_1.0 | all-reduce | flops 1152 | bytes 9216 | tf_op jit(solution)/shard_map/psum | solution.py:364
  168.2 0.6 stack.5.bn_ref
  168.8 3.4 broadcast_in_dim.23.vb_ref
  172.2 187.9 %shard_map.128 = (bf16[4096,384]{1,0:T(8,128)(2,1)}, f32[4096,384]{1,0:T(8,128)}, f32[13952,128]{1,0:T(8,128)}, f32[3,8,384]{2,1,0:T(8,128)}) custom-call(f32[4096,384]{1,0:T(8,128)} %get-tuple-element.23.conv_ref, bf16[4096,384]{1,0:T(8,128)(2,1)} %x_ref.1, bf16[4096,384]{1,0:T(8,128)(2,1)} %dy_ref.1, s32[32,1,128]{2,1,0:T(1,128)} %bitcast.45, ...), custom_call_target="tpu_custom_call" | custom-call | tf_op jit(solution)/shard_map/pallas_call | solution.py:335
  360.1 0.8 reduce_sum.28
  360.9 40.5 %psum.22 = f32[3,384]{1,0:T(4,128)S(1)} all-reduce(f32[3,384]{1,0:T(4,128)S(1)} %reduce_sum.28), channel_id=1, replica_groups=mesh['rows'=16,'grp'=2] {'rows','grp'}, use_global_device_ids=true, to_apply=%region_3.0 | all-reduce | flops 1152 | bytes 9216 | tf_op jit(solution)/shard_map/psum | solution.py:376
  401.4 0.0 copy-start.4
  401.4 5.4 add_convert_fusion
  406.8 0.6 fusion.15
  407.4 1.3 collective-permute-start.4
  408.7 1.3 collective-permute-start.5
  410.0 88.2 %fusion = f32[448,128]{1,0:T(8,128)S(1)} fusion(f32[13952,128]{1,0:T(8,128)} %get-tuple-element.37), kind=kCustom, calls=%all-reduce-scatter | all-reduce-scatter fusion | flops 1835009 | bytes 7372800
  498.3 0.7 slice.84
  499.0 2.0 collective-permute-start.6
  500.9 0.0 collective-permute-done.4
  500.9 0.0 collective-permute-done.5
  500.9 4.9 pad_maximum_fusion.1.delta_ref
  505.9 0.0 copy-start.1
  505.9 0.0 copy-start.2
  505.9 0.0 copy-start.3
  505.9 44.0 %shard_map.129 = (f32[4096,384]{1,0:T(8,128)}, f32[27,8,384]{2,1,0:T(8,128)}) custom-call(s32[4224,27]{1,0:T(8,128)} %copy.23.near_ref, bf16[4224,384]{1,0:T(8,128)(2,1)} %pad_maximum_fusion.1.delta_ref, bf16[4096,384]{1,0:T(8,128)(2,1)} %x_ref.1, f32[27,384]{1,0:T(8,128)} %reshape.62.w_ref, f32[4096,384]{1,0:T(8,128)} %get-tuple-element.34.first_ref), custom_call_target="tpu_custom_call" | custom-call | tf_op jit(solution)/shard_map/pallas_call | solution.py:147
  549.9 1.1 reduce_sum.29
  551.0 40.5 %psum.23 = f32[81,128]{1,0:T(8,128)S(1)} all-reduce(f32[81,128]{1,0:T(8,128)S(1)} %reshape.59), channel_id=1, replica_groups=mesh['rows'=16,'grp'=2] {'rows','grp'}, use_global_device_ids=true, to_apply=%region_6.0 | all-reduce | flops 10368 | bytes 82944 | tf_op jit(solution)/shard_map/psum | solution.py:390
  591.5 0.0 copy-done.4
  591.5 0.5 concatenate.24
  592.0 0.0 collective-permute-done.6
  592.0 1.5 concatenate.25
  593.6 0.0 copy-done.1
  593.6 0.0 copy-done.2
  593.6 0.0 copy-done.3
  593.6 1.1 fusion.12
  (7 shorter events, 0.1 us)
Async XLA Ops:
  7.2 22.4 %copy-start = (bf16[4096,384]{1,0:T(8,128)(2,1)S(1)}, bf16[4096,384]{1,0:T(8,128)(2,1)}, u32[]{:S(2)}) copy-start(bf16[4096,384]{1,0:T(8,128)(2,1)} %x_ref.1) | copy-start | bytes 9437188
  7.2 67.2 %all-gather.3.cloned.1.call-start = ((), (), s32[]{:S(2)}) async-start(), calls=%async_computation | async-start | bytes 3717120 | tf_op jit(solution)/shard_map/all_gather | solution.py:352
  9.8 19.7 %collective-permute-start = (bf16[64,384]{1,0:T(8,128)(2,1)S(1)}, bf16[64,384]{1,0:T(8,128)(2,1)S(1)}, u32[]{:S(2)}, u32[]{:S(2)}) collective-permute-start(bf16[64,384]{1,0:T(8,128)(2,1)S(1)} %get-tuple-element.58), channel_id=1, source_target_pairs={{0,1},{1,2},{2,3},{3,4},{4,5},{5,6},{6,7},{7,8},{8,9},{9,10},{10,1... | collective-permute-start | bytes 147464 | tf_op jit(solution)/shard_map/ppermute | solution.py:344
  12.2 17.4 %collective-permute-start.1 = (bf16[64,384]{1,0:T(8,128)(2,1)S(1)}, bf16[64,384]{1,0:T(8,128)(2,1)S(1)}, u32[]{:S(2)}, u32[]{:S(2)}) collective-permute-start(bf16[64,384]{1,0:T(8,128)(2,1)S(1)} %get-tuple-element.59), channel_id=1, source_target_pairs={{1,0},{2,1},{3,2},{4,3},{5,4},{6,5},{7,6},{8,7},{9,8},{10,9},{11,1... | collective-permute-start | bytes 147464 | tf_op jit(solution)/shard_map/ppermute | solution.py:345
  14.3 10.2 %collective-permute-start.2 = (s32[64,27]{0,1:T(8,128)S(1)}, s32[64,27]{0,1:T(8,128)S(1)}, u32[]{:S(2)}, u32[]{:S(2)}) collective-permute-start(s32[64,27]{0,1:T(8,128)S(1)} %get-tuple-element.61), channel_id=1, source_target_pairs={{0,1},{1,2},{2,3},{3,4},{4,5},{5,6},{6,7},{7,8},{8,9},{9,10},{10,1... | collective-permute-start | bytes 20744 | tf_op jit(solution)/shard_map/ppermute | solution.py:344
  19.4 5.0 collective-permute-start.3
  401.4 190.1 %copy-start.4 = (f32[384]{0:T(512)}, f32[384]{0:T(512)S(1)}, u32[]{:S(2)}) copy-start(f32[384]{0:T(512)S(1)} %get-tuple-element.39) | copy-start | bytes 4612
  407.4 93.5 %collective-permute-start.4 = (bf16[64,384]{1,0:T(8,128)(2,1)}, bf16[64,384]{1,0:T(8,128)(2,1)S(1)}, u32[]{:S(2)}, u32[]{:S(2)}) collective-permute-start(bf16[64,384]{1,0:T(8,128)(2,1)} %get-tuple-element.56), channel_id=1, source_target_pairs={{0,1},{1,2},{2,3},{3,4},{4,5},{5,6},{6,7},{7,8},{8,9},{9,10},{10,1... | collective-permute-start | bytes 147464 | tf_op jit(solution)/shard_map/ppermute | solution.py:344
  408.7 92.2 %collective-permute-start.5 = (bf16[64,384]{1,0:T(8,128)(2,1)S(1)}, bf16[64,384]{1,0:T(8,128)(2,1)S(1)}, u32[]{:S(2)}, u32[]{:S(2)}) collective-permute-start(bf16[64,384]{1,0:T(8,128)(2,1)S(1)} %get-tuple-element.57), channel_id=1, source_target_pairs={{1,0},{2,1},{3,2},{4,3},{5,4},{6,5},{7,6},{8,7},{9,8},{10,9},{11,1... | collective-permute-start | bytes 147464 | tf_op jit(solution)/shard_map/ppermute | solution.py:345
  499.0 93.0 %collective-permute-start.6 = (f32[372,128]{1,0:T(8,128)}, f32[372,128]{1,0:T(8,128)}, u32[]{:S(2)}, u32[]{:S(2)}) collective-permute-start(f32[372,128]{1,0:T(8,128)} %slice.84), channel_id=1, source_target_pairs={{0,1},{1,2},{2,3},{3,4},{4,5},{5,6},{6,7},{7,8},{8,9},{9,10},{10,1... | collective-permute-start | bytes 571400
  505.9 87.7 %copy-start.1 = (f32[55808]{0:T(1024)S(1)}, f32[55808]{0:T(1024)}, u32[]{:S(2)}) copy-start(f32[55808]{0:T(1024)} %param.11) | copy-start | bytes 669700
  505.9 87.7 %copy-start.2 = (f32[55808]{0:T(1024)S(1)}, f32[55808]{0:T(1024)}, u32[]{:S(2)}) copy-start(f32[55808]{0:T(1024)} %param.12) | copy-start | bytes 669700
  505.9 87.7 %copy-start.3 = (f32[55808]{0:T(1024)S(1)}, f32[55808]{0:T(1024)}, u32[]{:S(2)}) copy-start(f32[55808]{0:T(1024)} %param.13) | copy-start | bytes 669700
Sparse Core Ops, SparseCore 0:
  11.5 62.8 all-gather.2

commit v2 on v1

v2 whole, which is shorter than its diff:
```python
import functools

import jax
import jax.numpy as jnp
from jax import lax
from jax.experimental import pallas as pl
from jax.experimental.pallas import tpu as pltpu
from jax.sharding import PartitionSpec as P

C = 384
HEADS = 12
HD = 32
F = 1536
HALO = 64
STEP = 5
EPS = 1e-5
AXES = ("rows", "grp")
F32 = jnp.float32
BF = jnp.bfloat16

BLK = 128
T = 256
ROW_CONV = (10 * C + F) // 128
ROW_JOINT = ROW_CONV + 27 * C // 128
ROW_OUT = ROW_JOINT + C * 3 * C // 128
ROW_HIDDEN = ROW_OUT + C * C // 128
ROW_FINAL = ROW_HIDDEN + C * F // 128
ROW_END = ROW_FINAL + C * F // 128
VMEM = pltpu.CompilerParams(vmem_limit_bytes=60 * 1024 * 1024)


def nn(a, b):
    return jnp.dot(a, b, preferred_element_type=F32)


def nt(a, b):
    return lax.dot_general(a, b, (((1,), (1,)), ((), ())), preferred_element_type=F32)


def whole(*shape):
    return pl.BlockSpec(shape, lambda i: (0,) * len(shape), pipeline_mode=pl.Buffered(1))


def rows_of(width, size):
    return pl.BlockSpec((size, width), lambda i: (i, 0))


MESH = pl.DeviceIdType.MESH


def round_up(value, step):
    return -(-value // step) * step


def my_place():
    return lax.axis_index("rows") * lax.axis_size("grp") + lax.axis_index("grp")


def device(place, cores):
    return (place // cores, place % cores)


def stages_of(count):
    out, stride = [], 1
    while stride < count:
        size = min(8, count // stride)
        out.append((stride, size))
        stride *= size
    return out


def others(me, stride, size):
    mine = (me // stride) % size
    return mine, [(k, me + ((mine + k) % size - mine) * stride) for k in range(1, size)]


def greet(partners, cores):
    barrier = pltpu.get_barrier_semaphore()
    for place in partners:
        pl.semaphore_signal(barrier, inc=1, device_id=device(place, cores), device_id_type=MESH)
    pl.semaphore_wait(barrier, len(partners))


def send(source, target, send_sem, recv_sem, place, cores):
    return pltpu.make_async_remote_copy(
        src_ref=source,
        dst_ref=target,
        send_sem=send_sem,
        recv_sem=recv_sem,
        device_id=device(place, cores),
        device_id_type=MESH,
    )


def all_sum(value, me, count, cores, slots, send_sems, recv_sems):
    for s, (stride, size) in enumerate(stages_of(count)):
        mine, partners = others(me, stride, size)
        slots[s, mine] = value
        copies = [
            send(slots.at[s, mine], slots.at[s, mine], send_sems.at[s, k], recv_sems.at[s, k], place, cores)
            for k, place in partners
        ]
        for copy in copies:
            copy.start()
        for copy in copies:
            copy.wait()
        value = slots[s, 0]
        for i in range(1, size):
            value = value + slots[s, i]
    return value


def sum_scratch(count, rows, width):
    n = len(stages_of(count))
    return [
        pltpu.VMEM((n, 8, rows, width), F32),
        pltpu.SemaphoreType.DMA((n, 8)),
        pltpu.SemaphoreType.DMA((n, 8)),
    ]


def conv_kernel(count, cores, owners, near_ref, nodes_ref, mask_ref, master_ref,
                conv_ref, gathered_ref, first_ref, stats_ref,
                ext, early, weight, sums, own_s, local_sem, halo_send, halo_recv, e_send, e_recv, g_send, g_recv,
                slots, s_send, s_recv):
    step = pl.program_id(0)
    steps = pl.num_programs(0)
    block = (step + 1) % steps
    n = nodes_ref.shape[0]
    shard = master_ref.shape[0]
    padded = gathered_ref.shape[-2]
    half = padded // 2
    e_rows = early.shape[1]
    me = my_place()
    low, high = me % 8, me // 8
    y, x, g = low // 4, (low // 2) % 2, low % 2
    highs = stages_of(count // 8)
    left, right = (me + count - 1) % count, (me + 1) % count

    local = pltpu.make_async_copy(nodes_ref, ext.at[pl.ds(HALO, n)], local_sem.at[0])
    keep = pltpu.make_async_copy(own_s, gathered_ref.at[high, y, x, g], local_sem.at[1])
    to_left = send(nodes_ref.at[pl.ds(0, HALO)], ext.at[pl.ds(HALO + n, HALO)], halo_send.at[0], halo_recv.at[0], left, cores)
    to_right = send(nodes_ref.at[pl.ds(n - HALO, HALO)], ext.at[pl.ds(0, HALO)], halo_send.at[1], halo_recv.at[1], right, cores)

    def high_copies(s):
        stride, size = highs[s]
        mine, partners = others(high, stride, size)
        own = gathered_ref.at[pl.ds(high // stride * stride, stride), y, x, g]
        return [
            send(own, own, g_send.at[s, k], g_recv.at[s, k], place * 8 + low, cores)
            for k, place in partners
        ]

    nh = len(highs)
    y_place, x_place, g_place = me + 4 - 8 * y, me + 2 - 4 * x, me + 1 - 2 * g

    def quad_copies(t):
        top, bottom = pl.ds(0, half), pl.ds(half, half)
        if t == 0:
            a = gathered_ref.at[:, y, x, g, top]
            b = gathered_ref.at[:, y, x, g, bottom]
            to_a, to_b = y_place, x_place
        else:
            a = gathered_ref.at[:, :, x, g, top]
            b = gathered_ref.at[:, y, :, g, bottom]
            to_a, to_b = x_place, y_place
        s = nh + t
        return [send(a, a, g_send.at[s, 0], g_recv.at[s, 0], to_a, cores), send(b, b, g_send.at[s, 1], g_recv.at[s, 1], to_b, cores)]

    def core_copies():
        own = gathered_ref.at[:, :, :, g]
        return [send(own, own, g_send.at[nh + 2, 0], g_recv.at[nh + 2, 0], g_place, cores)]

    plan = [functools.partial(high_copies, s) for s in range(nh)]
    plan += [functools.partial(quad_copies, 0), functools.partial(quad_copies, 1), core_copies]
    cuts = [6] * nh + [11, 19, 27]
    for s in range(nh):
        cuts[s] = 3 + 5 * (s + 1) // nh

    @pl.when(step == 0)
    def _():
        local.start()
        sums[...] = jnp.zeros_like(sums)
        own = jnp.concatenate([master_ref[...], jnp.zeros((padded - shard, 128), F32)], axis=0).astype(BF)
        own_s[...] = own
        keep.start()
        wide = [h for h in range(1, count // 8)]
        partners = [left, right]
        partners += [(high + h) % (count // 8) * 8 + low for h in wide]
        partners += [place for _, place in others(me, 1, 8)[1]]
        greet(partners, cores)
        for o in range(owners):
            @pl.when(low == o)
            def _():
                @pl.when(high == 0)
                def _():
                    early[o] = own[:e_rows]
                    out = [
                        send(early.at[o], early.at[o], e_send.at[o, 8 + h], e_recv.at[o, 0], h * 8 + o, cores)
                        for h in wide
                    ]
                    for copy in out:
                        copy.start()
                    for copy in out:
                        copy.wait_send()
                @pl.when(high > 0)
                def _():
                    send(early.at[o], early.at[o], e_send.at[o, 8], e_recv.at[o, 0], left, cores).wait_recv()
                out = [
                    send(early.at[o], early.at[o], e_send.at[o, k], e_recv.at[o, 1], me + k - o, cores)
                    for k in range(8) if k != o
                ]
                for copy in out:
                    copy.start()
                for copy in out:
                    copy.wait_send()
        to_left.start()
        to_right.start()
        keep.wait()
        for copy in plan[0]():
            copy.start()
        for o in range(owners):
            @pl.when(low != o)
            def _():
                send(early.at[o], early.at[o], e_send.at[o, 8], e_recv.at[o, 1], left, cores).wait_recv()
        for o in range(owners):
            rows = min(shard, e_rows)
            first_ref[pl.ds(o * shard, rows), :] = early[o].astype(F32)[:rows]
        for k in range(3):
            weight[:, k * 128 : (k + 1) * 128] = first_ref[pl.ds(ROW_CONV + k, 27, stride=3), :]
        local.wait()

    for s in range(len(plan)):
        @pl.when(step == cuts[s])
        def _(s=s):
            for copy in plan[s]():
                copy.wait()
            if s + 1 < len(plan):
                for copy in plan[s + 1]():
                    copy.start()

    @pl.when(step == steps - 2)
    def _():
        to_left.wait()
        to_right.wait()

    window = ext[pl.ds(pl.multiple_of(block * BLK, BLK), 2 * BLK), :]
    near = near_ref[...]
    place = near + lax.broadcasted_iota(jnp.int32, near.shape, 0)
    place = jnp.where(near < 0, -1, place).astype(F32).astype(BF)
    lane = lax.broadcasted_iota(jnp.int32, (BLK, 2 * BLK), 1).astype(F32).astype(BF)
    one, zero = jnp.ones((), BF), jnp.zeros((), BF)
    total = jnp.zeros((BLK, C), F32)
    for j in range(27):
        pick = jnp.where(place[:, j : j + 1] == lane, one, zero)
        total += nn(pick, window) * weight[j : j + 1, :]
    conv_ref[...] = total
    live = jnp.broadcast_to(mask_ref[0].astype(F32), (BLK, BLK)).T
    live = jnp.concatenate([live] * 3, axis=1)
    kept = total * live
    sums[0] += jnp.sum(kept.reshape(BLK // 8, 8, C), axis=0)
    sums[1] += jnp.sum((kept * total).reshape(BLK // 8, 8, C), axis=0)
    sums[2] += jnp.sum(live.reshape(BLK // 8, 8, C), axis=0)

    @pl.when(step == steps - 1)
    def _():
        rows = [jnp.sum(sums[i], axis=0, keepdims=True) for i in range(3)]
        rows = jnp.concatenate(rows + [jnp.zeros((5, C), F32)], axis=0)
        stats_ref[...] = all_sum(rows, me, count, cores, slots, s_send, s_recv)


def convolve(near, nodes, mask3, master, count, cores):
    n = nodes.shape[0]
    steps = n // BLK
    shard = master.shape[0]
    padded = round_up(shard, 32)
    owners = -(-ROW_JOINT // shard)
    e_rows = min(padded, round_up(ROW_JOINT, 16))
    turned = lambda i: ((i + 1) % steps, 0)
    stages = len(stages_of(count // 8)) + 3
    first_rows = round_up((owners - 1) * shard + e_rows, 8)
    return pl.pallas_call(
        functools.partial(conv_kernel, count, cores, owners),
        grid=(steps,),
        in_specs=[
            pl.BlockSpec((BLK, 27), turned),
            pl.BlockSpec(memory_space=pl.ANY),
            pl.BlockSpec((1, 1, 128), lambda i: ((i + 1) % steps, 0, 0)),
            whole(shard, 128),
        ],
        out_specs=[
            pl.BlockSpec((BLK, C), turned),
            pl.BlockSpec(memory_space=pl.ANY),
            whole(first_rows, 128),
            whole(8, C),
        ],
        out_shape=[
            jax.ShapeDtypeStruct((n, C), F32),
            jax.ShapeDtypeStruct((count // 8, 2, 2, 2, padded, 128), BF),
            jax.ShapeDtypeStruct((first_rows, 128), F32),
            jax.ShapeDtypeStruct((8, C), F32),
        ],
        scratch_shapes=[
            pltpu.VMEM((n + 2 * HALO, C), BF),
            pltpu.VMEM((owners, e_rows, 128), BF),
            pltpu.VMEM((27, C), F32),
            pltpu.VMEM((3, 8, C), F32),
            pltpu.VMEM((padded, 128), BF),
            pltpu.SemaphoreType.DMA((2,)),
            pltpu.SemaphoreType.DMA((2,)),
            pltpu.SemaphoreType.DMA((2,)),
            pltpu.SemaphoreType.DMA((owners, 8 + count // 8)),
            pltpu.SemaphoreType.DMA((owners, 2)),
            pltpu.SemaphoreType.DMA((stages, 8)),
            pltpu.SemaphoreType.DMA((stages, 8)),
        ]
        + sum_scratch(count, 8, C),
        compiler_params=pltpu.CompilerParams(
            vmem_limit_bytes=60 * 1024 * 1024, collective_id=0, has_side_effects=True
        ),
    )(near, nodes, mask3, master)


def conv_back_kernel(count, cores, owners, near_hbm, first_hbm, conv_hbm, x_ref, mask_ref, sums_ref, stats_ref, rows_ref,
                     grads_ref, master_ref, m_ref, v_ref,
                     grad_ref, master_out, m_out, v_out, low_out, bias_out,
                     near, ext, delta, conv, weight, dw, kept, r1, r2, r3, r4, local_sem, halo_send, halo_recv, g_send, g_recv,
                     slots, s_send, s_recv, wslots, w_send, w_recv, total_s, early_s):
    step = pl.program_id(0)
    steps = pl.num_programs(0)
    block = (step + 1) % steps
    n = first_hbm.shape[0]
    shard = master_ref.shape[0]
    padded = grads_ref.shape[-2]
    half = padded // 2
    me = my_place()
    low, high = me % 8, me // 8
    y, x, g = low // 4, (low // 2) % 2, low % 2
    highs = stages_of(count // 8)[::-1]
    nh = len(highs)
    left, right = (me + count - 1) % count, (me + 1) % count
    y_place, x_place, g_place = me + 4 - 8 * y, me + 2 - 4 * x, me + 1 - 2 * g
    top, bottom = pl.ds(0, half), pl.ds(half, half)

    locals_ = [
        pltpu.make_async_copy(first_hbm, delta, local_sem.at[0]),
        pltpu.make_async_copy(conv_hbm, conv, local_sem.at[1]),
        pltpu.make_async_copy(near_hbm, near.at[pl.ds(HALO, n)], local_sem.at[2]),
        pltpu.make_async_copy(grads_ref.at[:, :, :, g], kept, local_sem.at[3]),
    ]
    near_halo = [
        send(near_hbm.at[pl.ds(0, HALO)], near.at[pl.ds(HALO + n, HALO)], halo_send.at[0], halo_recv.at[0], left, cores),
        send(near_hbm.at[pl.ds(n - HALO, HALO)], near.at[pl.ds(0, HALO)], halo_send.at[1], halo_recv.at[1], right, cores),
    ]
    delta_halo = [
        send(ext.at[pl.ds(HALO, HALO)], ext.at[pl.ds(HALO + n, HALO)], halo_send.at[2], halo_recv.at[2], left, cores),
        send(ext.at[pl.ds(n, HALO)], ext.at[pl.ds(0, HALO)], halo_send.at[3], halo_recv.at[3], right, cores),
    ]

    def core_copies():
        return [send(grads_ref.at[:, :, :, 1 - g], r1, g_send.at[0, 0], g_recv.at[0, 0], g_place, cores)]

    def core_add():
        def body(i, _):
            kept[i // 4, (i // 2) % 2, i % 2] = (
                kept[i // 4, (i // 2) % 2, i % 2].astype(F32) + r1[i // 4, (i // 2) % 2, i % 2].astype(F32)
            ).astype(BF)
            return 0
        lax.fori_loop(0, count // 2, body, 0)

    def quad_copies_0():
        return [
            send(kept.at[:, :, 1 - x, top], r2.at[0], g_send.at[1, 0], g_recv.at[1, 0], x_place, cores),
            send(kept.at[:, 1 - y, :, bottom], r2.at[1], g_send.at[1, 1], g_recv.at[1, 1], y_place, cores),
        ]

    def quad_add_0():
        def body(i, _):
            h, w = i // 2, i % 2
            kept[h, w, x, top] = (
                kept[h, w, x, top].astype(F32) + r2[0, h, w].astype(F32)
            ).astype(BF)
            kept[h, y, w, bottom] = (
                kept[h, y, w, bottom].astype(F32) + r2[1, h, w].astype(F32)
            ).astype(BF)
            return 0
        lax.fori_loop(0, count // 4, body, 0)

    def quad_copies_1():
        return [
            send(kept.at[:, 1 - y, x, top], r3.at[0], g_send.at[2, 0], g_recv.at[2, 0], y_place, cores),
            send(kept.at[:, y, 1 - x, bottom], r3.at[1], g_send.at[2, 1], g_recv.at[2, 1], x_place, cores),
        ]

    def quad_add_1():
        def body(h, _):
            kept[h, y, x, top] = (
                kept[h, y, x, top].astype(F32) + r3[0, h].astype(F32)
            ).astype(BF)
            kept[h, y, x, bottom] = (
                kept[h, y, x, bottom].astype(F32) + r3[1, h].astype(F32)
            ).astype(BF)
            return 0
        lax.fori_loop(0, count // 8, body, 0)

    bases = []
    base = 0
    for stride, size in highs:
        bases.append(base)
        base += (size - 1) * stride

    def high_copies(s):
        stride, size = highs[s]
        mine, partners = others(high, stride, size)
        out = []
        for k, place in partners:
            source = kept.at[pl.ds(place // stride * stride, stride), y, x]
            target = r4.at[pl.ds(bases[s] + (k - 1) * stride, stride)]
            out.append(send(source, target, g_send.at[3 + s, k], g_recv.at[3 + s, k], place * 8 + low, cores))
        return out

    def high_add(s):
        stride, size = highs[s]
        start = high // stride * stride
        def body(i, _):
            value = kept[start + i, y, x].astype(F32)
            for k in range(size - 1):
                value = value + r4[bases[s] + k * stride + i].astype(F32)
            if s == nh - 1:
                total_s[...] = value
            else:
                kept[start + i, y, x] = value.astype(BF)
            return 0
        lax.fori_loop(0, stride, body, 0)

    plan = [(core_copies, core_add), (quad_copies_0, quad_add_0), (quad_copies_1, quad_add_1)]
    plan += [(functools.partial(high_copies, s), functools.partial(high_add, s)) for s in range(nh)]
    cuts = [4, 13, 18] + [18 + 10 * (s + 1) // nh for s in range(nh)]

    @pl.when(step == 0)
    def _():
        for copy in locals_:
            copy.start()
        dw[...] = jnp.zeros_like(dw)
        partners = [left, right]
        partners += [(high + h) % (count // 8) * 8 + low for h in range(1, count // 8)]
        partners += [place for _, place in others(me, 1, 8)[1]]
        greet(partners, cores)
        mine = jnp.concatenate([jnp.sum(sums_ref[i], axis=0, keepdims=True) for i in range(3)] + [jnp.zeros((5, C), F32)], axis=0)
        total = all_sum(mine, me, count, cores, slots, s_send, s_recv)
        for copy in plan[0][0]():
            copy.start()
        for copy in near_halo:
            copy.start()
        gain_total, shift_total = total[0:1], total[1:2]
        bias_out[...] = total[2:3]
        early_s[...] = jnp.zeros_like(early_s)
        for i in range(3):
            early_s[i : i + 1, :] = gain_total[:, i * 128 : (i + 1) * 128]
            early_s[3 + i : 4 + i, :] = shift_total[:, i * 128 : (i + 1) * 128]
            early_s[ROW_CONV - 3 + i : ROW_CONV - 2 + i, :] = total[2:3, i * 128 : (i + 1) * 128]
        for k in range(3):
            weight[:, k * 128 : (k + 1) * 128] = rows_ref[pl.ds(ROW_CONV + k, 27, stride=3), :]
        gain = jnp.concatenate([rows_ref[i : i + 1, :] for i in range(3)], axis=1)
        live_total = stats_ref[2:3]
        average = stats_ref[0:1] / live_total
        variance = stats_ref[1:2] / live_total - average * average
        inverse = lax.rsqrt(variance + EPS)
        delta_variance = -0.5 * inverse * inverse * inverse * (gain * gain_total / inverse)
        delta_average = -gain * shift_total * inverse - 2.0 * average * delta_variance
        a = gain * inverse
        b = delta_average / live_total
        c = 2.0 * delta_variance / live_total
        for copy in locals_:
            copy.wait()

        def body(i, _):
            at = pl.ds(pl.multiple_of(i * BLK, BLK), BLK)
            live = jnp.broadcast_to(mask_ref[i].astype(F32), (BLK, BLK)).T
            live = jnp.concatenate([live] * 3, axis=1)
            value = delta[at, :] * a + live * (b + c * conv[at, :])
            ext[pl.ds(pl.multiple_of(i * BLK + HALO, HALO), BLK), :] = value.astype(BF)
            return 0

        lax.fori_loop(0, steps, body, 0)
        for copy in delta_halo:
            copy.start()

    for s in range(len(plan)):
        @pl.when(step == cuts[s])
        def _(s=s):
            for copy in plan[s][0]():
                copy.wait()
            plan[s][1]()
            if s + 1 < len(plan):
                for copy in plan[s + 1][0]():
                    copy.start()

    @pl.when(step == steps - 2)
    def _():
        for copy in near_halo + delta_halo:
            copy.wait()

    start = pl.multiple_of(block * BLK, BLK)
    window = ext[pl.ds(start, 2 * BLK), :]
    near_w = near[pl.ds(start, 2 * BLK), :]
    place = near_w + lax.broadcasted_iota(jnp.int32, near_w.shape, 0) - BLK
    place = jnp.where(near_w < 0, -1, place).astype(F32)
    place = jnp.concatenate([place, jnp.zeros((2 * BLK, 128 - 27), F32)], axis=1).T.astype(BF)
    target = lax.broadcasted_iota(jnp.int32, (BLK, 2 * BLK), 0).astype(F32).astype(BF)
    one, zero = jnp.ones((), BF), jnp.zeros((), BF)
    nodes = x_ref[...].astype(F32)
    total = delta[pl.ds(start, BLK), :]
    for j in range(27):
        pick = jnp.where(place[j : j + 1, :] == target, one, zero)
        come = nn(pick, window)
        total += come * weight[j : j + 1, :]
        dw[j] += jnp.sum((come * nodes).reshape(BLK // 8, 8, C), axis=0)
    grad_ref[...] = total

    @pl.when(step == steps - 1)
    def _():
        mine = jnp.sum(dw[...], axis=1)
        mine = jnp.concatenate([mine, jnp.zeros((5, C), F32)], axis=0)
        dws = all_sum(mine, me, count, cores, wslots, w_send, w_recv)
        for k in range(3):
            early_s[pl.ds(ROW_CONV + k, 27, stride=3), :] = dws[:27, k * 128 : (k + 1) * 128]
        for o in range(owners):
            @pl.when(me == o)
            def _():
                rows = min(shard, early_s.shape[0] - o * shard)
                total_s[0:rows, :] += early_s[o * shard : o * shard + rows, :]
        grad = total_s[0:shard, :]
        row = lax.broadcasted_iota(jnp.int32, (shard, 128), 0) + me * shard
        rate = jnp.where(row < ROW_CONV, 0.2, 0.03)
        old = master_ref[...]
        new_m = 0.9 * m_ref[...] + 0.1 * grad
        new_v = 0.95 * v_ref[...] + 0.05 * grad * grad
        first_hat = new_m / (1.0 - 0.9**STEP)
        second_hat = new_v / (1.0 - 0.95**STEP)
        new = old - rate * (first_hat / (jnp.sqrt(second_hat) + 1e-08) + 0.01 * old)
        master_out[...] = new
        m_out[...] = new_m
        v_out[...] = new_v
        low_out[...] = new.astype(BF)


def convolve_back(near, delta, conv, nodes, mask3, sums, stats, rows, grads, master, m, v, count, cores):
    n = nodes.shape[0]
    steps = n // BLK
    shard = master.shape[0]
    padded = grads.shape[-2]
    highs = count // 8
    owners = -(-ROW_JOINT // shard)
    turned = lambda i: ((i + 1) % steps, 0)
    anywhere = pl.BlockSpec(memory_space=pl.ANY)
    flat = whole(shard, 128)
    r4_rows = sum((size - 1) * stride for stride, size in stages_of(highs))
    return pl.pallas_call(
        functools.partial(conv_back_kernel, count, cores, owners),
        grid=(steps,),
        in_specs=[
            anywhere,
            anywhere,
            anywhere,
            pl.BlockSpec((BLK, C), turned),
            whole(*mask3.shape),
            whole(*sums.shape),
            whole(*stats.shape),
            whole(*rows.shape),
            anywhere,
            flat,
            flat,
            flat,
        ],
        out_specs=[pl.BlockSpec((BLK, C), turned), flat, flat, flat, flat, whole(1, C)],
        out_shape=[jax.ShapeDtypeStruct((n, C), F32)]
        + [jax.ShapeDtypeStruct((shard, 128), d) for d in (F32, F32, F32, BF)]
        + [jax.ShapeDtypeStruct((1, C), F32)],
        scratch_shapes=[
            pltpu.VMEM((n + 2 * HALO, 27), jnp.int32),
            pltpu.VMEM((n + 2 * HALO, C), BF),
            pltpu.VMEM((n, C), F32),
            pltpu.VMEM((n, C), F32),
            pltpu.VMEM((27, C), F32),
            pltpu.VMEM((27, 8, C), F32),
            pltpu.VMEM((highs, 2, 2, padded, 128), BF),
            pltpu.VMEM((highs, 2, 2, padded, 128), BF),
            pltpu.VMEM((2, highs, 2, padded // 2, 128), BF),
            pltpu.VMEM((2, highs, padded // 2, 128), BF),
            pltpu.VMEM((r4_rows, padded, 128), BF),
            pltpu.SemaphoreType.DMA((4,)),
            pltpu.SemaphoreType.DMA((4,)),
            pltpu.SemaphoreType.DMA((4,)),
            pltpu.SemaphoreType.DMA((3 + len(stages_of(highs)), 8)),
            pltpu.SemaphoreType.DMA((3 + len(stages_of(highs)), 8)),
        ]
        + sum_scratch(count, 8, C)
        + sum_scratch(count, 32, C)
        + [pltpu.VMEM((padded, 128), F32), pltpu.VMEM((round_up(ROW_JOINT, 8), 128), F32)],
        compiler_params=pltpu.CompilerParams(
            vmem_limit_bytes=60 * 1024 * 1024, collective_id=1, has_side_effects=True
        ),
    )(near, delta, conv, nodes, mask3, sums, stats, rows, grads, master, m, v)


def prepare(stats, rows, gathered, shard, flat, norm, spread, mats):
    for i in range(gathered.shape[0] * 8):
        flat[i * shard : (i + 1) * shard, :] = gathered[i // 8, (i // 4) % 2, (i // 2) % 2, i % 2].astype(F32)[:shard]
    for first, out, out_t in mats:
        height, width = out.shape
        per = width // 128
        for k in range(per):
            for r in range(0, height, C):
                piece = flat[pl.ds(first + r * per + k, C, stride=per), :]
                out[r : r + C, k * 128 : (k + 1) * 128] = piece.astype(BF)
                out_t[k * 128 : (k + 1) * 128, r : r + C] = piece.T.astype(BF)
    for i in range(ROW_CONV):
        spread[i * 128 : (i + 1) * 128, :] = jnp.broadcast_to(rows[i : i + 1, :], (128, 128)).T
    gain = jnp.concatenate([rows[i : i + 1, :] for i in range(3)], axis=1)
    shift = jnp.concatenate([rows[3 + i : 4 + i, :] for i in range(3)], axis=1)
    live_total = stats[2:3, :]
    average = stats[0:1, :] / live_total
    variance = stats[1:2, :] / live_total - average * average
    inverse = lax.rsqrt(variance + EPS)
    norm[0:1, :] = inverse * gain
    norm[1:2, :] = shift - average * inverse * gain
    norm[2:3, :] = inverse
    norm[3:4, :] = average * inverse


def mid_kernel(shard,conv_ref,nodes_ref,dy_ref,mask_ref,stats_ref,rows_ref,gathered_ref,
    out_ref,dfirst_ref,grads_ref,bns_ref,
    flat_ref,bn_ref,vb_ref,wj_ref,wjt_ref,wo_ref,wot_ref,wh_ref,wht_ref,wf_ref,wft_ref,
    gj_ref,go_ref,gh_ref,gf_ref,vs_ref,hb_ref,first_s,second_s,qkv_s,kn_s,vn_s,a_s,o_s,ob_s,do_s,dqkv_s,x_s,acc_s,dx_s):
    step=pl.program_id(0)
    rep=T//128
    @pl.when(step==0)
    def _():
        for r in (gj_ref,go_ref,gh_ref,gf_ref,vs_ref,hb_ref,bns_ref): r[...]=jnp.zeros_like(r)
        prepare(stats_ref,rows_ref,gathered_ref,shard,flat_ref,bn_ref,vb_ref,
            ((ROW_JOINT,wj_ref,wjt_ref),(ROW_OUT,wo_ref,wot_ref),(ROW_HIDDEN,wh_ref,wht_ref),(ROW_FINAL,wf_ref,wft_ref)))
    def col(i,n=C):
        v=vb_ref[pl.ds(i*C,n),:]
        return jnp.concatenate([v]*rep,axis=1) if rep>1 else v
    def fold(x):
        r=x[:,:128]
        for k in range(1,rep): r=r+x[:,128*k:128*(k+1)]
        return r
    scale_a=bn_ref[0:1,:]; shift_b=bn_ref[1:2,:]; r_row=bn_ref[2:3,:]; ar_row=bn_ref[3:4,:]
    first=nodes_ref[...].astype(F32)+(conv_ref[...]*scale_a+shift_b)
    firstT=first.T
    first_s[...]=firstT
    dy=dy_ref[...]
    dyT32=dy.astype(F32).T
    do_s[...]=dyT32
    def ln(x):
        m=jnp.mean(x,axis=0,keepdims=True); c=x-m
        rs=lax.rsqrt(jnp.mean(c*c,axis=0,keepdims=True)+EPS)
        return c*rs, rs
    xh1,rs1=ln(firstT)
    x1=(xh1*col(2)+col(3)).astype(BF)
    x_s[0]=x1
    q=nn(wjt_ref[0:C,:],x1)+col(4)
    qkv_s[0:C,:]=q.astype(BF)
    k=nn(wjt_ref[C:2*C,:],x1)
    qkv_s[C:2*C,:]=k.astype(BF)
    kn_s[...]=k.T.astype(BF)
    v=nn(wjt_ref[2*C:,:],x1)+col(5)
    qkv_s[2*C:,:]=v.astype(BF)
    vn_s[...]=v.T.astype(BF)
    scale=HD**-0.5
    c2=scale*1.4426950408889634
    pi=lax.broadcasted_iota(jnp.int32,(BLK,BLK),0); qi=lax.broadcasted_iota(jnp.int32,(BLK,BLK),1)
    same=(pi&3)==(qi&3)
    for b in range(rep):
        lv=jnp.broadcast_to(mask_ref[b].astype(F32),(BLK,BLK)).T
        live=(lv>0.5)&same
        bias=jnp.where(same,-1e9/scale,-1e30)
        live2=jnp.concatenate([live,live],axis=1); bias2=jnp.concatenate([bias,bias],axis=1)
        cs=slice(b*BLK,(b+1)*BLK)
        z=jnp.zeros((HD,BLK),BF)
        for g in range(3):
            kg=kn_s[cs,g*128:(g+1)*128]
            for hp in range(2):
                h0=hp*2
                def ex(i):
                    qh=qkv_s[g*128+i*32:g*128+(i+1)*32,cs]
                    return jnp.concatenate([qh if t==i else z for t in range(4)],axis=0)
                s=nn(kg,jnp.concatenate([ex(h0),ex(h0+1)],axis=1))
                s=jnp.where(live2,s,bias2)
                m=jnp.max(s,axis=0,keepdims=True)
                e=jnp.exp2((s-m)*c2)
                l=jnp.sum(e,axis=0,keepdims=True)
                a=(e*(1.0/l)).astype(BF)
                for i in range(2):
                    h=g*4+h0+i
                    ah=a[:,i*128:(i+1)*128]
                    a_s[h,:,cs]=ah
                    o_s[h*32:(h+1)*32,cs]=nn(qkv_s[2*C+h*32:2*C+(h+1)*32,cs],ah)
    ob=o_s[...].astype(BF)
    ob_s[...]=ob
    secondT=first_s[...]+(nn(wot_ref[...],ob)+col(6))
    second_s[...]=secondT
    xh2,rs2=ln(secondT)
    x2=(xh2*col(7)+col(8)).astype(BF)
    x_s[1]=x2
    dyTb=do_s[...].astype(BF)
    FC=384
    c0=0.7978845608028654; c1=0.044715
    for f in range(F//FC):
        fs=slice(f*FC,(f+1)*FC)
        hb=vb_ref[9*C+f*FC:9*C+(f+1)*FC,:]
        hb=jnp.concatenate([hb]*rep,axis=1)
        h=nn(wht_ref[fs,:],x2)+hb
        h2=h*h
        t=jnp.tanh(h*(c0+(c0*c1)*h2))
        p=0.5+0.5*t
        act=(h*p).astype(BF)
        dg=p*(1.0+h*(1.0-p)*(2*c0+(6*c0*c1)*h2))
        da=nn(wf_ref[fs,:],dyTb)
        dp32=da*dg
        dpb=dp32.astype(BF)
        hb_ref[fs,:]+=fold(dpb.astype(F32))
        o=nn(wft_ref[:,fs],act)
        d=nn(wh_ref[:,fs],dpb)
        if f==0:
            acc_s[...]=o; dx_s[...]=d
        else:
            acc_s[...]+=o; dx_s[...]+=d
        gf_ref[fs,:]+=nn(act,dy)
        gh_ref[:,fs]+=nt(x2,dpb)
    outT=second_s[...]+(acc_s[...]+col(15-2))
    out_ref[...]=outT.T.astype(BF)
    def ln_back(x,dx,gain,vi):
        xh,rs=ln(x)
        vs_ref[vi]+=fold(dx*xh)
        vs_ref[vi+1]+=fold(dx)
        dh=dx*gain
        m1=jnp.mean(dh,axis=0,keepdims=True)
        m2=jnp.mean(dh*xh,axis=0,keepdims=True)
        return rs*(dh-m1-xh*m2)
    dsec=do_s[...]+ln_back(second_s[...],dx_s[...],col(7),0)
    second_s[...]=dsec
    dbr=dsec.astype(BF)
    vs_ref[2]+=fold(dbr.astype(F32))
    go_ref[...]+=nt(ob_s[...],dbr)
    dat=nn(wo_ref[...],dbr)
    do_s[...]=dat
    dob=dat.astype(BF)
    for b in range(rep):
        cs=slice(b*BLK,(b+1)*BLK)
        z=jnp.zeros((HD,BLK),BF)
        lrow=mask_ref[b].astype(F32)
        for g in range(3):
            vg=vn_s[cs,g*128:(g+1)*128]
            for hp in range(2):
                h0=hp*2
                def ex(i):
                    qh=dob[g*128+i*32:g*128+(i+1)*32,cs]
                    return jnp.concatenate([qh if t==i else z for t in range(4)],axis=0)
                dA=nn(vg,jnp.concatenate([ex(h0),ex(h0+1)],axis=1))
                for i in range(2):
                    h=g*4+h0+i
                    hs=slice(h*32,(h+1)*32)
                    doh=dob[hs,cs]
                    delta=jnp.sum(doh.astype(F32)*o_s[hs,cs],axis=0,keepdims=True)
                    ah=a_s[h,:,cs]
                    ds=(ah.astype(F32)*(dA[:,i*128:(i+1)*128]-delta)).astype(BF)
                    kh=(qkv_s[C+h*32:C+(h+1)*32,cs].astype(F32)*lrow).astype(BF)
                    dqkv_s[h*32:(h+1)*32,cs]=(nn(kh,ds)*scale).astype(BF)
                    dqkv_s[C+h*32:C+(h+1)*32,cs]=(nt(qkv_s[hs,cs],ds)*(lrow*scale)).astype(BF)
                    dqkv_s[2*C+h*32:2*C+(h+1)*32,cs]=nt(doh,ah).astype(BF)
    vs_ref[3]+=fold(dqkv_s[0:C,:].astype(F32))
    vs_ref[4]+=fold(dqkv_s[2*C:,:].astype(F32))
    gj_ref[...]+=nt(x_s[0],dqkv_s[...])
    dx1=nn(wj_ref[...],dqkv_s[...])
    dfT=second_s[...]+ln_back(first_s[...],dx1,col(2),5)
    df=dfT.T
    dfirst_ref[...]=df
    cen=conv_ref[...]*r_row-ar_row
    bns_ref[0]+=jnp.sum((df*cen).reshape(T//8,8,C),axis=0)
    bns_ref[1]+=jnp.sum(df.reshape(T//8,8,C),axis=0)
    bns_ref[2]+=jnp.sum(dy.astype(F32).reshape(T//8,8,C),axis=0)
    @pl.when(step==pl.num_programs(0)-1)
    def _():
        flat_ref[...]=jnp.zeros_like(flat_ref)
        for vi,row in ((0,21),(1,24),(2,18),(3,12),(4,15),(5,6),(6,9)):
            for i in range(3):
                flat_ref[pl.ds(row+i,1),:]=jnp.sum(vs_ref[vi,i*128:(i+1)*128,:].T,axis=0,keepdims=True)
        for i in range(12):
            flat_ref[pl.ds(27+i,1),:]=jnp.sum(hb_ref[i*128:(i+1)*128,:].T,axis=0,keepdims=True)
        for first,mat in ((ROW_JOINT,gj_ref),(ROW_OUT,go_ref),(ROW_HIDDEN,gh_ref),(ROW_FINAL,gf_ref)):
            rows,cols=mat.shape
            per=cols//128
            for k in range(per):
                for r in range(0,rows,C):
                    flat_ref[pl.ds(first+r*per+k,C,stride=per),:]=mat[r:r+C,k*128:(k+1)*128]
        for i in range(grads_ref.shape[0]*8):
            part=flat_ref[i*shard:(i+1)*shard,:]
            pad=grads_ref.shape[-2]-shard
            grads_ref[i//8,(i//4)%2,(i//2)%2,i%2]=jnp.concatenate([part,jnp.zeros((pad,128),F32)],axis=0).astype(BF)


def middle(conv,nodes,dy,mask3,stats,rows,gathered,shard):
    n=conv.shape[0]
    row=rows_of(C,T)
    flat_rows=gathered.shape[0]*8*shard
    in_specs=[row,row,row,pl.BlockSpec((T//128,1,128),lambda i:(i,0,0)),whole(*stats.shape),whole(*rows.shape),whole(*gathered.shape)]
    outs=[((n,C),BF,row),((n,C),F32,row),(gathered.shape,BF,whole(*gathered.shape)),((3,8,C),F32,whole(3,8,C))]
    mats=[]
    for shape in ((C,3*C),(C,C),(C,F),(F,C)): mats+=[(shape,BF),(shape[::-1],BF)]
    scr=[pltpu.VMEM(s,d) for s,d in [((flat_rows,128),F32),((8,C),F32),((ROW_CONV*128,128),F32)]+mats+[((C,3*C),F32),((C,C),F32),((C,F),F32),((F,C),F32),((7,C,128),F32),((F,128),F32),((C,T),F32),((C,T),F32),((3*C,T),BF),((T,C),BF),((T,C),BF),((HEADS,BLK,T),BF),((C,T),F32),((C,T),BF),((C,T),F32),((3*C,T),BF),((2,C,T),BF),((C,T),F32),((C,T),F32)]]
    return pl.pallas_call(functools.partial(mid_kernel,shard),grid=(n//T,),in_specs=in_specs,out_specs=[o[2] for o in outs],
      out_shape=[jax.ShapeDtypeStruct(o[0],o[1]) for o in outs],scratch_shapes=scr,
      compiler_params=VMEM)(conv,nodes,dy,mask3,stats,rows,gathered)


def shards(nodes_in, out_grad, neighbours, node_mask, master, first_moment, second_moment):
    n = nodes_in.shape[0]
    count, cores = lax.axis_size(AXES), lax.axis_size("grp")
    shard = master.shape[0] // 128
    flat = [a.reshape(shard, 128) for a in (master, first_moment, second_moment)]
    mask3 = node_mask.reshape(n // 128, 1, 128)
    convolved, gathered, first_rows, stats = convolve(neighbours, nodes_in, mask3, flat[0], count, cores)
    output, delta_first, grads, norm_sums = middle(
        convolved, nodes_in, out_grad, mask3, stats, first_rows, gathered, shard
    )
    node_grad, new_master, new_first, new_second, new_low, bias_total = convolve_back(
        neighbours, delta_first, convolved, nodes_in, mask3, norm_sums, stats, first_rows, grads, *flat, count, cores
    )
    return (
        output,
        node_grad,
        new_master.reshape(-1),
        new_first.reshape(-1),
        new_second.reshape(-1),
        new_low.reshape(-1),
        bias_total.reshape(-1),
    )


def solution(mesh):
    rows, flat = P(AXES, None), P(AXES)
    return jax.shard_map(
        shards,
        mesh=mesh,
        in_specs=(rows, rows, rows, flat, flat, flat, flat),
        out_specs=(rows, rows, flat, flat, flat, flat, P()),
        check_vma=False,
    )
```

time: 603 us -> 348 us (0.58)
  blocking collectives: 208 us -> 0 us
  Pallas kernels: 278 us -> 334 us
  waiting for transfers between devices: 39.8 us -> 0 us
  other arithmetic: 23.1 us -> 1.23 us
  starting transfers between devices: 14.6 us -> 0 us
  between operations: 14.2 us -> 0.66 us
  local copies, waits for them, and re-layouts: 23.3 us -> 11.7 us
    psum x3 -> x0, blocking collectives: 120 us -> none  [the longest x1 40.5 us: shards(): conv_grad = lax.psum(jnp.sum(conv_grad, axis=1), AXES)]
    unnamed x1 -> x0, blocking collectives: 88.2 us -> none
    pallas_call x4 -> x3, Pallas kernels: 278 us -> 334 us  [the longest x1 187 us: middle(): pl.pallas_call(functools.partial(mid_kernel, shard), grid=(n // T,), in_s...]
    all_gather x1 -> x0, waiting for transfers between devices: 39.8 us -> none  [shards(): lax.all_gather(master.reshape(shard, 128).astype(BF), AXES, axis=0, tiled...]
    ppermute x6 -> x0, starting transfers between devices: 12.6 us -> none  [the longest x3 8.76 us: extended_2(): low = lax.ppermute(block[block.shape[0] - width:], AXES, forward)]
    concatenate x2 -> x0, other arithmetic: 9.97 us -> none  [extended_2(): return jnp.concatenate([low, block, high], axis=0)]
    convert_element_type x3 -> x0, other arithmetic: 7.18 us -> none  [the longest x1 5.4 us: shards(): delta_conv = (delta_first * (batch_gain * inverse) + live_rows * (delta_a...]
  transfers between devices with their start and end apart: 8 -> 0, of which waited for: 1 -> 0; matrix products, arithmetic and copies ran while one was open for 18% -> 0% of each run, Pallas kernels for 7% -> 0%
where the time goes in v2:
time: 348 us
  Pallas kernels  334 us (96%)
  local copies, waits for them, and re-layouts  11.7 us (3%)
    pallas_call x1, Pallas kernels, middle(): pl.pallas_call(functools.partial(mid_kernel, shard), grid=(n // T,), in_s...  187 us
    pallas_call x1, Pallas kernels, convolve_back(): pl.pallas_call(functools.partial(conv_back_kernel, count, cores, owners),...  73.7 us
    pallas_call x1, Pallas kernels, convolve(): pl.pallas_call(functools.partial(conv_kernel, count, cores, owners), grid...  73.3 us
    unnamed x14, local copies, waits for them, and re-layouts  11.7 us

profile of v2, /device:TPU:0, one launch (start us, length us, event | category | flops | bytes accessed | tf_op | source)
XLA Modules:
  0.0 348.0 jit_solution(5165506381884665118)
XLA Ops:
  0.6 3.0 copy.14.near_ref.near_hbm
  3.6 73.3 %shard_map.126 = (f32[4096,384]{1,0:T(8,128)}, bf16[4,2,2,2,448,128]{5,4,3,2,1,0:T(8,128)(2,1)}, f32[128,128]{1,0:T(8,128)}, f32[8,384]{1,0:T(8,128)}) custom-call(s32[4096,27]{1,0:T(8,128)} %copy.14.near_ref.near_hbm, bf16[4096,384]{1,0:T(8,128)(2,1)} %x_ref.1, s32[32,1,128]{2,1,0:T(1,128)} %bitcast.15, f32[436,128]{1,0:T(8,128)} %bitcast.8), custom_call_target="tpu_custom_call" | custom-call | tf_op jit(solution)/shard_map/pallas_call | solution.py:282
  76.9 187.5 %shard_map.127 = (bf16[4096,384]{1,0:T(8,128)(2,1)}, f32[4096,384]{1,0:T(8,128)}, bf16[4,2,2,2,448,128]{5,4,3,2,1,0:T(8,128)(2,1)}, f32[3,8,384]{2,1,0:T(8,128)}) custom-call(f32[4096,384]{1,0:T(8,128)} %get-tuple-element.21.conv_ref.conv_hbm, bf16[4096,384]{1,0:T(8,128)(2,1)} %x_ref.1, bf16[4096,384]{1,0:T(8,128)(2,1)} %dy_ref.1, s32[32,1,128]{2,1,0:T(1,128)} %bitcast.16, ...), custom_call_target="tpu_custom_call" | custom-call | tf_op jit(solution)/shard_map/pallas_call | solution.py:814
  264.4 73.7 %shard_map.128 = (f32[4096,384]{1,0:T(8,128)}, f32[436,128]{1,0:T(8,128)}, f32[436,128]{1,0:T(8,128)}, f32[436,128]{1,0:T(8,128)}, bf16[436,128]{1,0:T(8,128)(2,1)}, /*index=5*/f32[1,384]{1,0:T(1,128)}) custom-call(s32[4096,27]{1,0:T(8,128)} %copy.14.near_ref.near_hbm, f32[4096,384]{1,0:T(8,128)} %get-tuple-element.26.first_hbm, ...), custom_call_target="tpu_custom_call" | custom-call | tf_op jit(solution)/shard_map/pallas_call | solution.py:559
  338.1 1.2 reduce
  339.3 0.0 copy-start.2
  339.3 0.0 copy-start.1
  339.3 0.0 copy-start
  339.3 0.0 copy-start.3
  339.3 6.0 %copy.21 = f32[4096,384]{1,0:T(8,128)} copy(f32[4096,384]{1,0:T(8,128)} %get-tuple-element.43) | data formatting | bytes 12582912
  345.3 0.0 copy-done.2
  345.3 0.7 copy.22
  346.0 0.0 copy-done.1
  346.0 0.7 copy.23
  346.7 0.0 copy-done
  346.7 0.7 copy.24
  347.4 0.0 copy-done.3
  347.4 0.7 copy.25
Async XLA Ops:
  339.3 6.0 %copy-start.2 = (f32[436,128]{1,0:T(8,128)S(1)}, f32[436,128]{1,0:T(8,128)}, u32[]{:S(2)}) copy-start(f32[436,128]{1,0:T(8,128)} %get-tuple-element.30) | copy-start | bytes 669700
  339.3 6.7 %copy-start.1 = (f32[436,128]{1,0:T(8,128)S(1)}, f32[436,128]{1,0:T(8,128)}, u32[]{:S(2)}) copy-start(f32[436,128]{1,0:T(8,128)} %get-tuple-element.31) | copy-start | bytes 669700
  339.3 7.4 %copy-start = (f32[436,128]{1,0:T(8,128)S(1)}, f32[436,128]{1,0:T(8,128)}, u32[]{:S(2)}) copy-start(f32[436,128]{1,0:T(8,128)} %get-tuple-element.32) | copy-start | bytes 669700
  339.3 8.1 %copy-start.3 = (bf16[436,128]{1,0:T(8,128)(2,1)S(1)}, bf16[436,128]{1,0:T(8,128)(2,1)}, u32[]{:S(2)}) copy-start(bf16[436,128]{1,0:T(8,128)(2,1)} %get-tuple-element.33) | copy-start | bytes 334852

commit v3 on v2

--- a/solution.py
+++ b/solution.py
@@ -19,7 +19,7 @@
 BF = jnp.bfloat16
 
 BLK = 128
-T = 256
+T = 512
 ROW_CONV = (10 * C + F) // 128
 ROW_JOINT = ROW_CONV + 27 * C // 128
 ROW_OUT = ROW_JOINT + C * 3 * C // 128
@@ -673,31 +673,48 @@
     c2=scale*1.4426950408889634
     pi=lax.broadcasted_iota(jnp.int32,(BLK,BLK),0); qi=lax.broadcasted_iota(jnp.int32,(BLK,BLK),1)
     same=(pi&3)==(qi&3)
+    lives=[]
+    def bd(ref,row,blk):
+        parts=[]
+        z=jnp.zeros((HD,BLK),BF)
+        for i in range(2):
+            pass
+        return parts
+    z=jnp.zeros((HD,BLK),BF)
+    masks=[]
     for b in range(rep):
         lv=jnp.broadcast_to(mask_ref[b].astype(F32),(BLK,BLK)).T
         live=(lv>0.5)&same
         bias=jnp.where(same,-1e9/scale,-1e30)
-        live2=jnp.concatenate([live,live],axis=1); bias2=jnp.concatenate([bias,bias],axis=1)
-        cs=slice(b*BLK,(b+1)*BLK)
-        z=jnp.zeros((HD,BLK),BF)
-        for g in range(3):
-            kg=kn_s[cs,g*128:(g+1)*128]
-            for hp in range(2):
-                h0=hp*2
-                def ex(i):
-                    qh=qkv_s[g*128+i*32:g*128+(i+1)*32,cs]
-                    return jnp.concatenate([qh if t==i else z for t in range(4)],axis=0)
-                s=nn(kg,jnp.concatenate([ex(h0),ex(h0+1)],axis=1))
-                s=jnp.where(live2,s,bias2)
-                m=jnp.max(s,axis=0,keepdims=True)
-                e=jnp.exp2((s-m)*c2)
-                l=jnp.sum(e,axis=0,keepdims=True)
-                a=(e*(1.0/l)).astype(BF)
-                for i in range(2):
-                    h=g*4+h0+i
-                    ah=a[:,i*128:(i+1)*128]
-                    a_s[h,:,cs]=ah
-                    o_s[h*32:(h+1)*32,cs]=nn(qkv_s[2*C+h*32:2*C+(h+1)*32,cs],ah)
+        masks.append((jnp.concatenate([live,live],axis=1),jnp.concatenate([bias,bias],axis=1)))
+    def ex(ref,g,i,cs):
+        qh=ref[g*128+i*32:g*128+(i+1)*32,cs]
+        return jnp.concatenate([qh if t==i else z for t in range(4)],axis=0)
+    tasks=[(b,g,hp*2) for b in range(rep) for g in range(3) for hp in range(2)]
+    S={};A={}
+    def f_s(t):
+        b,g,h0=t; cs=slice(b*BLK,(b+1)*BLK)
+        S[t]=nn(kn_s[cs,g*128:(g+1)*128],jnp.concatenate([ex(qkv_s,g,h0,cs),ex(qkv_s,g,h0+1,cs)],axis=1))
+    def f_a(t):
+        b,g,h0=t; cs=slice(b*BLK,(b+1)*BLK)
+        s=jnp.where(masks[b][0],S.pop(t),masks[b][1])
+        m=jnp.max(s,axis=0,keepdims=True)
+        e=jnp.exp2((s-m)*c2)
+        l=jnp.sum(e,axis=0,keepdims=True)
+        a=(e*(1.0/l)).astype(BF)
+        for i in range(2): a_s[g*4+h0+i,:,cs]=a[:,i*128:(i+1)*128]
+        A[t]=a
+    def f_o(t):
+        b,g,h0=t; cs=slice(b*BLK,(b+1)*BLK)
+        a=A.pop(t)
+        for i in range(2):
+            h=g*4+h0+i
+            o_s[h*32:(h+1)*32,cs]=nn(qkv_s[2*C+h*32:2*C+(h+1)*32,cs],a[:,i*128:(i+1)*128])
+    def skew(stages,tasks):
+        for i in range(len(tasks)+len(stages)-1):
+            for k,st in enumerate(stages):
+                if 0<=i-k<len(tasks): st(tasks[i-k])
+    skew([f_s,f_a,f_o],tasks)
     ob=o_s[...].astype(BF)
     ob_s[...]=ob
     secondT=first_s[...]+(nn(wot_ref[...],ob)+col(6))
@@ -706,22 +723,29 @@
     x2=(xh2*col(7)+col(8)).astype(BF)
     x_s[1]=x2
     dyTb=do_s[...].astype(BF)
-    FC=384
+    FC=512
     c0=0.7978845608028654; c1=0.044715
-    for f in range(F//FC):
+    HH={};PP={}
+    def g_h(f):
+        fs=slice(f*FC,(f+1)*FC)
+        HH[f]=(nn(wht_ref[fs,:],x2),nn(wf_ref[fs,:],dyTb))
+    def g_g(f):
         fs=slice(f*FC,(f+1)*FC)
         hb=vb_ref[9*C+f*FC:9*C+(f+1)*FC,:]
         hb=jnp.concatenate([hb]*rep,axis=1)
-        h=nn(wht_ref[fs,:],x2)+hb
+        h,da=HH.pop(f)
+        h=h+hb
         h2=h*h
         t=jnp.tanh(h*(c0+(c0*c1)*h2))
         p=0.5+0.5*t
         act=(h*p).astype(BF)
         dg=p*(1.0+h*(1.0-p)*(2*c0+(6*c0*c1)*h2))
-        da=nn(wf_ref[fs,:],dyTb)
-        dp32=da*dg
-        dpb=dp32.astype(BF)
+        dpb=(da*dg).astype(BF)
         hb_ref[fs,:]+=fold(dpb.astype(F32))
+        PP[f]=(act,dpb)
+    def g_o(f):
+        fs=slice(f*FC,(f+1)*FC)
+        act,dpb=PP.pop(f)
         o=nn(wft_ref[:,fs],act)
         d=nn(wh_ref[:,fs],dpb)
         if f==0:
@@ -730,6 +754,7 @@
             acc_s[...]+=o; dx_s[...]+=d
         gf_ref[fs,:]+=nn(act,dy)
         gh_ref[:,fs]+=nt(x2,dpb)
+    skew([g_h,g_g,g_o],list(range(F//FC)))
     outT=second_s[...]+(acc_s[...]+col(15-2))
     out_ref[...]=outT.T.astype(BF)
     def ln_back(x,dx,gain,vi):
@@ -748,29 +773,30 @@
     dat=nn(wo_ref[...],dbr)
     do_s[...]=dat
     dob=dat.astype(BF)
-    for b in range(rep):
-        cs=slice(b*BLK,(b+1)*BLK)
-        z=jnp.zeros((HD,BLK),BF)
+    D={};G={}
+    def b_d(t):
+        b,g,h0=t; cs=slice(b*BLK,(b+1)*BLK)
+        D[t]=nn(vn_s[cs,g*128:(g+1)*128],jnp.concatenate([ex(dob,g,h0,cs),ex(dob,g,h0+1,cs)],axis=1))
+    def b_s(t):
+        b,g,h0=t; cs=slice(b*BLK,(b+1)*BLK)
+        dA=D.pop(t)
+        out=[]
+        for i in range(2):
+            h=g*4+h0+i; hs=slice(h*32,(h+1)*32)
+            delta=jnp.sum(dob[hs,cs].astype(F32)*o_s[hs,cs],axis=0,keepdims=True)
+            out.append((a_s[h,:,cs].astype(F32)*(dA[:,i*128:(i+1)*128]-delta)).astype(BF))
+        G[t]=out
+    def b_q(t):
+        b,g,h0=t; cs=slice(b*BLK,(b+1)*BLK)
         lrow=mask_ref[b].astype(F32)
-        for g in range(3):
-            vg=vn_s[cs,g*128:(g+1)*128]
-            for hp in range(2):
-                h0=hp*2
-                def ex(i):
-                    qh=dob[g*128+i*32:g*128+(i+1)*32,cs]
-                    return jnp.concatenate([qh if t==i else z for t in range(4)],axis=0)
-                dA=nn(vg,jnp.concatenate([ex(h0),ex(h0+1)],axis=1))
-                for i in range(2):
-                    h=g*4+h0+i
-                    hs=slice(h*32,(h+1)*32)
-                    doh=dob[hs,cs]
-                    delta=jnp.sum(doh.astype(F32)*o_s[hs,cs],axis=0,keepdims=True)
-                    ah=a_s[h,:,cs]
-                    ds=(ah.astype(F32)*(dA[:,i*128:(i+1)*128]-delta)).astype(BF)
-                    kh=(qkv_s[C+h*32:C+(h+1)*32,cs].astype(F32)*lrow).astype(BF)
-                    dqkv_s[h*32:(h+1)*32,cs]=(nn(kh,ds)*scale).astype(BF)
-                    dqkv_s[C+h*32:C+(h+1)*32,cs]=(nt(qkv_s[hs,cs],ds)*(lrow*scale)).astype(BF)
-                    dqkv_s[2*C+h*32:2*C+(h+1)*32,cs]=nt(doh,ah).astype(BF)
+        out=G.pop(t)
+        for i in range(2):
+            h=g*4+h0+i; hs=slice(h*32,(h+1)*32); ds=out[i]
+            kh=(qkv_s[C+h*32:C+(h+1)*32,cs].astype(F32)*lrow).astype(BF)
+            dqkv_s[h*32:(h+1)*32,cs]=(nn(kh,ds)*scale).astype(BF)
+            dqkv_s[C+h*32:C+(h+1)*32,cs]=(nt(qkv_s[hs,cs],ds)*(lrow*scale)).astype(BF)
+            dqkv_s[2*C+h*32:2*C+(h+1)*32,cs]=nt(dob[hs,cs],a_s[h,:,cs]).astype(BF)
+    skew([b_d,b_s,b_q],tasks)
     vs_ref[3]+=fold(dqkv_s[0:C,:].astype(F32))
     vs_ref[4]+=fold(dqkv_s[2*C:,:].astype(F32))
     gj_ref[...]+=nt(x_s[0],dqkv_s[...])

time: 348 us -> 273 us (0.78)
  Pallas kernels: 334 us -> 259 us
    pallas_call x1, Pallas kernels: 187 us -> 112 us  [middle(): pl.pallas_call(functools.partial(mid_kernel, shard), grid=(n // T,), in_s...]
where the time goes in v3:
time: 273 us
  Pallas kernels  259 us (95%)
  local copies, waits for them, and re-layouts  11.7 us (4%)
    pallas_call x1, Pallas kernels, middle(): pl.pallas_call(functools.partial(mid_kernel, shard), grid=(n // T,), in_s...  112 us
    pallas_call x1, Pallas kernels, convolve_back(): pl.pallas_call(functools.partial(conv_back_kernel, count, cores, owners),...  73.7 us
    pallas_call x1, Pallas kernels, convolve(): pl.pallas_call(functools.partial(conv_kernel, count, cores, owners), grid...  73.3 us
    unnamed x14, local copies, waits for them, and re-layouts  11.7 us

profile of v3, /device:TPU:0, one launch (start us, length us, event | category | flops | bytes accessed | tf_op | source)
XLA Modules:
  0.0 273.0 jit_solution(59537902912115071)
XLA Ops:
  0.6 3.0 %copy.14.near_ref.near_hbm = s32[4096,27]{1,0:T(8,128)} copy(s32[4096,27]{0,1:T(8,128)} %param.9) | data formatting | bytes 884736 | tf_op args[2]
  3.6 73.3 %shard_map.126 = (f32[4096,384]{1,0:T(8,128)}, bf16[4,2,2,2,448,128]{5,4,3,2,1,0:T(8,128)(2,1)}, f32[128,128]{1,0:T(8,128)}, f32[8,384]{1,0:T(8,128)}) custom-call(s32[4096,27]{1,0:T(8,128)} %copy.14.near_ref.near_hbm, bf16[4096,384]{1,0:T(8,128)(2,1)} %x_ref.1, s32[32,1,128]{2,1,0:T(1,128)} %bitcast.15, f32[436,128]{1,0:T(8,128)} %bitcast.8), custom_call_target="tpu_custom_call" | custom-call | tf_op jit(solution)/shard_map/pallas_call | solution.py:282
  76.9 112.4 %shard_map.127 = (bf16[4096,384]{1,0:T(8,128)(2,1)}, f32[4096,384]{1,0:T(8,128)}, bf16[4,2,2,2,448,128]{5,4,3,2,1,0:T(8,128)(2,1)}, f32[3,8,384]{2,1,0:T(8,128)}) custom-call(f32[4096,384]{1,0:T(8,128)} %get-tuple-element.21.conv_ref.conv_hbm, bf16[4096,384]{1,0:T(8,128)(2,1)} %x_ref.1, bf16[4096,384]{1,0:T(8,128)(2,1)} %dy_ref.1, s32[32,1,128]{2,1,0:T(1,128)} %bitcast.16, ...), custom_call_target="tpu_custom_call" | custom-call | tf_op jit(solution)/shard_map/pallas_call | solution.py:840
  189.3 73.7 %shard_map.128 = (f32[4096,384]{1,0:T(8,128)}, f32[436,128]{1,0:T(8,128)}, f32[436,128]{1,0:T(8,128)}, f32[436,128]{1,0:T(8,128)}, bf16[436,128]{1,0:T(8,128)(2,1)}, /*index=5*/f32[1,384]{1,0:T(1,128)}) custom-call(s32[4096,27]{1,0:T(8,128)} %copy.14.near_ref.near_hbm, f32[4096,384]{1,0:T(8,128)} %get-tuple-element.26.first_hbm, ...), custom_call_target="tpu_custom_call" | custom-call | tf_op jit(solution)/shard_map/pallas_call | solution.py:559
  263.0 1.2 reduce
  264.3 0.0 copy-start.2
  264.3 0.0 copy-start.1
  264.3 0.0 copy-start
  264.3 0.0 copy-start.3
  264.3 6.0 %copy.21 = f32[4096,384]{1,0:T(8,128)} copy(f32[4096,384]{1,0:T(8,128)} %get-tuple-element.43) | data formatting | bytes 12582912
  270.2 0.0 copy-done.2
  270.3 0.7 copy.22
  271.0 0.0 copy-done.1
  271.0 0.7 copy.23
  271.7 0.0 copy-done
  271.7 0.7 copy.24
  272.4 0.0 copy-done.3
  272.4 0.7 copy.25
Async XLA Ops:
  264.3 6.0 %copy-start.2 = (f32[436,128]{1,0:T(8,128)S(1)}, f32[436,128]{1,0:T(8,128)}, u32[]{:S(2)}) copy-start(f32[436,128]{1,0:T(8,128)} %get-tuple-element.30) | copy-start | bytes 669700
  264.3 6.7 %copy-start.1 = (f32[436,128]{1,0:T(8,128)S(1)}, f32[436,128]{1,0:T(8,128)}, u32[]{:S(2)}) copy-start(f32[436,128]{1,0:T(8,128)} %get-tuple-element.31) | copy-start | bytes 669700
  264.3 7.4 %copy-start = (f32[436,128]{1,0:T(8,128)S(1)}, f32[436,128]{1,0:T(8,128)}, u32[]{:S(2)}) copy-start(f32[436,128]{1,0:T(8,128)} %get-tuple-element.32) | copy-start | bytes 669700
  264.3 8.1 %copy-start.3 = (bf16[436,128]{1,0:T(8,128)(2,1)S(1)}, bf16[436,128]{1,0:T(8,128)(2,1)}, u32[]{:S(2)}) copy-start(bf16[436,128]{1,0:T(8,128)(2,1)} %get-tuple-element.33) | copy-start | bytes 334852

commit v4 on v3

--- a/solution.py
+++ b/solution.py
@@ -20,6 +20,7 @@
 
 BLK = 128
 T = 512
+TB = 512
 ROW_CONV = (10 * C + F) // 128
 ROW_JOINT = ROW_CONV + 27 * C // 128
 ROW_OUT = ROW_JOINT + C * 3 * C // 128
@@ -41,11 +42,32 @@
     return pl.BlockSpec(shape, lambda i: (0,) * len(shape), pipeline_mode=pl.Buffered(1))
 
 
+def skew(stages, tasks):
+    for i in range(len(tasks) + len(stages) - 1):
+        for k, stage in enumerate(stages):
+            if 0 <= i - k < len(tasks):
+                stage(tasks[i - k])
+
+
+def along_sublanes(row):
+    parts = [row[:, i : i + 128] for i in range(0, row.shape[1], 128)]
+    return jnp.concatenate([jnp.broadcast_to(p, (128, 128)).T for p in parts], axis=0)
+
+
+def lane_sums(value):
+    parts = [value[i : i + 128, :].T for i in range(0, value.shape[0], 128)]
+    return jnp.concatenate([jnp.sum(p, axis=0, keepdims=True) for p in parts], axis=1)
+
+
 def rows_of(width, size):
     return pl.BlockSpec((size, width), lambda i: (i, 0))
 
 
 MESH = pl.DeviceIdType.MESH
+
+
+def CUTS_GATHER(nh):
+    return [1 + (s + 1) // nh for s in range(nh)] + [4, 7]
 
 
 def round_up(value, step):
@@ -92,7 +114,7 @@
     )
 
 
-def all_sum(value, me, count, cores, slots, send_sems, recv_sems):
+def all_sum(value, me, count, cores, slots, send_sems, recv_sems, beside=None):
     for s, (stride, size) in enumerate(stages_of(count)):
         mine, partners = others(me, stride, size)
         slots[s, mine] = value
@@ -102,6 +124,8 @@
         ]
         for copy in copies:
             copy.start()
+        if beside is not None:
+            beside(s)
         for copy in copies:
             copy.wait()
         value = slots[s, 0]
@@ -119,10 +143,10 @@
     ]
 
 
-def conv_kernel(count, cores, owners, near_ref, nodes_ref, mask_ref, master_ref,
-                conv_ref, gathered_ref, first_ref, stats_ref,
-                ext, early, weight, sums, own_s, local_sem, halo_send, halo_recv, e_send, e_recv, g_send, g_recv,
-                slots, s_send, s_recv):
+def conv_kernel(count, cores, owners, near_ref, nodes_ref, dy_ref, mask_ref, master_ref,
+                convt_ref, conv_ref, nodest_ref, dyt_ref, gathered_ref, first_ref, stats_ref,
+                ext, extt, dy_s, early, weight, sums, own_s, local_sem, halo_send, halo_recv, e_send, e_recv, g_send,
+                g_recv, slots, s_send, s_recv):
     step = pl.program_id(0)
     steps = pl.num_programs(0)
     block = (step + 1) % steps
@@ -139,6 +163,12 @@
 
     local = pltpu.make_async_copy(nodes_ref, ext.at[pl.ds(HALO, n)], local_sem.at[0])
     keep = pltpu.make_async_copy(own_s, gathered_ref.at[high, y, x, g], local_sem.at[1])
+    local_dy = pltpu.make_async_copy(dy_ref, dy_s, local_sem.at[2])
+
+    def turn(k):
+        at = pl.ds(pl.multiple_of(k * BLK, BLK), BLK)
+        extt[:, at] = ext[at, :].T
+        return 0
     to_left = send(nodes_ref.at[pl.ds(0, HALO)], ext.at[pl.ds(HALO + n, HALO)], halo_send.at[0], halo_recv.at[0], left, cores)
     to_right = send(nodes_ref.at[pl.ds(n - HALO, HALO)], ext.at[pl.ds(0, HALO)], halo_send.at[1], halo_recv.at[1], right, cores)
 
@@ -173,13 +203,12 @@
 
     plan = [functools.partial(high_copies, s) for s in range(nh)]
     plan += [functools.partial(quad_copies, 0), functools.partial(quad_copies, 1), core_copies]
-    cuts = [6] * nh + [11, 19, 27]
-    for s in range(nh):
-        cuts[s] = 3 + 5 * (s + 1) // nh
+    cuts = CUTS_GATHER(nh)
 
     @pl.when(step == 0)
     def _():
         local.start()
+        local_dy.start()
         sums[...] = jnp.zeros_like(sums)
         own = jnp.concatenate([master_ref[...], jnp.zeros((padded - shard, 128), F32)], axis=0).astype(BF)
         own_s[...] = own
@@ -219,6 +248,8 @@
         keep.wait()
         for copy in plan[0]():
             copy.start()
+        local.wait()
+        lax.fori_loop(1, n // BLK, lambda k, _: turn(k), 0)
         for o in range(owners):
             @pl.when(low != o)
             def _():
@@ -226,87 +257,126 @@
         for o in range(owners):
             rows = min(shard, e_rows)
             first_ref[pl.ds(o * shard, rows), :] = early[o].astype(F32)[:rows]
-        for k in range(3):
-            weight[:, k * 128 : (k + 1) * 128] = first_ref[pl.ds(ROW_CONV + k, 27, stride=3), :]
-        local.wait()
-
-    for s in range(len(plan)):
+        for j in range(27):
+            row = jnp.concatenate([first_ref[ROW_CONV + 3 * j + i : ROW_CONV + 3 * j + i + 1, :] for i in range(3)], axis=1)
+            weight[j] = along_sublanes(row)
+
+    for s in range(len(plan) - 1):
         @pl.when(step == cuts[s])
         def _(s=s):
             for copy in plan[s]():
                 copy.wait()
-            if s + 1 < len(plan):
-                for copy in plan[s + 1]():
-                    copy.start()
+            for copy in plan[s + 1]():
+                copy.start()
 
     @pl.when(step == steps - 2)
     def _():
         to_left.wait()
         to_right.wait()
-
-    window = ext[pl.ds(pl.multiple_of(block * BLK, BLK), 2 * BLK), :]
-    near = near_ref[...]
-    place = near + lax.broadcasted_iota(jnp.int32, near.shape, 0)
-    place = jnp.where(near < 0, -1, place).astype(F32).astype(BF)
-    lane = lax.broadcasted_iota(jnp.int32, (BLK, 2 * BLK), 1).astype(F32).astype(BF)
+        turn(0)
+        turn(n // BLK)
+
+    sub = lax.broadcasted_iota(jnp.int32, (2 * BLK, BLK), 0).astype(F32).astype(BF)
     one, zero = jnp.ones((), BF), jnp.zeros((), BF)
-    total = jnp.zeros((BLK, C), F32)
-    for j in range(27):
-        pick = jnp.where(place[:, j : j + 1] == lane, one, zero)
-        total += nn(pick, window) * weight[j : j + 1, :]
-    conv_ref[...] = total
-    live = jnp.broadcast_to(mask_ref[0].astype(F32), (BLK, BLK)).T
-    live = jnp.concatenate([live] * 3, axis=1)
-    kept = total * live
-    sums[0] += jnp.sum(kept.reshape(BLK // 8, 8, C), axis=0)
-    sums[1] += jnp.sum((kept * total).reshape(BLK // 8, 8, C), axis=0)
-    sums[2] += jnp.sum(live.reshape(BLK // 8, 8, C), axis=0)
+    pairs = [(j, j + 1) for j in range(0, 12, 2)] + [(12, 14)] + [(j, j + 1) for j in range(15, 27, 2)]
+    at = pl.multiple_of(block * T, T)
+    lane = lax.broadcasted_iota(jnp.int32, (27, BLK), 1)
+    places, totals, picks, comes = {}, {}, {}, {}
+    for b in range(T // BLK):
+        near = near_ref[:, b * BLK : (b + 1) * BLK]
+        places[b] = jnp.where(near < 0, -1, near + lane).astype(F32).astype(BF)
+
+    def pick(task):
+        b, q = task
+        if q == 0:
+            center = ext[pl.ds(at + b * BLK + HALO, BLK), :].astype(F32).T
+            nodest_ref[:, b * BLK : (b + 1) * BLK] = center.astype(BF)
+            totals[b] = center * weight[13]
+        picks[task] = jnp.concatenate(
+            [jnp.where(places[b][j : j + 1, :] == sub, one, zero) for j in pairs[q]], axis=1
+        )
+
+    def multiply(task):
+        b, q = task
+        comes[task] = nn(extt[:, pl.ds(at + b * BLK, 2 * BLK)], picks.pop(task))
+
+    def add(task):
+        b, q = task
+        come = comes.pop(task)
+        totals[b] = totals[b] + (come[:, :BLK] * weight[pairs[q][0]] + come[:, BLK:] * weight[pairs[q][1]])
+        if q == len(pairs) - 1:
+            total = totals.pop(b)
+            convt_ref[:, b * BLK : (b + 1) * BLK] = total
+            conv_ref[b * BLK : (b + 1) * BLK, :] = total.T.astype(BF)
+            live = mask_ref[b].astype(F32)
+            kept = total * live
+            sums[0] += kept
+            sums[1] += kept * total
+            sums[2, 0:1] += live
+
+    skew([pick, multiply, add], [(b, q) for b in range(T // BLK) for q in range(len(pairs))])
 
     @pl.when(step == steps - 1)
     def _():
-        rows = [jnp.sum(sums[i], axis=0, keepdims=True) for i in range(3)]
+        rows = [lane_sums(sums[i]) for i in range(2)]
+        rows += [jnp.broadcast_to(jnp.sum(sums[2, 0:1], axis=1, keepdims=True), (1, C))]
         rows = jnp.concatenate(rows + [jnp.zeros((5, C), F32)], axis=0)
-        stats_ref[...] = all_sum(rows, me, count, cores, slots, s_send, s_recv)
-
-
-def convolve(near, nodes, mask3, master, count, cores):
+        local_dy.wait()
+        cut = len(stages_of(count))
+
+        def beside(s):
+            def body(k, _):
+                at = pl.ds(pl.multiple_of(k * BLK, BLK), BLK)
+                dyt_ref[:, at] = dy_s[at, :].T
+                return 0
+            lax.fori_loop(n // BLK * s // cut, n // BLK * (s + 1) // cut, body, 0)
+
+        stats_ref[...] = all_sum(rows, me, count, cores, slots, s_send, s_recv, beside)
+        for copy in plan[-1]():
+            copy.wait()
+
+
+def convolve(near, nodes, dy, mask3, master, count, cores):
     n = nodes.shape[0]
-    steps = n // BLK
+    steps = n // T
     shard = master.shape[0]
     padded = round_up(shard, 32)
     owners = -(-ROW_JOINT // shard)
     e_rows = min(padded, round_up(ROW_JOINT, 16))
-    turned = lambda i: ((i + 1) % steps, 0)
+    down = pl.BlockSpec((T, C), lambda i: ((i + 1) % steps, 0))
+    across = pl.BlockSpec((C, T), lambda i: (0, (i + 1) % steps))
+    anywhere = pl.BlockSpec(memory_space=pl.ANY)
     stages = len(stages_of(count // 8)) + 3
     first_rows = round_up((owners - 1) * shard + e_rows, 8)
     return pl.pallas_call(
         functools.partial(conv_kernel, count, cores, owners),
         grid=(steps,),
         in_specs=[
-            pl.BlockSpec((BLK, 27), turned),
-            pl.BlockSpec(memory_space=pl.ANY),
-            pl.BlockSpec((1, 1, 128), lambda i: ((i + 1) % steps, 0, 0)),
+            pl.BlockSpec((27, T), lambda i: (0, (i + 1) % steps)),
+            anywhere,
+            anywhere,
+            pl.BlockSpec((T // BLK, 1, 128), lambda i: ((i + 1) % steps, 0, 0)),
             whole(shard, 128),
         ],
-        out_specs=[
-            pl.BlockSpec((BLK, C), turned),
-            pl.BlockSpec(memory_space=pl.ANY),
-            whole(first_rows, 128),
-            whole(8, C),
-        ],
+        out_specs=[across, down, across, whole(C, n), anywhere, whole(first_rows, 128), whole(8, C)],
         out_shape=[
-            jax.ShapeDtypeStruct((n, C), F32),
+            jax.ShapeDtypeStruct((C, n), F32),
+            jax.ShapeDtypeStruct((n, C), BF),
+            jax.ShapeDtypeStruct((C, n), BF),
+            jax.ShapeDtypeStruct((C, n), BF),
             jax.ShapeDtypeStruct((count // 8, 2, 2, 2, padded, 128), BF),
             jax.ShapeDtypeStruct((first_rows, 128), F32),
             jax.ShapeDtypeStruct((8, C), F32),
         ],
         scratch_shapes=[
             pltpu.VMEM((n + 2 * HALO, C), BF),
+            pltpu.VMEM((C, n + 2 * HALO), BF),
+            pltpu.VMEM((n, C), BF),
             pltpu.VMEM((owners, e_rows, 128), BF),
-            pltpu.VMEM((27, C), F32),
-            pltpu.VMEM((3, 8, C), F32),
+            pltpu.VMEM((27, C, 128), F32),
+            pltpu.VMEM((3, C, 128), F32),
             pltpu.VMEM((padded, 128), BF),
-            pltpu.SemaphoreType.DMA((2,)),
+            pltpu.SemaphoreType.DMA((3,)),
             pltpu.SemaphoreType.DMA((2,)),
             pltpu.SemaphoreType.DMA((2,)),
             pltpu.SemaphoreType.DMA((owners, 8 + count // 8)),
@@ -318,19 +388,19 @@
         compiler_params=pltpu.CompilerParams(
             vmem_limit_bytes=60 * 1024 * 1024, collective_id=0, has_side_effects=True
         ),
-    )(near, nodes, mask3, master)
-
-
-def conv_back_kernel(count, cores, owners, near_hbm, first_hbm, conv_hbm, x_ref, mask_ref, sums_ref, stats_ref, rows_ref,
-                     grads_ref, master_ref, m_ref, v_ref,
-                     grad_ref, master_out, m_out, v_out, low_out, bias_out,
-                     near, ext, delta, conv, weight, dw, kept, r1, r2, r3, r4, local_sem, halo_send, halo_recv, g_send, g_recv,
-                     slots, s_send, s_recv, wslots, w_send, w_recv, total_s, early_s):
+    )(near, nodes, dy, mask3, master)
+
+
+def conv_back_kernel(count, cores, owners, near_hbm, first_hbm, conv_hbm, x_ref, mask_ref, sums_ref, stats_ref,
+                     rows_ref, grads_ref,
+                     grad_ref, total_s, bias_out,
+                     near, ext, delta, conv, weight, dw, kept, r1, r2, r3, r4, local_sem, halo_send, halo_recv, g_send,
+                     g_recv, slots, s_send, s_recv, w_own, w_slots, w_high, w_sem, w_recv, w_recv_high, early_s):
     step = pl.program_id(0)
     steps = pl.num_programs(0)
     block = (step + 1) % steps
     n = first_hbm.shape[0]
-    shard = master_ref.shape[0]
+    shard = total_s.shape[0]
     padded = grads_ref.shape[-2]
     half = padded // 2
     me = my_place()
@@ -345,12 +415,12 @@
     locals_ = [
         pltpu.make_async_copy(first_hbm, delta, local_sem.at[0]),
         pltpu.make_async_copy(conv_hbm, conv, local_sem.at[1]),
-        pltpu.make_async_copy(near_hbm, near.at[pl.ds(HALO, n)], local_sem.at[2]),
+        pltpu.make_async_copy(near_hbm, near.at[:, pl.ds(BLK, n)], local_sem.at[2]),
         pltpu.make_async_copy(grads_ref.at[:, :, :, g], kept, local_sem.at[3]),
     ]
     near_halo = [
-        send(near_hbm.at[pl.ds(0, HALO)], near.at[pl.ds(HALO + n, HALO)], halo_send.at[0], halo_recv.at[0], left, cores),
-        send(near_hbm.at[pl.ds(n - HALO, HALO)], near.at[pl.ds(0, HALO)], halo_send.at[1], halo_recv.at[1], right, cores),
+        send(near_hbm.at[:, pl.ds(0, BLK)], near.at[:, pl.ds(BLK + n, BLK)], halo_send.at[0], halo_recv.at[0], left, cores),
+        send(near_hbm.at[:, pl.ds(n - BLK, BLK)], near.at[:, pl.ds(0, BLK)], halo_send.at[1], halo_recv.at[1], right, cores),
     ]
     delta_halo = [
         send(ext.at[pl.ds(HALO, HALO)], ext.at[pl.ds(HALO + n, HALO)], halo_send.at[2], halo_recv.at[2], left, cores),
@@ -427,7 +497,7 @@
             for k in range(size - 1):
                 value = value + r4[bases[s] + k * stride + i].astype(F32)
             if s == nh - 1:
-                total_s[...] = value
+                total_s[...] = value[:shard]
             else:
                 kept[start + i, y, x] = value.astype(BF)
             return 0
@@ -435,7 +505,7 @@
 
     plan = [(core_copies, core_add), (quad_copies_0, quad_add_0), (quad_copies_1, quad_add_1)]
     plan += [(functools.partial(high_copies, s), functools.partial(high_add, s)) for s in range(nh)]
-    cuts = [4, 13, 18] + [18 + 10 * (s + 1) // nh for s in range(nh)]
+    cuts = CUTS_SCATTER(nh)
 
     @pl.when(step == 0)
     def _():
@@ -446,14 +516,13 @@
         partners += [(high + h) % (count // 8) * 8 + low for h in range(1, count // 8)]
         partners += [place for _, place in others(me, 1, 8)[1]]
         greet(partners, cores)
-        mine = jnp.concatenate([jnp.sum(sums_ref[i], axis=0, keepdims=True) for i in range(3)] + [jnp.zeros((5, C), F32)], axis=0)
-        total = all_sum(mine, me, count, cores, slots, s_send, s_recv)
-        for copy in plan[0][0]():
-            copy.start()
-        for copy in near_halo:
-            copy.start()
+        def beside(s):
+            if s == 0:
+                for copy in plan[0][0]() + near_halo:
+                    copy.start()
+        total = all_sum(sums_ref[...], me, count, cores, slots, s_send, s_recv, beside)
         gain_total, shift_total = total[0:1], total[1:2]
-        bias_out[...] = total[2:3]
+        bias_out[...] = jnp.concatenate([total[2:3, i * 128 : (i + 1) * 128] for i in range(3)], axis=0)
         early_s[...] = jnp.zeros_like(early_s)
         for i in range(3):
             early_s[i : i + 1, :] = gain_total[:, i * 128 : (i + 1) * 128]
@@ -478,11 +547,11 @@
             at = pl.ds(pl.multiple_of(i * BLK, BLK), BLK)
             live = jnp.broadcast_to(mask_ref[i].astype(F32), (BLK, BLK)).T
             live = jnp.concatenate([live] * 3, axis=1)
-            value = delta[at, :] * a + live * (b + c * conv[at, :])
+            value = delta[at, :] * a + live * (b + c * conv[at, :].astype(F32))
             ext[pl.ds(pl.multiple_of(i * BLK + HALO, HALO), BLK), :] = value.astype(BF)
             return 0
 
-        lax.fori_loop(0, steps, body, 0)
+        lax.fori_loop(0, n // BLK, body, 0)
         for copy in delta_halo:
             copy.start()
 
@@ -501,60 +570,100 @@
         for copy in near_halo + delta_halo:
             copy.wait()
 
-    start = pl.multiple_of(block * BLK, BLK)
-    window = ext[pl.ds(start, 2 * BLK), :]
-    near_w = near[pl.ds(start, 2 * BLK), :]
-    place = near_w + lax.broadcasted_iota(jnp.int32, near_w.shape, 0) - BLK
-    place = jnp.where(near_w < 0, -1, place).astype(F32)
-    place = jnp.concatenate([place, jnp.zeros((2 * BLK, 128 - 27), F32)], axis=1).T.astype(BF)
+    start = pl.multiple_of(block * TB, TB)
     target = lax.broadcasted_iota(jnp.int32, (BLK, 2 * BLK), 0).astype(F32).astype(BF)
     one, zero = jnp.ones((), BF), jnp.zeros((), BF)
-    nodes = x_ref[...].astype(F32)
-    total = delta[pl.ds(start, BLK), :]
-    for j in range(27):
-        pick = jnp.where(place[j : j + 1, :] == target, one, zero)
-        come = nn(pick, window)
-        total += come * weight[j : j + 1, :]
-        dw[j] += jnp.sum((come * nodes).reshape(BLK // 8, 8, C), axis=0)
-    grad_ref[...] = total
+    lane = lax.broadcasted_iota(jnp.int32, (27, 2 * BLK), 1) - BLK
+    places, totals, picks, comes, xs = {}, {}, {}, {}, {}
+    for b in range(TB // BLK):
+        near_w = near[:, pl.ds(start + b * BLK, 3 * BLK)][:, HALO : HALO + 2 * BLK]
+        places[b] = jnp.where(near_w < 0, -1, near_w + lane).astype(F32).astype(BF)
+
+    def pick(task):
+        b, q = task
+        picks[task] = jnp.concatenate(
+            [jnp.where(places[b][j : j + 1, :] == target, one, zero) for j in range(3 * q, 3 * q + 3)], axis=0
+        )
+
+    def multiply(task):
+        b, q = task
+        comes[task] = nn(picks.pop(task), ext[pl.ds(start + b * BLK, 2 * BLK), :])
+
+    def add(task):
+        b, q = task
+        come = comes.pop(task)
+        if q == 0:
+            xs[b] = x_ref[b * BLK : (b + 1) * BLK, :].astype(F32)
+            totals[b] = delta[pl.ds(start + b * BLK, BLK), :]
+        for i in range(3):
+            j, part = 3 * q + i, come[i * BLK : (i + 1) * BLK]
+            totals[b] = totals[b] + part * weight[j : j + 1, :]
+            dw[j] += jnp.sum((part * xs[b]).reshape(BLK // 8, 8, C), axis=0)
+        if q == 8:
+            grad_ref[b * BLK : (b + 1) * BLK, :] = totals.pop(b)
+
+    skew([pick, multiply, add], [(b, q) for b in range(TB // BLK) for q in range(9)])
 
     @pl.when(step == steps - 1)
     def _():
-        mine = jnp.sum(dw[...], axis=1)
-        mine = jnp.concatenate([mine, jnp.zeros((5, C), F32)], axis=0)
-        dws = all_sum(mine, me, count, cores, wslots, w_send, w_recv)
-        for k in range(3):
-            early_s[pl.ds(ROW_CONV + k, 27, stride=3), :] = dws[:27, k * 128 : (k + 1) * 128]
+        w_own[0:27] = jnp.sum(dw[...], axis=1)
+        w_own[27:32] = jnp.zeros((5, C), F32)
+        to_first = send(w_own, w_slots.at[low], w_sem.at[0], w_recv.at[low], me - low, cores)
+
+        @pl.when(low != 0)
+        def _():
+            to_first.start()
+            to_first.wait_send()
+
+        @pl.when(low == 0)
+        def _():
+            for k in range(1, 8):
+                send(w_own, w_slots.at[k], w_sem.at[0], w_recv.at[k], me + k, cores).wait_recv()
+            w_own[...] = w_own[...] + sum(w_slots[k] for k in range(1, 8))
+
+            @pl.when(high != 0)
+            def _():
+                up = send(w_own, w_high.at[high], w_sem.at[0], w_recv_high.at[high], 0, cores)
+                up.start()
+                up.wait_send()
+
+            @pl.when(high == 0)
+            def _():
+                for h in range(1, count // 8):
+                    send(w_own, w_high.at[h], w_sem.at[0], w_recv_high.at[h], h * 8, cores).wait_recv()
+                w_own[...] = w_own[...] + sum(w_high[h] for h in range(1, count // 8))
+                out = [send(w_own, w_high.at[0], w_sem.at[o], w_recv_high.at[0], o, cores) for o in range(1, owners)]
+                for copy in out:
+                    copy.start()
+                for copy in out:
+                    copy.wait_send()
+
         for o in range(owners):
             @pl.when(me == o)
-            def _():
+            def _(o=o):
+                if o == 0:
+                    sums = w_own[...]
+                else:
+                    send(w_own, w_high.at[0], w_sem.at[0], w_recv_high.at[0], 0, cores).wait_recv()
+                    sums = w_high[0]
+                for k in range(3):
+                    early_s[pl.ds(ROW_CONV + k, 27, stride=3), :] = sums[:27, k * 128 : (k + 1) * 128]
                 rows = min(shard, early_s.shape[0] - o * shard)
                 total_s[0:rows, :] += early_s[o * shard : o * shard + rows, :]
-        grad = total_s[0:shard, :]
-        row = lax.broadcasted_iota(jnp.int32, (shard, 128), 0) + me * shard
-        rate = jnp.where(row < ROW_CONV, 0.2, 0.03)
-        old = master_ref[...]
-        new_m = 0.9 * m_ref[...] + 0.1 * grad
-        new_v = 0.95 * v_ref[...] + 0.05 * grad * grad
-        first_hat = new_m / (1.0 - 0.9**STEP)
-        second_hat = new_v / (1.0 - 0.95**STEP)
-        new = old - rate * (first_hat / (jnp.sqrt(second_hat) + 1e-08) + 0.01 * old)
-        master_out[...] = new
-        m_out[...] = new_m
-        v_out[...] = new_v
-        low_out[...] = new.astype(BF)
-
-
-def convolve_back(near, delta, conv, nodes, mask3, sums, stats, rows, grads, master, m, v, count, cores):
+
+
+def CUTS_SCATTER(nh):
+    return [1, 3, 4] + [4 + 3 * (s + 1) // nh for s in range(nh)]
+
+
+def convolve_back(near, delta, conv, nodes, mask3, sums, stats, rows, grads, shard, count, cores):
     n = nodes.shape[0]
-    steps = n // BLK
-    shard = master.shape[0]
+    steps = n // TB
     padded = grads.shape[-2]
     highs = count // 8
     owners = -(-ROW_JOINT // shard)
-    turned = lambda i: ((i + 1) % steps, 0)
+    turned = pl.BlockSpec((TB, C), lambda i: ((i + 1) % steps, 0))
     anywhere = pl.BlockSpec(memory_space=pl.ANY)
-    flat = whole(shard, 128)
     r4_rows = sum((size - 1) * stride for stride, size in stages_of(highs))
     return pl.pallas_call(
         functools.partial(conv_back_kernel, count, cores, owners),
@@ -563,25 +672,24 @@
             anywhere,
             anywhere,
             anywhere,
-            pl.BlockSpec((BLK, C), turned),
+            turned,
             whole(*mask3.shape),
             whole(*sums.shape),
             whole(*stats.shape),
             whole(*rows.shape),
             anywhere,
-            flat,
-            flat,
-            flat,
         ],
-        out_specs=[pl.BlockSpec((BLK, C), turned), flat, flat, flat, flat, whole(1, C)],
-        out_shape=[jax.ShapeDtypeStruct((n, C), F32)]
-        + [jax.ShapeDtypeStruct((shard, 128), d) for d in (F32, F32, F32, BF)]
-        + [jax.ShapeDtypeStruct((1, C), F32)],
+        out_specs=[turned, whole(shard, 128), whole(3, 128)],
+        out_shape=[
+            jax.ShapeDtypeStruct((n, C), F32),
+            jax.ShapeDtypeStruct((shard, 128), F32),
+            jax.ShapeDtypeStruct((3, 128), F32),
+        ],
         scratch_shapes=[
-            pltpu.VMEM((n + 2 * HALO, 27), jnp.int32),
+            pltpu.VMEM((27, n + 2 * BLK), jnp.int32),
             pltpu.VMEM((n + 2 * HALO, C), BF),
             pltpu.VMEM((n, C), F32),
-            pltpu.VMEM((n, C), F32),
+            pltpu.VMEM((n, C), BF),
             pltpu.VMEM((27, C), F32),
             pltpu.VMEM((27, 8, C), F32),
             pltpu.VMEM((highs, 2, 2, padded, 128), BF),
@@ -596,12 +704,19 @@
             pltpu.SemaphoreType.DMA((3 + len(stages_of(highs)), 8)),
         ]
         + sum_scratch(count, 8, C)
-        + sum_scratch(count, 32, C)
-        + [pltpu.VMEM((padded, 128), F32), pltpu.VMEM((round_up(ROW_JOINT, 8), 128), F32)],
+        + [
+            pltpu.VMEM((32, C), F32),
+            pltpu.VMEM((8, 32, C), F32),
+            pltpu.VMEM((highs, 32, C), F32),
+            pltpu.SemaphoreType.DMA((max(owners, 1),)),
+            pltpu.SemaphoreType.DMA((8,)),
+            pltpu.SemaphoreType.DMA((highs,)),
+            pltpu.VMEM((round_up(ROW_JOINT, 8), 128), F32),
+        ],
         compiler_params=pltpu.CompilerParams(
             vmem_limit_bytes=60 * 1024 * 1024, collective_id=1, has_side_effects=True
         ),
-    )(near, delta, conv, nodes, mask3, sums, stats, rows, grads, master, m, v)
+    )(near, delta, conv, nodes, mask3, sums, stats, rows, grads)
 
 
 def prepare(stats, rows, gathered, shard, flat, norm, spread, mats):
@@ -623,21 +738,21 @@
     average = stats[0:1, :] / live_total
     variance = stats[1:2, :] / live_total - average * average
     inverse = lax.rsqrt(variance + EPS)
-    norm[0:1, :] = inverse * gain
-    norm[1:2, :] = shift - average * inverse * gain
-    norm[2:3, :] = inverse
-    norm[3:4, :] = average * inverse
-
-
-def mid_kernel(shard,conv_ref,nodes_ref,dy_ref,mask_ref,stats_ref,rows_ref,gathered_ref,
+    norm[0] = along_sublanes(inverse * gain)
+    norm[1] = along_sublanes(shift - average * inverse * gain)
+    norm[2] = along_sublanes(inverse)
+    norm[3] = along_sublanes(average * inverse)
+
+
+def mid_kernel(shard,conv_ref,nodes_ref,dyt_ref,mask_ref,stats_ref,rows_ref,gathered_ref,
     out_ref,dfirst_ref,grads_ref,bns_ref,
     flat_ref,bn_ref,vb_ref,wj_ref,wjt_ref,wo_ref,wot_ref,wh_ref,wht_ref,wf_ref,wft_ref,
-    gj_ref,go_ref,gh_ref,gf_ref,vs_ref,hb_ref,first_s,second_s,qkv_s,kn_s,vn_s,a_s,o_s,ob_s,do_s,dqkv_s,x_s,acc_s,dx_s):
+    gj_ref,go_ref,gh_ref,gf_ref,vs_ref,hb_ref,first_s,second_s,qkv_s,kn_s,vn_s,a_s,o_s,ob_s,inv_s,dob_s,dqkv_s,x_s,acc_s,dx_s):
     step=pl.program_id(0)
     rep=T//128
     @pl.when(step==0)
     def _():
-        for r in (gj_ref,go_ref,gh_ref,gf_ref,vs_ref,hb_ref,bns_ref): r[...]=jnp.zeros_like(r)
+        for r in (gj_ref,go_ref,gh_ref,gf_ref,vs_ref,hb_ref): r[...]=jnp.zeros_like(r)
         prepare(stats_ref,rows_ref,gathered_ref,shard,flat_ref,bn_ref,vb_ref,
             ((ROW_JOINT,wj_ref,wjt_ref),(ROW_OUT,wo_ref,wot_ref),(ROW_HIDDEN,wh_ref,wht_ref),(ROW_FINAL,wf_ref,wft_ref)))
     def col(i,n=C):
@@ -647,13 +762,9 @@
         r=x[:,:128]
         for k in range(1,rep): r=r+x[:,128*k:128*(k+1)]
         return r
-    scale_a=bn_ref[0:1,:]; shift_b=bn_ref[1:2,:]; r_row=bn_ref[2:3,:]; ar_row=bn_ref[3:4,:]
-    first=nodes_ref[...].astype(F32)+(conv_ref[...]*scale_a+shift_b)
-    firstT=first.T
+    def wide(v): return jnp.concatenate([v]*rep,axis=1)
+    firstT=nodes_ref[...].astype(F32)+(conv_ref[...]*wide(bn_ref[0])+wide(bn_ref[1]))
     first_s[...]=firstT
-    dy=dy_ref[...]
-    dyT32=dy.astype(F32).T
-    do_s[...]=dyT32
     def ln(x):
         m=jnp.mean(x,axis=0,keepdims=True); c=x-m
         rs=lax.rsqrt(jnp.mean(c*c,axis=0,keepdims=True)+EPS)
@@ -661,59 +772,50 @@
     xh1,rs1=ln(firstT)
     x1=(xh1*col(2)+col(3)).astype(BF)
     x_s[0]=x1
-    q=nn(wjt_ref[0:C,:],x1)+col(4)
+    scale=HD**-0.5
+    c2=scale*1.4426950408889634
+    live_row=jnp.concatenate([mask_ref[b].astype(F32) for b in range(rep)],axis=1)
+    q=(nn(wjt_ref[0:C,:],x1)+col(4))*c2
     qkv_s[0:C,:]=q.astype(BF)
-    k=nn(wjt_ref[C:2*C,:],x1)
+    k=nn(wjt_ref[C:2*C,:],x1)*live_row
     qkv_s[C:2*C,:]=k.astype(BF)
     kn_s[...]=k.T.astype(BF)
     v=nn(wjt_ref[2*C:,:],x1)+col(5)
     qkv_s[2*C:,:]=v.astype(BF)
     vn_s[...]=v.T.astype(BF)
-    scale=HD**-0.5
-    c2=scale*1.4426950408889634
     pi=lax.broadcasted_iota(jnp.int32,(BLK,BLK),0); qi=lax.broadcasted_iota(jnp.int32,(BLK,BLK),1)
-    same=(pi&3)==(qi&3)
-    lives=[]
-    def bd(ref,row,blk):
-        parts=[]
-        z=jnp.zeros((HD,BLK),BF)
-        for i in range(2):
-            pass
-        return parts
-    z=jnp.zeros((HD,BLK),BF)
-    masks=[]
+    wq=jnp.where(pi<4,jnp.where((qi&3)==pi,0.0,-1e30),jnp.where(pi==4,-1e9*1.4426950408889634,0.0)).astype(BF)
+    wq=jnp.concatenate([wq,wq],axis=1)
+    wps=[]
     for b in range(rep):
         lv=jnp.broadcast_to(mask_ref[b].astype(F32),(BLK,BLK)).T
-        live=(lv>0.5)&same
-        bias=jnp.where(same,-1e9/scale,-1e30)
-        masks.append((jnp.concatenate([live,live],axis=1),jnp.concatenate([bias,bias],axis=1)))
-    def ex(ref,g,i,cs):
-        qh=ref[g*128+i*32:g*128+(i+1)*32,cs]
-        return jnp.concatenate([qh if t==i else z for t in range(4)],axis=0)
+        wps.append(jnp.where(qi<4,jnp.where((pi&3)==qi,1.0,0.0),jnp.where(qi==4,1.0-lv,0.0)).astype(BF))
+    z=jnp.zeros((HD,BLK),BF)
+    def ex(part,i):
+        return jnp.concatenate([part if t==i else z for t in range(4)],axis=0)
     tasks=[(b,g,hp*2) for b in range(rep) for g in range(3) for hp in range(2)]
     S={};A={}
     def f_s(t):
         b,g,h0=t; cs=slice(b*BLK,(b+1)*BLK)
-        S[t]=nn(kn_s[cs,g*128:(g+1)*128],jnp.concatenate([ex(qkv_s,g,h0,cs),ex(qkv_s,g,h0+1,cs)],axis=1))
+        qs=[ex(qkv_s[g*128+i*32:g*128+(i+1)*32,cs],i) for i in (h0,h0+1)]
+        S[t]=nn(jnp.concatenate([kn_s[cs,g*128:(g+1)*128],wps[b]],axis=1),jnp.concatenate([jnp.concatenate(qs,axis=1),wq],axis=0))
     def f_a(t):
         b,g,h0=t; cs=slice(b*BLK,(b+1)*BLK)
-        s=jnp.where(masks[b][0],S.pop(t),masks[b][1])
+        s=S.pop(t)
         m=jnp.max(s,axis=0,keepdims=True)
-        e=jnp.exp2((s-m)*c2)
-        l=jnp.sum(e,axis=0,keepdims=True)
-        a=(e*(1.0/l)).astype(BF)
-        for i in range(2): a_s[g*4+h0+i,:,cs]=a[:,i*128:(i+1)*128]
-        A[t]=a
+        e=jnp.exp2(s-m)
+        inv=1.0/jnp.sum(e,axis=0,keepdims=True)
+        a=e.astype(BF)
+        for i in range(2):
+            a_s[g*4+h0+i,:,cs]=a[:,i*128:(i+1)*128]
+            inv_s[g*4+h0+i:g*4+h0+i+1,cs]=inv[:,i*128:(i+1)*128]
+        A[t]=(a,inv)
     def f_o(t):
         b,g,h0=t; cs=slice(b*BLK,(b+1)*BLK)
-        a=A.pop(t)
+        a,inv=A.pop(t)
         for i in range(2):
             h=g*4+h0+i
-            o_s[h*32:(h+1)*32,cs]=nn(qkv_s[2*C+h*32:2*C+(h+1)*32,cs],a[:,i*128:(i+1)*128])
-    def skew(stages,tasks):
-        for i in range(len(tasks)+len(stages)-1):
-            for k,st in enumerate(stages):
-                if 0<=i-k<len(tasks): st(tasks[i-k])
+            o_s[h*32:(h+1)*32,cs]=nn(qkv_s[2*C+h*32:2*C+(h+1)*32,cs],a[:,i*128:(i+1)*128])*inv[:,i*128:(i+1)*128]
     skew([f_s,f_a,f_o],tasks)
     ob=o_s[...].astype(BF)
     ob_s[...]=ob
@@ -722,7 +824,7 @@
     xh2,rs2=ln(secondT)
     x2=(xh2*col(7)+col(8)).astype(BF)
     x_s[1]=x2
-    dyTb=do_s[...].astype(BF)
+    dyTb=dyt_ref[...]
     FC=512
     c0=0.7978845608028654; c1=0.044715
     HH={};PP={}
@@ -752,7 +854,7 @@
             acc_s[...]=o; dx_s[...]=d
         else:
             acc_s[...]+=o; dx_s[...]+=d
-        gf_ref[fs,:]+=nn(act,dy)
+        gf_ref[fs,:]+=nt(act,dyTb)
         gh_ref[:,fs]+=nt(x2,dpb)
     skew([g_h,g_g,g_o],list(range(F//FC)))
     outT=second_s[...]+(acc_s[...]+col(15-2))
@@ -765,52 +867,52 @@
         m1=jnp.mean(dh,axis=0,keepdims=True)
         m2=jnp.mean(dh*xh,axis=0,keepdims=True)
         return rs*(dh-m1-xh*m2)
-    dsec=do_s[...]+ln_back(second_s[...],dx_s[...],col(7),0)
+    dsec=dyt_ref[...].astype(F32)+ln_back(second_s[...],dx_s[...],col(7),0)
     second_s[...]=dsec
     dbr=dsec.astype(BF)
     vs_ref[2]+=fold(dbr.astype(F32))
     go_ref[...]+=nt(ob_s[...],dbr)
     dat=nn(wo_ref[...],dbr)
-    do_s[...]=dat
-    dob=dat.astype(BF)
+    for h in range(HEADS):
+        hs=slice(h*32,(h+1)*32)
+        dob_s[hs,:]=(dat[hs,:]*inv_s[h:h+1,:]).astype(BF)
     D={};G={}
     def b_d(t):
         b,g,h0=t; cs=slice(b*BLK,(b+1)*BLK)
-        D[t]=nn(vn_s[cs,g*128:(g+1)*128],jnp.concatenate([ex(dob,g,h0,cs),ex(dob,g,h0+1,cs)],axis=1))
+        ds=[ex(dob_s[g*128+i*32:g*128+(i+1)*32,cs],i) for i in (h0,h0+1)]
+        D[t]=nn(vn_s[cs,g*128:(g+1)*128],jnp.concatenate(ds,axis=1))
     def b_s(t):
         b,g,h0=t; cs=slice(b*BLK,(b+1)*BLK)
         dA=D.pop(t)
         out=[]
         for i in range(2):
             h=g*4+h0+i; hs=slice(h*32,(h+1)*32)
-            delta=jnp.sum(dob[hs,cs].astype(F32)*o_s[hs,cs],axis=0,keepdims=True)
-            out.append((a_s[h,:,cs].astype(F32)*(dA[:,i*128:(i+1)*128]-delta)).astype(BF))
+            delta=jnp.sum(dob_s[hs,cs].astype(F32)*o_s[hs,cs],axis=0,keepdims=True)
+            out.append(a_s[h,:,cs]*(dA[:,i*128:(i+1)*128]-delta).astype(BF))
         G[t]=out
     def b_q(t):
         b,g,h0=t; cs=slice(b*BLK,(b+1)*BLK)
-        lrow=mask_ref[b].astype(F32)
+        lrow=live_row[:,cs]
         out=G.pop(t)
         for i in range(2):
             h=g*4+h0+i; hs=slice(h*32,(h+1)*32); ds=out[i]
-            kh=(qkv_s[C+h*32:C+(h+1)*32,cs].astype(F32)*lrow).astype(BF)
-            dqkv_s[h*32:(h+1)*32,cs]=(nn(kh,ds)*scale).astype(BF)
-            dqkv_s[C+h*32:C+(h+1)*32,cs]=(nt(qkv_s[hs,cs],ds)*(lrow*scale)).astype(BF)
-            dqkv_s[2*C+h*32:2*C+(h+1)*32,cs]=nt(dob[hs,cs],a_s[h,:,cs]).astype(BF)
+            dqkv_s[h*32:(h+1)*32,cs]=(nn(qkv_s[C+h*32:C+(h+1)*32,cs],ds)*scale).astype(BF)
+            dqkv_s[C+h*32:C+(h+1)*32,cs]=(nt(qkv_s[hs,cs],ds)*(lrow*(scale/c2))).astype(BF)
+            dqkv_s[2*C+h*32:2*C+(h+1)*32,cs]=nt(dob_s[hs,cs],a_s[h,:,cs]).astype(BF)
     skew([b_d,b_s,b_q],tasks)
     vs_ref[3]+=fold(dqkv_s[0:C,:].astype(F32))
     vs_ref[4]+=fold(dqkv_s[2*C:,:].astype(F32))
     gj_ref[...]+=nt(x_s[0],dqkv_s[...])
     dx1=nn(wj_ref[...],dqkv_s[...])
     dfT=second_s[...]+ln_back(first_s[...],dx1,col(2),5)
-    df=dfT.T
-    dfirst_ref[...]=df
-    cen=conv_ref[...]*r_row-ar_row
-    bns_ref[0]+=jnp.sum((df*cen).reshape(T//8,8,C),axis=0)
-    bns_ref[1]+=jnp.sum(df.reshape(T//8,8,C),axis=0)
-    bns_ref[2]+=jnp.sum(dy.astype(F32).reshape(T//8,8,C),axis=0)
+    dfirst_ref[...]=dfT.T
+    vs_ref[7]+=fold(dfT*(conv_ref[...]*wide(bn_ref[2])-wide(bn_ref[3])))
+    vs_ref[8]+=fold(dfT)
+    vs_ref[9]+=fold(dyt_ref[...].astype(F32))
     @pl.when(step==pl.num_programs(0)-1)
     def _():
         flat_ref[...]=jnp.zeros_like(flat_ref)
+        bns_ref[...]=jnp.concatenate([lane_sums(vs_ref[i]) for i in (7,8,9)]+[jnp.zeros((5,C),F32)],axis=0)
         for vi,row in ((0,21),(1,24),(2,18),(3,12),(4,15),(5,6),(6,9)):
             for i in range(3):
                 flat_ref[pl.ds(row+i,1),:]=jnp.sum(vs_ref[vi,i*128:(i+1)*128,:].T,axis=0,keepdims=True)
@@ -829,14 +931,15 @@
 
 
 def middle(conv,nodes,dy,mask3,stats,rows,gathered,shard):
-    n=conv.shape[0]
-    row=rows_of(C,T)
+    n=conv.shape[1]
+    across=pl.BlockSpec((C,T),lambda i:(0,i))
+    down=rows_of(C,T)
     flat_rows=gathered.shape[0]*8*shard
-    in_specs=[row,row,row,pl.BlockSpec((T//128,1,128),lambda i:(i,0,0)),whole(*stats.shape),whole(*rows.shape),whole(*gathered.shape)]
-    outs=[((n,C),BF,row),((n,C),F32,row),(gathered.shape,BF,whole(*gathered.shape)),((3,8,C),F32,whole(3,8,C))]
+    in_specs=[across,across,across,pl.BlockSpec((T//128,1,128),lambda i:(i,0,0)),whole(*stats.shape),whole(*rows.shape),whole(*gathered.shape)]
+    outs=[((n,C),BF,down),((n,C),F32,down),(gathered.shape,BF,whole(*gathered.shape)),((8,C),F32,whole(8,C))]
     mats=[]
     for shape in ((C,3*C),(C,C),(C,F),(F,C)): mats+=[(shape,BF),(shape[::-1],BF)]
-    scr=[pltpu.VMEM(s,d) for s,d in [((flat_rows,128),F32),((8,C),F32),((ROW_CONV*128,128),F32)]+mats+[((C,3*C),F32),((C,C),F32),((C,F),F32),((F,C),F32),((7,C,128),F32),((F,128),F32),((C,T),F32),((C,T),F32),((3*C,T),BF),((T,C),BF),((T,C),BF),((HEADS,BLK,T),BF),((C,T),F32),((C,T),BF),((C,T),F32),((3*C,T),BF),((2,C,T),BF),((C,T),F32),((C,T),F32)]]
+    scr=[pltpu.VMEM(s,d) for s,d in [((flat_rows,128),F32),((4,C,128),F32),((ROW_CONV*128,128),F32)]+mats+[((C,3*C),F32),((C,C),F32),((C,F),F32),((F,C),F32),((10,C,128),F32),((F,128),F32),((C,T),F32),((C,T),F32),((3*C,T),BF),((T,C),BF),((T,C),BF),((HEADS,BLK,T),BF),((C,T),F32),((C,T),BF),((16,T),F32),((C,T),BF),((3*C,T),BF),((2,C,T),BF),((C,T),F32),((C,T),F32)]]
     return pl.pallas_call(functools.partial(mid_kernel,shard),grid=(n//T,),in_specs=in_specs,out_specs=[o[2] for o in outs],
       out_shape=[jax.ShapeDtypeStruct(o[0],o[1]) for o in outs],scratch_shapes=scr,
       compiler_params=VMEM)(conv,nodes,dy,mask3,stats,rows,gathered)
@@ -846,22 +949,30 @@
     n = nodes_in.shape[0]
     count, cores = lax.axis_size(AXES), lax.axis_size("grp")
     shard = master.shape[0] // 128
-    flat = [a.reshape(shard, 128) for a in (master, first_moment, second_moment)]
     mask3 = node_mask.reshape(n // 128, 1, 128)
-    convolved, gathered, first_rows, stats = convolve(neighbours, nodes_in, mask3, flat[0], count, cores)
-    output, delta_first, grads, norm_sums = middle(
-        convolved, nodes_in, out_grad, mask3, stats, first_rows, gathered, shard
+    near = neighbours.T
+    conv_t, conv, nodes_t, dy_t, gathered, first_rows, stats = convolve(
+        near, nodes_in, out_grad, mask3, master.reshape(shard, 128), count, cores
     )
-    node_grad, new_master, new_first, new_second, new_low, bias_total = convolve_back(
-        neighbours, delta_first, convolved, nodes_in, mask3, norm_sums, stats, first_rows, grads, *flat, count, cores
+    output, delta_first, grads, norm_sums = middle(conv_t, nodes_t, dy_t, mask3, stats, first_rows, gathered, shard)
+    node_grad, shard_delta, bias_total = convolve_back(
+        near, delta_first, conv, nodes_in, mask3, norm_sums, stats, first_rows, grads, shard, count, cores
     )
+    shard_delta = shard_delta.reshape(-1)
+    position = lax.axis_index(AXES) * master.shape[0] + lax.iota(jnp.int32, master.shape[0])
+    step_rate = jnp.where(position < 10 * C + F, 0.2, 0.03)
+    new_first = 0.9 * first_moment + 0.1 * shard_delta
+    new_second = 0.95 * second_moment + 0.05 * shard_delta * shard_delta
+    first_hat = new_first / (1.0 - 0.9**STEP)
+    second_hat = new_second / (1.0 - 0.95**STEP)
+    new_master = master - step_rate * (first_hat / (jnp.sqrt(second_hat) + 1e-08) + 0.01 * master)
     return (
         output,
         node_grad,
-        new_master.reshape(-1),
-        new_first.reshape(-1),
-        new_second.reshape(-1),
-        new_low.reshape(-1),
+        new_master,
+        new_first,
+        new_second,
+        new_master.astype(BF),
         bias_total.reshape(-1),
     )
 

time: 273 us -> 240 us (0.88)
  Pallas kernels: 259 us -> 231 us
  local copies, waits for them, and re-layouts: 11.7 us -> 6.49 us
    pallas_call x1, Pallas kernels: 73.3 us -> 58.3 us  [convolve(): pl.pallas_call(functools.partial(conv_kernel, count, cores, owners), grid...]
    pallas_call x1, Pallas kernels: 73.7 us -> 66.9 us  [convolve_back(): pl.pallas_call(functools.partial(conv_back_kernel, count, cores, owners),...]
    pallas_call x1, Pallas kernels: 112 us -> 106 us  [middle(): pl.pallas_call(functools.partial(mid_kernel, shard), grid=(n // T,), in_s...]
    unnamed x14 -> x10, local copies, waits for them, and re-layouts: 11.7 us -> 6.49 us
where the time goes in v4:
time: 240 us
  Pallas kernels  231 us (96%)
  local copies, waits for them, and re-layouts  6.49 us (3%)
    pallas_call x1, Pallas kernels, middle(): pl.pallas_call(functools.partial(mid_kernel, shard), grid=(n // T,), in_s...  106 us
    pallas_call x1, Pallas kernels, convolve_back(): pl.pallas_call(functools.partial(conv_back_kernel, count, cores, owners),...  66.9 us
    pallas_call x1, Pallas kernels, convolve(): pl.pallas_call(functools.partial(conv_kernel, count, cores, owners), grid...  58.3 us
    unnamed x10, local copies, waits for them, and re-layouts  6.49 us

profile of v4, /device:TPU:0, one launch (start us, length us, event | category | flops | bytes accessed | tf_op | source)
XLA Modules:
  0.0 240.3 jit_solution(4636485116118300879)
XLA Ops:
  0.6 58.3 %shard_map.126 = (f32[384,4096]{1,0:T(8,128)}, bf16[4096,384]{1,0:T(8,128)(2,1)}, bf16[384,4096]{1,0:T(8,128)(2,1)}, bf16[384,4096]{1,0:T(8,128)(2,1)}, bf16[4,2...) custom-call(s32[27,4096]{1,0:T(8,128)} %bitcast.11, bf16[4096,384]{1,0:T(8,128)(2,1)} %x_ref.1, ...), custom_call_target="tpu_custom_call" | custom-call | tf_op jit(solution)/shard_map/pallas_call | solution.py:351
  58.9 106.0 %shard_map.127 = (bf16[4096,384]{1,0:T(8,128)(2,1)}, f32[4096,384]{1,0:T(8,128)}, bf16[4,2,2,2,448,128]{5,4,3,2,1,0:T(8,128)(2,1)}, f32[8,384]{1,0:T(8,128)}) custom-call(f32[384,4096]{1,0:T(8,128)} %get-tuple-element.21.conv_ref, bf16[384,4096]{1,0:T(8,128)(2,1)} %get-tuple-element.22.nodes_ref, bf16[384,4096]{1,0:T(8,128)(2,1)} %get-tuple-element.23.dyt_ref, ...), custom_call_target="tpu_custom_call" | custom-call | tf_op jit(solution)/shard_map/pallas_call | solution.py:943
  164.9 0.0 copy-start
  164.9 0.0 copy-start.1
  164.9 0.0 copy-start.2
  164.9 66.9 %shard_map.128 = (f32[4096,384]{1,0:T(8,128)}, f32[436,128]{1,0:T(8,128)}, f32[3,128]{1,0:T(4,128)}) custom-call(s32[27,4096]{1,0:T(8,128)} %bitcast.12, f32[4096,384]{1,0:T(8,128)} %get-tuple-element.28.first_hbm, bf16[4096,384]{1,0:T(8,128)(2,1)} %get-tuple-element.29.conv_hbm, bf16[4096,384]{1,0:T(8,128)(2,1)} %x_ref.1, s32[32,1,128]{2,1,0:T(1,128)} %bitcast.16, ...), custom_call_target="tpu_custom_call" | custom-call | tf_op jit(solution)/shard_map/pallas_call | solution.py:668
  231.8 0.0 copy-done
  231.8 0.0 copy-done.1
  231.8 0.0 copy-done.2
  231.8 1.9 fusion.2
  233.8 0.0 copy-start.3
  233.8 5.9 %copy.16 = f32[4096,384]{1,0:T(8,128)} copy(f32[4096,384]{1,0:T(8,128)} %get-tuple-element.47) | data formatting | bytes 12582912
  239.7 0.0 copy-done.3
  239.7 0.6 copy.17
Async XLA Ops:
  164.9 66.9 %copy-start = (f32[55808]{0:T(1024)S(1)}, f32[55808]{0:T(1024)}, u32[]{:S(2)}) copy-start(f32[55808]{0:T(1024)} %param.11) | copy-start | bytes 669700
  164.9 66.9 %copy-start.1 = (f32[55808]{0:T(1024)S(1)}, f32[55808]{0:T(1024)}, u32[]{:S(2)}) copy-start(f32[55808]{0:T(1024)} %param.12) | copy-start | bytes 669700
  164.9 66.9 %copy-start.2 = (f32[55808]{0:T(1024)S(1)}, f32[55808]{0:T(1024)}, u32[]{:S(2)}) copy-start(f32[55808]{0:T(1024)} %param.13) | copy-start | bytes 669700
  233.8 5.9 %copy-start.3 = (f32[3,128]{1,0:T(4,128)S(1)}, f32[3,128]{1,0:T(4,128)}, u32[]{:S(2)}) copy-start(f32[3,128]{1,0:T(4,128)} %get-tuple-element.34) | copy-start | bytes 4612

commit v5 on v4

--- a/solution.py
+++ b/solution.py
@@ -67,7 +67,7 @@
 
 
 def CUTS_GATHER(nh):
-    return [1 + (s + 1) // nh for s in range(nh)] + [4, 7]
+    return [1] * nh + [3, 7]
 
 
 def round_up(value, step):
@@ -165,6 +165,11 @@
     keep = pltpu.make_async_copy(own_s, gathered_ref.at[high, y, x, g], local_sem.at[1])
     local_dy = pltpu.make_async_copy(dy_ref, dy_s, local_sem.at[2])
 
+    def turn_dy(k):
+        at = pl.ds(pl.multiple_of(k * BLK, BLK), BLK)
+        dyt_ref[:, at] = dy_s[at, :].T
+        return 0
+
     def turn(k):
         at = pl.ds(pl.multiple_of(k * BLK, BLK), BLK)
         extt[:, at] = ext[at, :].T
@@ -218,31 +223,27 @@
         partners += [(high + h) % (count // 8) * 8 + low for h in wide]
         partners += [place for _, place in others(me, 1, 8)[1]]
         greet(partners, cores)
+        early_copies = []
         for o in range(owners):
+            up = [send(early.at[o], early.at[o], e_send.at[o, 8 + h], e_recv.at[o, 0], h * 8 + o, cores) for h in wide]
+            out = [
+                send(early.at[o], early.at[o], e_send.at[o, k], e_recv.at[o, 1], me + k - o, cores)
+                for k in range(8) if k != o
+            ]
+            early_copies.append((up, out))
+
             @pl.when(low == o)
-            def _():
+            def _(o=o, up=up, out=out):
                 @pl.when(high == 0)
                 def _():
                     early[o] = own[:e_rows]
-                    out = [
-                        send(early.at[o], early.at[o], e_send.at[o, 8 + h], e_recv.at[o, 0], h * 8 + o, cores)
-                        for h in wide
-                    ]
-                    for copy in out:
+                    for copy in up:
                         copy.start()
-                    for copy in out:
-                        copy.wait_send()
                 @pl.when(high > 0)
                 def _():
                     send(early.at[o], early.at[o], e_send.at[o, 8], e_recv.at[o, 0], left, cores).wait_recv()
-                out = [
-                    send(early.at[o], early.at[o], e_send.at[o, k], e_recv.at[o, 1], me + k - o, cores)
-                    for k in range(8) if k != o
-                ]
                 for copy in out:
                     copy.start()
-                for copy in out:
-                    copy.wait_send()
         to_left.start()
         to_right.start()
         keep.wait()
@@ -260,6 +261,15 @@
         for j in range(27):
             row = jnp.concatenate([first_ref[ROW_CONV + 3 * j + i : ROW_CONV + 3 * j + i + 1, :] for i in range(3)], axis=1)
             weight[j] = along_sublanes(row)
+        for o, (up, out) in enumerate(early_copies):
+            @pl.when(low == o)
+            def _(up=up, out=out):
+                @pl.when(high == 0)
+                def _():
+                    for copy in up:
+                        copy.wait_send()
+                for copy in out:
+                    copy.wait_send()
 
     for s in range(len(plan) - 1):
         @pl.when(step == cuts[s])
@@ -325,11 +335,7 @@
         cut = len(stages_of(count))
 
         def beside(s):
-            def body(k, _):
-                at = pl.ds(pl.multiple_of(k * BLK, BLK), BLK)
-                dyt_ref[:, at] = dy_s[at, :].T
-                return 0
-            lax.fori_loop(n // BLK * s // cut, n // BLK * (s + 1) // cut, body, 0)
+            lax.fori_loop(n // BLK * s // cut, n // BLK * (s + 1) // cut, lambda k, _: turn_dy(k), 0)
 
         stats_ref[...] = all_sum(rows, me, count, cores, slots, s_send, s_recv, beside)
         for copy in plan[-1]():
@@ -395,7 +401,7 @@
                      rows_ref, grads_ref,
                      grad_ref, total_s, bias_out,
                      near, ext, delta, conv, weight, dw, kept, r1, r2, r3, r4, local_sem, halo_send, halo_recv, g_send,
-                     g_recv, slots, s_send, s_recv, w_own, w_slots, w_high, w_sem, w_recv, w_recv_high, early_s):
+                     g_recv, slots, s_send, s_recv, w_own, w_slots, w_high, w_sem, w_recv, w_recv_high, early_s, factors, w_sum):
     step = pl.program_id(0)
     steps = pl.num_programs(0)
     block = (step + 1) % steps
@@ -426,6 +432,16 @@
         send(ext.at[pl.ds(HALO, HALO)], ext.at[pl.ds(HALO + n, HALO)], halo_send.at[2], halo_recv.at[2], left, cores),
         send(ext.at[pl.ds(n, HALO)], ext.at[pl.ds(0, HALO)], halo_send.at[3], halo_recv.at[3], right, cores),
     ]
+
+    blocks, per = n // BLK, TB // BLK
+
+    def make_rows(i):
+        at = pl.ds(pl.multiple_of(i * BLK, BLK), BLK)
+        live = jnp.broadcast_to(mask_ref[i].astype(F32), (BLK, BLK)).T
+        live = jnp.concatenate([live] * 3, axis=1)
+        value = delta[at, :] * factors[0:1, :] + live * (factors[1:2, :] + factors[2:3, :] * conv[at, :].astype(F32))
+        ext[pl.ds(pl.multiple_of(i * BLK + HALO, HALO), BLK), :] = value.astype(BF)
+        return 0
 
     def core_copies():
         return [send(grads_ref.at[:, :, :, 1 - g], r1, g_send.at[0, 0], g_recv.at[0, 0], g_place, cores)]
@@ -543,15 +559,12 @@
         for copy in locals_:
             copy.wait()
 
-        def body(i, _):
-            at = pl.ds(pl.multiple_of(i * BLK, BLK), BLK)
-            live = jnp.broadcast_to(mask_ref[i].astype(F32), (BLK, BLK)).T
-            live = jnp.concatenate([live] * 3, axis=1)
-            value = delta[at, :] * a + live * (b + c * conv[at, :].astype(F32))
-            ext[pl.ds(pl.multiple_of(i * BLK + HALO, HALO), BLK), :] = value.astype(BF)
-            return 0
-
-        lax.fori_loop(0, n // BLK, body, 0)
+        factors[0:1, :] = a
+        factors[1:2, :] = b
+        factors[2:3, :] = c
+        make_rows(0)
+        make_rows(blocks - 1)
+        lax.fori_loop(per - 1, 2 * per + 1, lambda k, _: make_rows(k), 0)
         for copy in delta_halo:
             copy.start()
 
@@ -604,10 +617,14 @@
 
     skew([pick, multiply, add], [(b, q) for b in range(TB // BLK) for q in range(9)])
 
+    for k in range(per):
+        i = ((block + 1) * per + 1 + k) % blocks
+        make_rows(jnp.where((i == 0) | (i == blocks - 1), blocks - 2, i))
+
     @pl.when(step == steps - 1)
     def _():
-        w_own[0:27] = jnp.sum(dw[...], axis=1)
-        w_own[27:32] = jnp.zeros((5, C), F32)
+        mine = jnp.concatenate([jnp.sum(dw[...], axis=1), jnp.zeros((5, C), F32)], axis=0)
+        w_own[...] = mine.astype(BF)
         to_first = send(w_own, w_slots.at[low], w_sem.at[0], w_recv.at[low], me - low, cores)
 
         @pl.when(low != 0)
@@ -619,7 +636,8 @@
         def _():
             for k in range(1, 8):
                 send(w_own, w_slots.at[k], w_sem.at[0], w_recv.at[k], me + k, cores).wait_recv()
-            w_own[...] = w_own[...] + sum(w_slots[k] for k in range(1, 8))
+            mine_8 = mine + sum(w_slots[k].astype(F32) for k in range(1, 8))
+            w_own[...] = mine_8.astype(BF)
 
             @pl.when(high != 0)
             def _():
@@ -631,7 +649,9 @@
             def _():
                 for h in range(1, count // 8):
                     send(w_own, w_high.at[h], w_sem.at[0], w_recv_high.at[h], h * 8, cores).wait_recv()
-                w_own[...] = w_own[...] + sum(w_high[h] for h in range(1, count // 8))
+                mine_all = mine_8 + sum(w_high[h].astype(F32) for h in range(1, count // 8))
+                w_own[...] = mine_all.astype(BF)
+                w_sum[...] = mine_all
                 out = [send(w_own, w_high.at[0], w_sem.at[o], w_recv_high.at[0], o, cores) for o in range(1, owners)]
                 for copy in out:
                     copy.start()
@@ -642,10 +662,10 @@
             @pl.when(me == o)
             def _(o=o):
                 if o == 0:
-                    sums = w_own[...]
+                    sums = w_sum[...]
                 else:
                     send(w_own, w_high.at[0], w_sem.at[0], w_recv_high.at[0], 0, cores).wait_recv()
-                    sums = w_high[0]
+                    sums = w_high[0].astype(F32)
                 for k in range(3):
                     early_s[pl.ds(ROW_CONV + k, 27, stride=3), :] = sums[:27, k * 128 : (k + 1) * 128]
                 rows = min(shard, early_s.shape[0] - o * shard)
@@ -705,13 +725,15 @@
         ]
         + sum_scratch(count, 8, C)
         + [
-            pltpu.VMEM((32, C), F32),
-            pltpu.VMEM((8, 32, C), F32),
-            pltpu.VMEM((highs, 32, C), F32),
+            pltpu.VMEM((32, C), BF),
+            pltpu.VMEM((8, 32, C), BF),
+            pltpu.VMEM((highs, 32, C), BF),
             pltpu.SemaphoreType.DMA((max(owners, 1),)),
             pltpu.SemaphoreType.DMA((8,)),
             pltpu.SemaphoreType.DMA((highs,)),
             pltpu.VMEM((round_up(ROW_JOINT, 8), 128), F32),
+            pltpu.VMEM((8, C), F32),
+            pltpu.VMEM((32, C), F32),
         ],
         compiler_params=pltpu.CompilerParams(
             vmem_limit_bytes=60 * 1024 * 1024, collective_id=1, has_side_effects=True
@@ -854,7 +876,7 @@
             acc_s[...]=o; dx_s[...]=d
         else:
             acc_s[...]+=o; dx_s[...]+=d
-        gf_ref[fs,:]+=nt(act,dyTb)
+        gf_ref[:,fs]+=nt(dyTb,act)
         gh_ref[:,fs]+=nt(x2,dpb)
     skew([g_h,g_g,g_o],list(range(F//FC)))
     outT=second_s[...]+(acc_s[...]+col(15-2))
@@ -918,12 +940,14 @@
                 flat_ref[pl.ds(row+i,1),:]=jnp.sum(vs_ref[vi,i*128:(i+1)*128,:].T,axis=0,keepdims=True)
         for i in range(12):
             flat_ref[pl.ds(27+i,1),:]=jnp.sum(hb_ref[i*128:(i+1)*128,:].T,axis=0,keepdims=True)
-        for first,mat in ((ROW_JOINT,gj_ref),(ROW_OUT,go_ref),(ROW_HIDDEN,gh_ref),(ROW_FINAL,gf_ref)):
+        for first,mat in ((ROW_JOINT,gj_ref),(ROW_OUT,go_ref),(ROW_HIDDEN,gh_ref)):
             rows,cols=mat.shape
             per=cols//128
             for k in range(per):
                 for r in range(0,rows,C):
                     flat_ref[pl.ds(first+r*per+k,C,stride=per),:]=mat[r:r+C,k*128:(k+1)*128]
+        for k in range(3):
+            flat_ref[pl.ds(ROW_FINAL+k,F,stride=3),:]=gf_ref[k*128:(k+1)*128,:].T
         for i in range(grads_ref.shape[0]*8):
             part=flat_ref[i*shard:(i+1)*shard,:]
             pad=grads_ref.shape[-2]-shard
@@ -939,7 +963,7 @@
     outs=[((n,C),BF,down),((n,C),F32,down),(gathered.shape,BF,whole(*gathered.shape)),((8,C),F32,whole(8,C))]
     mats=[]
     for shape in ((C,3*C),(C,C),(C,F),(F,C)): mats+=[(shape,BF),(shape[::-1],BF)]
-    scr=[pltpu.VMEM(s,d) for s,d in [((flat_rows,128),F32),((4,C,128),F32),((ROW_CONV*128,128),F32)]+mats+[((C,3*C),F32),((C,C),F32),((C,F),F32),((F,C),F32),((10,C,128),F32),((F,128),F32),((C,T),F32),((C,T),F32),((3*C,T),BF),((T,C),BF),((T,C),BF),((HEADS,BLK,T),BF),((C,T),F32),((C,T),BF),((16,T),F32),((C,T),BF),((3*C,T),BF),((2,C,T),BF),((C,T),F32),((C,T),F32)]]
+    scr=[pltpu.VMEM(s,d) for s,d in [((flat_rows,128),F32),((4,C,128),F32),((ROW_CONV*128,128),F32)]+mats+[((C,3*C),F32),((C,C),F32),((C,F),F32),((C,F),F32),((10,C,128),F32),((F,128),F32),((C,T),F32),((C,T),F32),((3*C,T),BF),((T,C),BF),((T,C),BF),((HEADS,BLK,T),BF),((C,T),F32),((C,T),BF),((16,T),F32),((C,T),BF),((3*C,T),BF),((2,C,T),BF),((C,T),F32),((C,T),F32)]]
     return pl.pallas_call(functools.partial(mid_kernel,shard),grid=(n//T,),in_specs=in_specs,out_specs=[o[2] for o in outs],
       out_shape=[jax.ShapeDtypeStruct(o[0],o[1]) for o in outs],scratch_shapes=scr,
       compiler_params=VMEM)(conv,nodes,dy,mask3,stats,rows,gathered)

time: 240 us -> 235 us (0.979)
  Pallas kernels: 231 us -> 225 us
where the time goes in v5:
time: 235 us; the launch traced here: 234 us
  Pallas kernels  225 us (96%)
  local copies, waits for them, and re-layouts  6.49 us (3%)
    pallas_call x1, Pallas kernels, middle(): pl.pallas_call(functools.partial(mid_kernel, shard), grid=(n // T,), in_s...  105 us
    pallas_call x1, Pallas kernels, convolve_back(): pl.pallas_call(functools.partial(conv_back_kernel, count, cores, owners),...  64.6 us
    pallas_call x1, Pallas kernels, convolve(): pl.pallas_call(functools.partial(conv_kernel, count, cores, owners), grid...  56.2 us
    unnamed x10, local copies, waits for them, and re-layouts  6.49 us

profile of v5, /device:TPU:0, one launch (start us, length us, event | category | flops | bytes accessed | tf_op | source)
XLA Modules:
  0.0 234.4 jit_solution(2210683026404078526)
XLA Ops:
  0.6 56.2 %shard_map.126 = (f32[384,4096]{1,0:T(8,128)}, bf16[4096,384]{1,0:T(8,128)(2,1)}, bf16[384,4096]{1,0:T(8,128)(2,1)}, bf16[384,4096]{1,0:T(8,128)(2,1)}, bf16[4,2...) custom-call(s32[27,4096]{1,0:T(8,128)} %bitcast.11, bf16[4096,384]{1,0:T(8,128)(2,1)} %x_ref.1, ...), custom_call_target="tpu_custom_call" | custom-call | tf_op jit(solution)/shard_map/pallas_call | solution.py:357
  56.8 104.5 %shard_map.127 = (bf16[4096,384]{1,0:T(8,128)(2,1)}, f32[4096,384]{1,0:T(8,128)}, bf16[4,2,2,2,448,128]{5,4,3,2,1,0:T(8,128)(2,1)}, f32[8,384]{1,0:T(8,128)}) custom-call(f32[384,4096]{1,0:T(8,128)} %get-tuple-element.21.conv_ref, bf16[384,4096]{1,0:T(8,128)(2,1)} %get-tuple-element.22.nodes_ref, bf16[384,4096]{1,0:T(8,128)(2,1)} %get-tuple-element.23.dyt_ref, ...), custom_call_target="tpu_custom_call" | custom-call | tf_op jit(solution)/shard_map/pallas_call | solution.py:967
  161.3 0.0 copy-start
  161.4 0.0 copy-start.1
  161.4 0.0 copy-start.2
  161.4 64.6 %shard_map.128 = (f32[4096,384]{1,0:T(8,128)}, f32[436,128]{1,0:T(8,128)}, f32[3,128]{1,0:T(4,128)}) custom-call(s32[27,4096]{1,0:T(8,128)} %bitcast.12, f32[4096,384]{1,0:T(8,128)} %get-tuple-element.28.first_hbm, bf16[4096,384]{1,0:T(8,128)(2,1)} %get-tuple-element.29.conv_hbm, bf16[4096,384]{1,0:T(8,128)(2,1)} %x_ref.1, s32[32,1,128]{2,1,0:T(1,128)} %bitcast.16, ...), custom_call_target="tpu_custom_call" | custom-call | tf_op jit(solution)/shard_map/pallas_call | solution.py:688
  226.0 0.0 copy-done
  226.0 0.0 copy-done.1
  226.0 0.0 copy-done.2
  226.0 1.9 fusion.2
  228.0 0.0 copy-start.3
  228.0 5.9 %copy.16 = f32[4096,384]{1,0:T(8,128)} copy(f32[4096,384]{1,0:T(8,128)} %get-tuple-element.47) | data formatting | bytes 12582912
  233.9 0.0 copy-done.3
  233.9 0.6 copy.17
Async XLA Ops:
  161.3 64.6 %copy-start = (f32[55808]{0:T(1024)S(1)}, f32[55808]{0:T(1024)}, u32[]{:S(2)}) copy-start(f32[55808]{0:T(1024)} %param.11) | copy-start | bytes 669700
  161.4 64.6 %copy-start.1 = (f32[55808]{0:T(1024)S(1)}, f32[55808]{0:T(1024)}, u32[]{:S(2)}) copy-start(f32[55808]{0:T(1024)} %param.12) | copy-start | bytes 669700
  161.4 64.6 %copy-start.2 = (f32[55808]{0:T(1024)S(1)}, f32[55808]{0:T(1024)}, u32[]{:S(2)}) copy-start(f32[55808]{0:T(1024)} %param.13) | copy-start | bytes 669700
  228.0 5.9 %copy-start.3 = (f32[3,128]{1,0:T(4,128)S(1)}, f32[3,128]{1,0:T(4,128)}, u32[]{:S(2)}) copy-start(f32[3,128]{1,0:T(4,128)} %get-tuple-element.34) | copy-start | bytes 4612

commit v6 on v5

--- a/solution.py
+++ b/solution.py
@@ -613,7 +613,7 @@
             totals[b] = totals[b] + part * weight[j : j + 1, :]
             dw[j] += jnp.sum((part * xs[b]).reshape(BLK // 8, 8, C), axis=0)
         if q == 8:
-            grad_ref[b * BLK : (b + 1) * BLK, :] = totals.pop(b)
+            grad_ref[b * BLK : (b + 1) * BLK, :] = totals.pop(b).astype(BF)
 
     skew([pick, multiply, add], [(b, q) for b in range(TB // BLK) for q in range(9)])
 
@@ -701,7 +701,7 @@
         ],
         out_specs=[turned, whole(shard, 128), whole(3, 128)],
         out_shape=[
-            jax.ShapeDtypeStruct((n, C), F32),
+            jax.ShapeDtypeStruct((n, C), BF),
             jax.ShapeDtypeStruct((shard, 128), F32),
             jax.ShapeDtypeStruct((3, 128), F32),
         ],
@@ -912,6 +912,11 @@
             delta=jnp.sum(dob_s[hs,cs].astype(F32)*o_s[hs,cs],axis=0,keepdims=True)
             out.append(a_s[h,:,cs]*(dA[:,i*128:(i+1)*128]-delta).astype(BF))
         G[t]=out
+    def b_v(t):
+        b,g,h0=t; cs=slice(b*BLK,(b+1)*BLK)
+        for i in range(2):
+            h=g*4+h0+i; hs=slice(h*32,(h+1)*32)
+            dqkv_s[2*C+h*32:2*C+(h+1)*32,cs]=nt(dob_s[hs,cs],a_s[h,:,cs]).astype(BF)
     def b_q(t):
         b,g,h0=t; cs=slice(b*BLK,(b+1)*BLK)
         lrow=live_row[:,cs]
@@ -920,8 +925,7 @@
             h=g*4+h0+i; hs=slice(h*32,(h+1)*32); ds=out[i]
             dqkv_s[h*32:(h+1)*32,cs]=(nn(qkv_s[C+h*32:C+(h+1)*32,cs],ds)*scale).astype(BF)
             dqkv_s[C+h*32:C+(h+1)*32,cs]=(nt(qkv_s[hs,cs],ds)*(lrow*(scale/c2))).astype(BF)
-            dqkv_s[2*C+h*32:2*C+(h+1)*32,cs]=nt(dob_s[hs,cs],a_s[h,:,cs]).astype(BF)
-    skew([b_d,b_s,b_q],tasks)
+    skew([b_d,b_v,b_s,b_q],tasks)
     vs_ref[3]+=fold(dqkv_s[0:C,:].astype(F32))
     vs_ref[4]+=fold(dqkv_s[2*C:,:].astype(F32))
     gj_ref[...]+=nt(x_s[0],dqkv_s[...])
@@ -992,7 +996,7 @@
     new_master = master - step_rate * (first_hat / (jnp.sqrt(second_hat) + 1e-08) + 0.01 * master)
     return (
         output,
-        node_grad,
+        node_grad.astype(F32),
         new_master,
         new_first,
         new_second,

time: 235 us -> 232 us (0.987)
  local copies, waits for them, and re-layouts: 6.49 us -> 0.61 us
  other arithmetic: 1.95 us -> 6.09 us
    unnamed x10 -> x11, local copies, waits for them, and re-layouts: 6.49 us -> 0.61 us
    convert_element_type x0 -> x1, other arithmetic: none -> 5.07 us  [shards(): node_grad.astype(F32)]
where the time goes in v6:
time: 232 us
  Pallas kernels  224 us (97%)
  other arithmetic  6.09 us (3%)
    pallas_call x1, Pallas kernels, middle(): pl.pallas_call(functools.partial(mid_kernel, shard), grid=(n // T,), in_s...  104 us
    pallas_call x1, Pallas kernels, convolve_back(): pl.pallas_call(functools.partial(conv_back_kernel, count, cores, owners),...  64.5 us
    pallas_call x1, Pallas kernels, convolve(): pl.pallas_call(functools.partial(conv_kernel, count, cores, owners), grid...  56.2 us
    convert_element_type x1, other arithmetic, shards(): node_grad.astype(F32)  5.07 us

profile of v6, /device:TPU:0, one launch (start us, length us, event | category | flops | bytes accessed | tf_op | source)
XLA Modules:
  0.0 231.7 jit_solution(2675683496541693703)
XLA Ops:
  0.6 56.2 %shard_map.126 = (f32[384,4096]{1,0:T(8,128)}, bf16[4096,384]{1,0:T(8,128)(2,1)}, bf16[384,4096]{1,0:T(8,128)(2,1)}, bf16[384,4096]{1,0:T(8,128)(2,1)}, bf16[4,2...) custom-call(s32[27,4096]{1,0:T(8,128)} %bitcast.11, bf16[4096,384]{1,0:T(8,128)(2,1)} %x_ref.1, ...), custom_call_target="tpu_custom_call" | custom-call | tf_op jit(solution)/shard_map/pallas_call | solution.py:357
  56.9 103.6 %shard_map.127 = (bf16[4096,384]{1,0:T(8,128)(2,1)}, f32[4096,384]{1,0:T(8,128)}, bf16[4,2,2,2,448,128]{5,4,3,2,1,0:T(8,128)(2,1)}, f32[8,384]{1,0:T(8,128)}) custom-call(f32[384,4096]{1,0:T(8,128)} %get-tuple-element.21.conv_ref, bf16[384,4096]{1,0:T(8,128)(2,1)} %get-tuple-element.22.nodes_ref, bf16[384,4096]{1,0:T(8,128)(2,1)} %get-tuple-element.23.dyt_ref, ...), custom_call_target="tpu_custom_call" | custom-call | tf_op jit(solution)/shard_map/pallas_call | solution.py:971
  160.5 64.5 %shard_map.128 = (bf16[4096,384]{1,0:T(8,128)(2,1)}, f32[436,128]{1,0:T(8,128)}, f32[3,128]{1,0:T(4,128)}) custom-call(s32[27,4096]{1,0:T(8,128)} %bitcast.12, f32[4096,384]{1,0:T(8,128)} %get-tuple-element.28.first_hbm, bf16[4096,384]{1,0:T(8,128)(2,1)} %get-tuple-element.29.conv_hbm, bf16[4096,384]{1,0:T(8,128)(2,1)} %x_ref.1, s32[32,1,128]{2,1,0:T(1,128)} %bitcast.16, ...), custom_call_target="tpu_custom_call" | custom-call | tf_op jit(solution)/shard_map/pallas_call | solution.py:688
  225.0 0.0 copy-start
  225.0 0.0 copy-start.1
  225.0 0.0 copy-start.2
  225.0 0.0 copy-start.3
  225.0 0.0 copy-start.4
  225.0 5.1 %convert_element_type.6 = f32[4096,384]{1,0:T(8,128)} convert(bf16[4096,384]{1,0:T(8,128)(2,1)} %get-tuple-element.32) | non-fusion elementwise | flops 1572864 | bytes 9437184 | tf_op jit(solution)/shard_map/convert_element_type | solution.py:999
  230.1 0.0 copy-done
  230.1 0.0 copy-done.1
  230.1 0.0 copy-done.2
  230.1 0.0 copy-done.3
  230.1 1.0 fusion.2
  231.1 0.0 copy-done.4
  231.1 0.6 copy.15
Async XLA Ops:
  225.0 5.1 %copy-start = (f32[55808]{0:T(1024)S(1)}, f32[55808]{0:T(1024)}, u32[]{:S(2)}) copy-start(f32[55808]{0:T(1024)} %param.11) | copy-start | bytes 669700
  225.0 5.1 %copy-start.1 = (f32[55808]{0:T(1024)S(1)}, f32[55808]{0:T(1024)}, u32[]{:S(2)}) copy-start(f32[55808]{0:T(1024)} %param.12) | copy-start | bytes 669700
  225.0 5.1 %copy-start.2 = (f32[55808]{0:T(1024)S(1)}, f32[55808]{0:T(1024)}, u32[]{:S(2)}) copy-start(f32[55808]{0:T(1024)} %param.13) | copy-start | bytes 669700
  225.0 5.1 %copy-start.3 = (f32[436,128]{1,0:T(8,128)S(1)}, f32[436,128]{1,0:T(8,128)}, u32[]{:S(2)}) copy-start(f32[436,128]{1,0:T(8,128)} %get-tuple-element.33) | copy-start | bytes 669700
  225.0 6.1 %copy-start.4 = (f32[3,128]{1,0:T(4,128)S(1)}, f32[3,128]{1,0:T(4,128)}, u32[]{:S(2)}) copy-start(f32[3,128]{1,0:T(4,128)} %get-tuple-element.34) | copy-start | bytes 4612

commit v7 on v6

--- a/solution.py
+++ b/solution.py
@@ -258,9 +258,15 @@
         for o in range(owners):
             rows = min(shard, e_rows)
             first_ref[pl.ds(o * shard, rows), :] = early[o].astype(F32)[:rows]
-        for j in range(27):
-            row = jnp.concatenate([first_ref[ROW_CONV + 3 * j + i : ROW_CONV + 3 * j + i + 1, :] for i in range(3)], axis=1)
-            weight[j] = along_sublanes(row)
+        table = jnp.concatenate([first_ref[pl.ds(ROW_CONV + k, 27, stride=3), :] for k in range(3)], axis=1)
+        table = jnp.concatenate([table, jnp.zeros((BLK - 27, C), F32)], axis=0).T.astype(BF)
+        entry = lax.broadcasted_iota(jnp.int32, (BLK, 2 * BLK), 0)
+        second = lax.broadcasted_iota(jnp.int32, (BLK, 2 * BLK), 1) // BLK
+        for j in range(0, 27, 2):
+            both = nn(table, jnp.where(entry == j + second, 1.0, 0.0).astype(BF))
+            weight[j] = both[:, :BLK]
+            if j + 1 < 27:
+                weight[j + 1] = both[:, BLK:]
         for o, (up, out) in enumerate(early_copies):
             @pl.when(low == o)
             def _(up=up, out=out):

time: 232 us -> 231 us (level)
  no operation moved by 1% of the time
where the time goes in v7:
time: 231 us
  Pallas kernels  224 us (97%)
  other arithmetic  6.09 us (3%)
    pallas_call x1, Pallas kernels, middle(): pl.pallas_call(functools.partial(mid_kernel, shard), grid=(n // T,), in_s...  104 us
    pallas_call x1, Pallas kernels, convolve_back(): pl.pallas_call(functools.partial(conv_back_kernel, count, cores, owners),...  64.5 us
    pallas_call x1, Pallas kernels, convolve(): pl.pallas_call(functools.partial(conv_kernel, count, cores, owners), grid...  55.7 us
    convert_element_type x1, other arithmetic, shards(): node_grad.astype(F32)  5.07 us

profile of v7, /device:TPU:0, one launch (start us, length us, event | category | flops | bytes accessed | tf_op | source)
XLA Modules:
  0.0 231.2 jit_solution(14888547555229744557)
XLA Ops:
  0.6 55.7 %shard_map.126 = (f32[384,4096]{1,0:T(8,128)}, bf16[4096,384]{1,0:T(8,128)(2,1)}, bf16[384,4096]{1,0:T(8,128)(2,1)}, bf16[384,4096]{1,0:T(8,128)(2,1)}, bf16[4,2...) custom-call(s32[27,4096]{1,0:T(8,128)} %bitcast.11, bf16[4096,384]{1,0:T(8,128)(2,1)} %x_ref.1, ...), custom_call_target="tpu_custom_call" | custom-call | tf_op jit(solution)/shard_map/pallas_call | solution.py:363
  56.3 103.6 %shard_map.127 = (bf16[4096,384]{1,0:T(8,128)(2,1)}, f32[4096,384]{1,0:T(8,128)}, bf16[4,2,2,2,448,128]{5,4,3,2,1,0:T(8,128)(2,1)}, f32[8,384]{1,0:T(8,128)}) custom-call(f32[384,4096]{1,0:T(8,128)} %get-tuple-element.21.conv_ref, bf16[384,4096]{1,0:T(8,128)(2,1)} %get-tuple-element.22.nodes_ref, bf16[384,4096]{1,0:T(8,128)(2,1)} %get-tuple-element.23.dyt_ref, ...), custom_call_target="tpu_custom_call" | custom-call | tf_op jit(solution)/shard_map/pallas_call | solution.py:977
  159.9 64.5 %shard_map.128 = (bf16[4096,384]{1,0:T(8,128)(2,1)}, f32[436,128]{1,0:T(8,128)}, f32[3,128]{1,0:T(4,128)}) custom-call(s32[27,4096]{1,0:T(8,128)} %bitcast.12, f32[4096,384]{1,0:T(8,128)} %get-tuple-element.28.first_hbm, bf16[4096,384]{1,0:T(8,128)(2,1)} %get-tuple-element.29.conv_hbm, bf16[4096,384]{1,0:T(8,128)(2,1)} %x_ref.1, s32[32,1,128]{2,1,0:T(1,128)} %bitcast.16, ...), custom_call_target="tpu_custom_call" | custom-call | tf_op jit(solution)/shard_map/pallas_call | solution.py:694
  224.5 0.0 copy-start
  224.5 0.0 copy-start.1
  224.5 0.0 copy-start.2
  224.5 0.0 copy-start.3
  224.5 0.0 copy-start.4
  224.5 5.1 %convert_element_type.6 = f32[4096,384]{1,0:T(8,128)} convert(bf16[4096,384]{1,0:T(8,128)(2,1)} %get-tuple-element.32) | non-fusion elementwise | flops 1572864 | bytes 9437184 | tf_op jit(solution)/shard_map/convert_element_type | solution.py:1005
  229.6 0.0 copy-done
  229.6 0.0 copy-done.1
  229.6 0.0 copy-done.2
  229.6 0.0 copy-done.3
  229.6 1.0 fusion.2
  230.6 0.0 copy-done.4
  230.6 0.6 copy.15
Async XLA Ops:
  224.5 5.1 %copy-start = (f32[55808]{0:T(1024)S(1)}, f32[55808]{0:T(1024)}, u32[]{:S(2)}) copy-start(f32[55808]{0:T(1024)} %param.11) | copy-start | bytes 669700
  224.5 5.1 %copy-start.1 = (f32[55808]{0:T(1024)S(1)}, f32[55808]{0:T(1024)}, u32[]{:S(2)}) copy-start(f32[55808]{0:T(1024)} %param.12) | copy-start | bytes 669700
  224.5 5.1 %copy-start.2 = (f32[55808]{0:T(1024)S(1)}, f32[55808]{0:T(1024)}, u32[]{:S(2)}) copy-start(f32[55808]{0:T(1024)} %param.13) | copy-start | bytes 669700
  224.5 5.1 %copy-start.3 = (f32[436,128]{1,0:T(8,128)S(1)}, f32[436,128]{1,0:T(8,128)}, u32[]{:S(2)}) copy-start(f32[436,128]{1,0:T(8,128)} %get-tuple-element.33) | copy-start | bytes 669700
  224.5 6.1 %copy-start.4 = (f32[3,128]{1,0:T(4,128)S(1)}, f32[3,128]{1,0:T(4,128)}, u32[]{:S(2)}) copy-start(f32[3,128]{1,0:T(4,128)} %get-tuple-element.34) | copy-start | bytes 4612
